TPU v7x, 128 devices: a whole 4x4x4 slice. The times are simulated.
128 devices in a mesh: rows: 16 (over x, z), grp: 8 (over y, core).
Axes of the slice: x: 4, y: 4, z: 4, core: 2. Of those that a mesh axis runs over, the one named last changes fastest.
Arguments:
- bin_codes: int32 [524288, 512], P(('rows', 'grp')), may hold values from 0 to 31
- leaf_index: int32 [524288, 1], P(('rows', 'grp')), may hold values from 0 to 7; in each aligned block of 4096 rows (0 to 4095, 4096 to 8191, ...) at most 1024 rows name the same one
- gradients: bfloat16 [524288, 16], P(('rows', 'grp')), may hold values from -6 to 6
- row_weights: bfloat16 [524288], P(('rows', 'grp')), may hold values from 0.5 to 2
- split_feature: int32 [1], replicated, may hold values from 0 to 511
- split_bin: int32 [1], replicated, may hold values from 0 to 30
Outputs:
- gain_table: float32 [16384], P('rows')
- best_gain: float32 [1], replicated
- moved_gradients: bfloat16 [128, 131072], P(('rows', 'grp'))
- moved_weights: bfloat16 [128, 8192], P(('rows', 'grp'))
Inputs may be any that keep to these rules, and one draw needn't show every extreme that they name: `leaf_index`: among the rows of one device, each leaf holds at most 1024 rows, and some leaf holds exactly 1024 on some devices.
All inputs are finite; a program needn't handle non-finite values.
Results may differ from a plain program's by a relative error of at most 0.0004.
Values may be sent and summed in bfloat16 or wider, within the bound.
No kernel may reach another device: no remote copies, remote signals or barrier semaphores. Data moves between devices by JAX's collectives and lax.ppermute only.
A program may use at most 128 MiB of HBM per device.

v0:
```python
import math

import jax
import jax.numpy as jnp
from jax import lax
from jax.sharding import Mesh
from jax.sharding import PartitionSpec as P

BINS = 32
TARGETS = 16
LEAVES = 8
CAP = 1024
GRP = ("grp_0", "grp_1")
ROWS_GRP = ("rows_0", "rows_1", "grp_0", "grp_1")
ROWS = ("rows_0", "rows_1")


ridge = 1.0


def split_up(array, dim, count):
    before, after = (array.shape[:dim], array.shape[dim + 1 :])
    return jnp.moveaxis(array.reshape(*before, count, -1, *after), dim, 0)


def summed_on_arrival(array, axis, dim):
    blocks = split_up(array, dim, lax.axis_size(axis))
    arrived = lax.all_to_all(blocks, axis, split_axis=0, concat_axis=0, tiled=True)
    return arrived.sum(axis=0)


def summed_rows(array, axes, dim):
    far, near = axes
    blocks = split_up(array, dim, lax.axis_size(far))
    nearer = summed_on_arrival(blocks, near, dim + 1)
    arrived = lax.all_to_all(nearer, far, split_axis=0, concat_axis=0, tiled=True)
    return arrived.sum(axis=0)


def in_one_piece(arrays, axis, dim, along):
    ends, at = ([], 0)
    for a in arrays[:-1]:
        at += a.shape[along]
        ends.append(at)
    both = jnp.concatenate(arrays, axis=along)
    return tuple(jnp.split(summed_rows(both, axis, dim), ends, axis=along))


def from_everyone(array, axis):
    copies = jnp.broadcast_to(array, (lax.axis_size(axis), *array.shape))
    return lax.all_to_all(copies, axis, split_axis=0, concat_axis=0, tiled=True)


def laid_out(blocks, dim):
    blocks = jnp.moveaxis(blocks, 0, dim)
    shape = blocks.shape
    return blocks.reshape(*shape[:dim], shape[dim] * shape[dim + 1], *shape[dim + 2 :])


def gather_directly(array, axis, dim):
    blocks = from_everyone(array, axis)
    return laid_out(blocks, dim)


def over_copies(array, axis):
    everything = from_everyone(array, axis)
    return jnp.max(everything, axis=0)


def split_scores(grad_hist, weight_hist):
    left_g = jnp.cumsum(grad_hist, axis=1)
    left_w = jnp.cumsum(weight_hist, axis=1)
    upper_g = jnp.flip(jnp.cumsum(jnp.flip(grad_hist, axis=1), axis=1), axis=1)
    upper_w = jnp.flip(jnp.cumsum(jnp.flip(weight_hist, axis=1), axis=1), axis=1)
    right_g = jnp.concatenate([upper_g[:, 1:], jnp.zeros_like(upper_g[:, :1])], axis=1)
    right_w = jnp.concatenate([upper_w[:, 1:], jnp.zeros_like(upper_w[:, :1])], axis=1)
    left_x = left_w + ridge
    right_y = right_w + ridge
    diff = left_g * right_y[..., None] - right_g * left_x[..., None]
    terms = diff * diff / (left_x * right_y * (left_x + right_y))[..., None]
    return jnp.sum(terms, axis=(2, 3)) / (LEAVES * TARGETS)


def place_rows(leaf, child, grads, weights):
    key_ids = leaf * 2 + child
    key_hot = (key_ids[:, None] == jnp.arange(2 * LEAVES, dtype=jnp.int32)[None, :]).astype(
        jnp.int32
    )
    before = jnp.cumsum(key_hot, axis=0) - key_hot
    rank = jnp.sum(before * key_hot, axis=1)
    counts = jnp.sum(key_hot, axis=0)
    leaf_hot = (leaf[:, None] == jnp.arange(LEAVES, dtype=jnp.int32)[None, :]).astype(jnp.int32)
    first = jnp.sum(leaf_hot * counts[0::2][None, :], axis=1)
    slot = leaf * CAP + rank + child * first
    buf_g = jnp.zeros((LEAVES * CAP, grads.shape[1]), grads.dtype).at[slot].set(grads)
    buf_w = jnp.zeros((LEAVES * CAP,), weights.dtype).at[slot].set(weights)
    return (buf_g.reshape(LEAVES, CAP * grads.shape[1]), buf_w.reshape(LEAVES, CAP))


def owned_gains(grad_sum, weight_sum):
    grad_hist = grad_sum.reshape(-1, BINS, LEAVES, TARGETS)
    weight_hist = weight_sum.reshape(-1, BINS, LEAVES)
    return split_scores(grad_hist, weight_hist).reshape(-1)


def histograms(codes, leaf, grads, weights, step):
    row_count = codes.shape[0]
    feature_count = codes.shape[1]
    width = math.gcd(64, feature_count)
    block_count = feature_count // width
    turns = row_count // step
    leaf_hot = (leaf[:, None] == jnp.arange(LEAVES, dtype=jnp.int32)[None, :]).astype(jnp.bfloat16)
    grad_cols = (leaf_hot[:, :, None] * grads[:, None, :]).reshape(row_count, LEAVES * TARGETS)
    weight_cols = leaf_hot * weights[:, None]
    bin_ids = jnp.arange(BINS, dtype=jnp.int32)
    dims = (((0,), (0,)), ((), ()))

    def one_block(index):
        codes_block = lax.dynamic_slice_in_dim(codes, index * width, width, 1)

        def add_rows(carry, turn):
            bin_hot = (
                (codes_block[:, :, None] == bin_ids[None, None, :])
                .astype(jnp.bfloat16)
                .reshape(step, width * BINS)
            )
            grad_part = lax.dot_general(
                bin_hot, grad_cols, dims, preferred_element_type=jnp.float32
            )
            weight_part = lax.dot_general(
                bin_hot, weight_cols, dims, preferred_element_type=jnp.float32
            )
            return ((carry[0] + grad_part, carry[1] + weight_part), None)

        start_sums = (
            jnp.zeros((width * BINS, LEAVES * TARGETS), jnp.float32),
            jnp.zeros((width * BINS, LEAVES), jnp.float32),
        )
        sums, unused = lax.scan(add_rows, start_sums, jnp.arange(turns, dtype=jnp.int32))
        return sums

    grad_term, weight_term = lax.map(one_block, jnp.arange(block_count, dtype=jnp.int32))
    return (
        grad_term.reshape(feature_count * BINS, LEAVES * TARGETS),
        weight_term.reshape(feature_count * BINS, LEAVES),
    )


def shards(bin_codes, leaf_index, gradients, row_weights, split_feature, split_bin):
    local_rows = bin_codes.shape[0]
    leaf = leaf_index[:, 0]
    column = lax.dynamic_slice_in_dim(bin_codes, split_feature[0], 1, 1)[:, 0]
    child = (column > split_bin[0]).astype(jnp.int32)
    send_g, send_w = place_rows(leaf, child, gradients, row_weights)
    moved_gradients, moved_weights = (
        lax.all_to_all(send_g, GRP, split_axis=0, concat_axis=1, tiled=True),
        lax.all_to_all(send_w, GRP, split_axis=0, concat_axis=1, tiled=True),
    )
    grad_term, weight_term = histograms(bin_codes, leaf, gradients, row_weights, local_rows)
    grad_sum, weight_sum = in_one_piece(
        (grad_term, weight_term), (("rows_0", "rows_1", "grp_0"), "grp_1"), 0, 1
    )
    gain_local = owned_gains(grad_sum, weight_sum)
    gain_table = gather_directly(gain_local, GRP, 0)
    best_gain = over_copies(jnp.max(gain_table), ROWS).reshape(1)
    return (gain_table, best_gain, moved_gradients, moved_weights)


def solution(mesh):
    torus = Mesh(mesh.devices.reshape(4, 4, 4, 2), ("rows_0", "rows_1", "grp_0", "grp_1"))
    in_specs = (P(ROWS_GRP, None), P(ROWS_GRP, None), P(ROWS_GRP, None), P(ROWS_GRP), P(), P())
    out_specs = (P(ROWS), P(), P(ROWS_GRP, None), P(ROWS_GRP, None))
    return jax.shard_map(
        shards, mesh=torus, in_specs=in_specs, out_specs=out_specs, check_vma=False
    )
```

profile of v0, /device:TPU:1, one launch (start us, length us, event | category | flops | bytes accessed | tf_op | source)
XLA Modules:
  0.0 346.0 jit_solution(11459931182927773766)
XLA Ops:
  1.4 9.0 %copy.52 = s32[4096,512]{0,1:T(8,128)} copy(s32[4096,512]{1,0:T(8,128)} %param.8) | data formatting | bytes 16777216
  10.4 149.8 %while.13 = (s32[]{:T(128)}, f32[8,2048,128]{2,1,0:T(8,128)}, f32[8,2048,8]{1,2,0:T(8,128)}, s32[8]{0:T(128)S(1)}, s32[4096,512]{0,1:T(8,128)}, /*index=5*/bf16[...) while((s32[]{:T(128)}, f32[8,2048,128]{2,1,0:T(8,128)}, ...), condition=%wide.region_1.2_spmd.clone, body=%wide.region_0.0_spmd.clone.sunk | while | flops 2290679808 | bytes 31776972 | solution.py:142
  13.2 5.3 %bitcast_compare_fusion.2 = pred[4096,2048]{0,1:T(32,128)(4,1)S(1)} fusion(s32[2048]{0:T(1024)S(1)} %eq.164, s32[4096,64]{0,1:T(8,128)S(1)} %constant_dynamic-slice_fusion.2), kind=kLoop, calls=%fused_computation.5.clone.1 | loop fusion | flops 8388608 | bytes 9445376 | tf_op jit(solution)/shard_map/while/body/eval_jaxpr/while/body/eval_jaxpr/eq | solution.py:123
  18.5 5.1 %fusion.45 = f32[8,2048,8]{1,2,0:T(8,128)} fusion(f32[8,2048,8]{1,2,0:T(8,128)} %get-tuple-element.234, s32[]{:T(128)S(6)} %copy.74, pred[4096,2048]{0,1:T(32,128)(4,1)S(1)} %bitcast_compare_fusion.2, s32[4096]{0:T(1024)S(1)} %get-tuple-element.252, bf16[4096]{0:T(1024)(128)(2,1)S(1)} %get-tuple-element.253), kind=kOutput, calls=%fused_computation.9.clone.1 | convolution fusion | flops 134283264 | bytes 8478724 | tf_op jit(solution)/shard_map/while/body/eval_jaxpr/while/body/eval_jaxpr/dot_general | solution.py:130
  23.5 5.6 %fusion.44 = f32[8,2048,128]{2,1,0:T(8,128)} fusion(f32[8,2048,128]{2,1,0:T(8,128)} %get-tuple-element.233, s32[]{:T(128)S(6)} %copy.74, pred[4096,2048]{0,1:T(32,128)(4,1)S(1)} %bitcast_compare_fusion.2, bf16[4096,128]{0,1:T(8,128)(2,1)S(1)} %bitcast.71), kind=kOutput, calls=%fused_computation.7.clone.1 | convolution fusion | flops 2147483648 | bytes 10485764 | tf_op jit(solution)/shard_map/while/body/eval_jaxpr/while/body/eval_jaxpr/dot_general | solution.py:127
  31.9 5.3 %bitcast_compare_fusion.2 = pred[4096,2048]{0,1:T(32,128)(4,1)S(1)} fusion(s32[2048]{0:T(1024)S(1)} %eq.164, s32[4096,64]{0,1:T(8,128)S(1)} %constant_dynamic-slice_fusion.2), kind=kLoop, calls=%fused_computation.5.clone.1 | loop fusion | flops 8388608 | bytes 9445376 | tf_op jit(solution)/shard_map/while/body/eval_jaxpr/while/body/eval_jaxpr/eq | solution.py:123
  37.2 5.1 %fusion.45 = f32[8,2048,8]{1,2,0:T(8,128)} fusion(f32[8,2048,8]{1,2,0:T(8,128)} %get-tuple-element.234, s32[]{:T(128)S(6)} %copy.74, pred[4096,2048]{0,1:T(32,128)(4,1)S(1)} %bitcast_compare_fusion.2, s32[4096]{0:T(1024)S(1)} %get-tuple-element.252, bf16[4096]{0:T(1024)(128)(2,1)S(1)} %get-tuple-element.253), kind=kOutput, calls=%fused_computation.9.clone.1 | convolution fusion | flops 134283264 | bytes 8478724 | tf_op jit(solution)/shard_map/while/body/eval_jaxpr/while/body/eval_jaxpr/dot_general | solution.py:130
  42.3 5.7 %fusion.44 = f32[8,2048,128]{2,1,0:T(8,128)} fusion(f32[8,2048,128]{2,1,0:T(8,128)} %get-tuple-element.233, s32[]{:T(128)S(6)} %copy.74, pred[4096,2048]{0,1:T(32,128)(4,1)S(1)} %bitcast_compare_fusion.2, bf16[4096,128]{0,1:T(8,128)(2,1)S(1)} %bitcast.71), kind=kOutput, calls=%fused_computation.7.clone.1 | convolution fusion | flops 2147483648 | bytes 10485764 | tf_op jit(solution)/shard_map/while/body/eval_jaxpr/while/body/eval_jaxpr/dot_general | solution.py:127
  50.7 5.3 %bitcast_compare_fusion.2 = pred[4096,2048]{0,1:T(32,128)(4,1)S(1)} fusion(s32[2048]{0:T(1024)S(1)} %eq.164, s32[4096,64]{0,1:T(8,128)S(1)} %constant_dynamic-slice_fusion.2), kind=kLoop, calls=%fused_computation.5.clone.1 | loop fusion | flops 8388608 | bytes 9445376 | tf_op jit(solution)/shard_map/while/body/eval_jaxpr/while/body/eval_jaxpr/eq | solution.py:123
  56.0 5.1 %fusion.45 = f32[8,2048,8]{1,2,0:T(8,128)} fusion(f32[8,2048,8]{1,2,0:T(8,128)} %get-tuple-element.234, s32[]{:T(128)S(6)} %copy.74, pred[4096,2048]{0,1:T(32,128)(4,1)S(1)} %bitcast_compare_fusion.2, s32[4096]{0:T(1024)S(1)} %get-tuple-element.252, bf16[4096]{0:T(1024)(128)(2,1)S(1)} %get-tuple-element.253), kind=kOutput, calls=%fused_computation.9.clone.1 | convolution fusion | flops 134283264 | bytes 8478724 | tf_op jit(solution)/shard_map/while/body/eval_jaxpr/while/body/eval_jaxpr/dot_general | solution.py:130
  61.0 5.6 %fusion.44 = f32[8,2048,128]{2,1,0:T(8,128)} fusion(f32[8,2048,128]{2,1,0:T(8,128)} %get-tuple-element.233, s32[]{:T(128)S(6)} %copy.74, pred[4096,2048]{0,1:T(32,128)(4,1)S(1)} %bitcast_compare_fusion.2, bf16[4096,128]{0,1:T(8,128)(2,1)S(1)} %bitcast.71), kind=kOutput, calls=%fused_computation.7.clone.1 | convolution fusion | flops 2147483648 | bytes 10485764 | tf_op jit(solution)/shard_map/while/body/eval_jaxpr/while/body/eval_jaxpr/dot_general | solution.py:127
  68.0 1.3 constant_dynamic-slice_fusion.2
  69.4 5.3 %bitcast_compare_fusion.2 = pred[4096,2048]{0,1:T(32,128)(4,1)S(1)} fusion(s32[2048]{0:T(1024)S(1)} %eq.164, s32[4096,64]{0,1:T(8,128)S(1)} %constant_dynamic-slice_fusion.2), kind=kLoop, calls=%fused_computation.5.clone.1 | loop fusion | flops 8388608 | bytes 9445376 | tf_op jit(solution)/shard_map/while/body/eval_jaxpr/while/body/eval_jaxpr/eq | solution.py:123
  74.7 5.1 %fusion.45 = f32[8,2048,8]{1,2,0:T(8,128)} fusion(f32[8,2048,8]{1,2,0:T(8,128)} %get-tuple-element.234, s32[]{:T(128)S(6)} %copy.74, pred[4096,2048]{0,1:T(32,128)(4,1)S(1)} %bitcast_compare_fusion.2, s32[4096]{0:T(1024)S(1)} %get-tuple-element.252, bf16[4096]{0:T(1024)(128)(2,1)S(1)} %get-tuple-element.253), kind=kOutput, calls=%fused_computation.9.clone.1 | convolution fusion | flops 134283264 | bytes 8478724 | tf_op jit(solution)/shard_map/while/body/eval_jaxpr/while/body/eval_jaxpr/dot_general | solution.py:130
  79.7 5.6 %fusion.44 = f32[8,2048,128]{2,1,0:T(8,128)} fusion(f32[8,2048,128]{2,1,0:T(8,128)} %get-tuple-element.233, s32[]{:T(128)S(6)} %copy.74, pred[4096,2048]{0,1:T(32,128)(4,1)S(1)} %bitcast_compare_fusion.2, bf16[4096,128]{0,1:T(8,128)(2,1)S(1)} %bitcast.71), kind=kOutput, calls=%fused_computation.7.clone.1 | convolution fusion | flops 2147483648 | bytes 10485764 | tf_op jit(solution)/shard_map/while/body/eval_jaxpr/while/body/eval_jaxpr/dot_general | solution.py:127
  88.1 5.3 %bitcast_compare_fusion.2 = pred[4096,2048]{0,1:T(32,128)(4,1)S(1)} fusion(s32[2048]{0:T(1024)S(1)} %eq.164, s32[4096,64]{0,1:T(8,128)S(1)} %constant_dynamic-slice_fusion.2), kind=kLoop, calls=%fused_computation.5.clone.1 | loop fusion | flops 8388608 | bytes 9445376 | tf_op jit(solution)/shard_map/while/body/eval_jaxpr/while/body/eval_jaxpr/eq | solution.py:123
  93.4 5.1 %fusion.45 = f32[8,2048,8]{1,2,0:T(8,128)} fusion(f32[8,2048,8]{1,2,0:T(8,128)} %get-tuple-element.234, s32[]{:T(128)S(6)} %copy.74, pred[4096,2048]{0,1:T(32,128)(4,1)S(1)} %bitcast_compare_fusion.2, s32[4096]{0:T(1024)S(1)} %get-tuple-element.252, bf16[4096]{0:T(1024)(128)(2,1)S(1)} %get-tuple-element.253), kind=kOutput, calls=%fused_computation.9.clone.1 | convolution fusion | flops 134283264 | bytes 8478724 | tf_op jit(solution)/shard_map/while/body/eval_jaxpr/while/body/eval_jaxpr/dot_general | solution.py:130
  98.5 5.6 %fusion.44 = f32[8,2048,128]{2,1,0:T(8,128)} fusion(f32[8,2048,128]{2,1,0:T(8,128)} %get-tuple-element.233, s32[]{:T(128)S(6)} %copy.74, pred[4096,2048]{0,1:T(32,128)(4,1)S(1)} %bitcast_compare_fusion.2, bf16[4096,128]{0,1:T(8,128)(2,1)S(1)} %bitcast.71), kind=kOutput, calls=%fused_computation.7.clone.1 | convolution fusion | flops 2147483648 | bytes 10485764 | tf_op jit(solution)/shard_map/while/body/eval_jaxpr/while/body/eval_jaxpr/dot_general | solution.py:127
  106.8 5.3 %bitcast_compare_fusion.2 = pred[4096,2048]{0,1:T(32,128)(4,1)S(1)} fusion(s32[2048]{0:T(1024)S(1)} %eq.164, s32[4096,64]{0,1:T(8,128)S(1)} %constant_dynamic-slice_fusion.2), kind=kLoop, calls=%fused_computation.5.clone.1 | loop fusion | flops 8388608 | bytes 9445376 | tf_op jit(solution)/shard_map/while/body/eval_jaxpr/while/body/eval_jaxpr/eq | solution.py:123
  112.1 5.1 %fusion.45 = f32[8,2048,8]{1,2,0:T(8,128)} fusion(f32[8,2048,8]{1,2,0:T(8,128)} %get-tuple-element.234, s32[]{:T(128)S(6)} %copy.74, pred[4096,2048]{0,1:T(32,128)(4,1)S(1)} %bitcast_compare_fusion.2, s32[4096]{0:T(1024)S(1)} %get-tuple-element.252, bf16[4096]{0:T(1024)(128)(2,1)S(1)} %get-tuple-element.253), kind=kOutput, calls=%fused_computation.9.clone.1 | convolution fusion | flops 134283264 | bytes 8478724 | tf_op jit(solution)/shard_map/while/body/eval_jaxpr/while/body/eval_jaxpr/dot_general | solution.py:130
  117.2 5.6 %fusion.44 = f32[8,2048,128]{2,1,0:T(8,128)} fusion(f32[8,2048,128]{2,1,0:T(8,128)} %get-tuple-element.233, s32[]{:T(128)S(6)} %copy.74, pred[4096,2048]{0,1:T(32,128)(4,1)S(1)} %bitcast_compare_fusion.2, bf16[4096,128]{0,1:T(8,128)(2,1)S(1)} %bitcast.71), kind=kOutput, calls=%fused_computation.7.clone.1 | convolution fusion | flops 2147483648 | bytes 10485764 | tf_op jit(solution)/shard_map/while/body/eval_jaxpr/while/body/eval_jaxpr/dot_general | solution.py:127
  125.5 5.3 %bitcast_compare_fusion.2 = pred[4096,2048]{0,1:T(32,128)(4,1)S(1)} fusion(s32[2048]{0:T(1024)S(1)} %eq.164, s32[4096,64]{0,1:T(8,128)S(1)} %constant_dynamic-slice_fusion.2), kind=kLoop, calls=%fused_computation.5.clone.1 | loop fusion | flops 8388608 | bytes 9445376 | tf_op jit(solution)/shard_map/while/body/eval_jaxpr/while/body/eval_jaxpr/eq | solution.py:123
  130.8 5.1 %fusion.45 = f32[8,2048,8]{1,2,0:T(8,128)} fusion(f32[8,2048,8]{1,2,0:T(8,128)} %get-tuple-element.234, s32[]{:T(128)S(6)} %copy.74, pred[4096,2048]{0,1:T(32,128)(4,1)S(1)} %bitcast_compare_fusion.2, s32[4096]{0:T(1024)S(1)} %get-tuple-element.252, bf16[4096]{0:T(1024)(128)(2,1)S(1)} %get-tuple-element.253), kind=kOutput, calls=%fused_computation.9.clone.1 | convolution fusion | flops 134283264 | bytes 8478724 | tf_op jit(solution)/shard_map/while/body/eval_jaxpr/while/body/eval_jaxpr/dot_general | solution.py:130
  135.9 5.6 %fusion.44 = f32[8,2048,128]{2,1,0:T(8,128)} fusion(f32[8,2048,128]{2,1,0:T(8,128)} %get-tuple-element.233, s32[]{:T(128)S(6)} %copy.74, pred[4096,2048]{0,1:T(32,128)(4,1)S(1)} %bitcast_compare_fusion.2, bf16[4096,128]{0,1:T(8,128)(2,1)S(1)} %bitcast.71), kind=kOutput, calls=%fused_computation.7.clone.1 | convolution fusion | flops 2147483648 | bytes 10485764 | tf_op jit(solution)/shard_map/while/body/eval_jaxpr/while/body/eval_jaxpr/dot_general | solution.py:127
  144.3 5.3 %bitcast_compare_fusion.2 = pred[4096,2048]{0,1:T(32,128)(4,1)S(1)} fusion(s32[2048]{0:T(1024)S(1)} %eq.164, s32[4096,64]{0,1:T(8,128)S(1)} %constant_dynamic-slice_fusion.2), kind=kLoop, calls=%fused_computation.5.clone.1 | loop fusion | flops 8388608 | bytes 9445376 | tf_op jit(solution)/shard_map/while/body/eval_jaxpr/while/body/eval_jaxpr/eq | solution.py:123
  149.6 5.1 %fusion.45 = f32[8,2048,8]{1,2,0:T(8,128)} fusion(f32[8,2048,8]{1,2,0:T(8,128)} %get-tuple-element.234, s32[]{:T(128)S(6)} %copy.74, pred[4096,2048]{0,1:T(32,128)(4,1)S(1)} %bitcast_compare_fusion.2, s32[4096]{0:T(1024)S(1)} %get-tuple-element.252, bf16[4096]{0:T(1024)(128)(2,1)S(1)} %get-tuple-element.253), kind=kOutput, calls=%fused_computation.9.clone.1 | convolution fusion | flops 134283264 | bytes 8478724 | tf_op jit(solution)/shard_map/while/body/eval_jaxpr/while/body/eval_jaxpr/dot_general | solution.py:130
  154.6 5.6 %fusion.44 = f32[8,2048,128]{2,1,0:T(8,128)} fusion(f32[8,2048,128]{2,1,0:T(8,128)} %get-tuple-element.233, s32[]{:T(128)S(6)} %copy.74, pred[4096,2048]{0,1:T(32,128)(4,1)S(1)} %bitcast_compare_fusion.2, bf16[4096,128]{0,1:T(8,128)(2,1)S(1)} %bitcast.71), kind=kOutput, calls=%fused_computation.7.clone.1 | convolution fusion | flops 2147483648 | bytes 10485764 | tf_op jit(solution)/shard_map/while/body/eval_jaxpr/while/body/eval_jaxpr/dot_general | solution.py:127
  160.2 5.6 %copy.53 = f32[64,2,128,8]{3,2,1,0:T(8,128)} copy(f32[64,2,128,8]{2,3,1,0:T(8,128)} %bitcast.2) | data formatting | bytes 1048576 | tf_op jit(solution)/shard_map/concatenate | solution.py:45
  165.9 11.6 %maximum_bitcast_fusion = f32[2,64,128,136]{3,2,0,1:T(8,128)} fusion(f32[64,2,128,8]{3,2,1,0:T(8,128)} %copy.53, f32[64,2,128,128]{3,2,1,0:T(8,128)} %bitcast.72), kind=kLoop, calls=%fused_computation.18 | loop fusion | flops 2228224 | bytes 17825792 | tf_op jit(solution)/shard_map/transpose | solution.py:23
  177.4 13.9 %copy.54 = f32[2,64,128,136]{2,3,1,0:T(8,128)} copy(f32[2,64,128,136]{3,2,0,1:T(8,128)} %maximum_bitcast_fusion) | data formatting | bytes 17825792 | tf_op jit(solution)/shard_map/transpose | solution.py:23
  191.4 20.3 %all_to_all.56 = f32[2,64,128,136]{2,3,1,0:T(8,128)} all-to-all(f32[2,64,128,136]{2,3,1,0:T(8,128)} %copy.54), channel_id=1, replica_groups=mesh['rows_0'=4,'rows_1'=4,'grp_0'=4,'grp_1'=2] {'grp_1'}, dimensions={0} | all-to-all | bytes 17825792 | tf_op jit(solution)/shard_map/all_to_all | solution.py:28
  211.7 6.7 %reduce_sum.58 = f32[64,128,136]{1,2,0:T(8,128)} reduce(f32[2,64,128,136]{2,3,1,0:T(8,128)} %all_to_all.56, f32[]{:T(128)} %constant.24.clone.1), dimensions={0}, to_apply=%region_2.3 | reduce | flops 1114112 | bytes 13369348 | tf_op jit(solution)/shard_map/reduce_sum | solution.py:29
  218.4 11.5 %all-to-all-start.1 = ((f32[64,128,136]{1,2,0:T(8,128)}), f32[64,128,136]{1,2,0:T(8,128)}, u32[]{:S(2)}, u32[]{:S(2)}) async-start(f32[64,128,136]{1,2,0:T(8,128)} %reduce_sum.58), calls=%async_computation.1 | async-start | bytes 8912896 | tf_op jit(solution)/shard_map/all_to_all | solution.py:36
  229.9 1.3 copy.62
  233.4 4.6 %reduce-window.6 = s32[16,32,128]{2,1,0:T(8,128)S(1)} reduce-window(s32[16,32,128]{2,1,0:T(8,128)S(1)} %fusion.21, s32[]{:T(128)} %constant.23.clone.1), window={size=1x1x128 pad=0_0x0_0x127_0}, to_apply=%region_11.12 | reduce-window | flops 8323072 | bytes 524292 | tf_op jit(solution)/shard_map/reduce-window
  240.3 28.6 %scatter_custom_fusion.1 = bf16[8192]{0:T(1024)(128)(2,1)S(1)} fusion(s32[4096]{0:T(1024)S(1)} %bitcast.90, bf16[4096]{0:T(1024)(128)(2,1)S(1)} %get-tuple-element.275, bf16[]{:T(256)} %constant.26.clone.1), kind=kCustom, calls=%fused_computation.46 | custom fusion | bytes 16386 | tf_op jit(solution)/shard_map/scatter | solution.py:96
  270.8 11.9 %scatter_custom_fusion = bf16[8192,16]{1,0:T(8,128)(2,1)S(1)} fusion(s32[4096]{0:T(1024)S(1)} %bitcast.91, bf16[4096,16]{1,0:T(8,128)(2,1)} %copy.62, bf16[]{:T(256)} %constant.26.clone.1), kind=kCustom, calls=%fused_computation.19 | custom fusion | bytes 262656 | tf_op jit(solution)/shard_map/scatter | solution.py:95
  282.7 1.5 all_to_all.48
  284.1 2.2 reduce.5
  287.2 5.9 %all-to-all-start.5 = ((bf16[8,2,512]{2,1,0:T(2,128)(2,1)}), bf16[8,2,512]{2,1,0:T(2,128)(2,1)S(1)}, u32[]{:S(2)}, u32[]{:S(2)}) async-start(bf16[8,2,512]{2,1,0:T(2,128)(2,1)} %reshape.142), calls=%async_computation.5 | async-start | bytes 32768 | tf_op jit(solution)/shard_map/all_to_all | solution.py:157
  293.1 2.5 reduce_sum.59
  296.6 7.6 %fusion.28 = f32[4,32,8,16]{3,2,1,0:T(8,128)S(1)} fusion(f32[4,32,8,16]{3,2,1,0:T(8,128)S(1)} %copy.57), kind=kOutput, calls=%fused_computation.50 | output fusion | flops 507904 | bytes 131072 | tf_op jit(solution)/shard_map/jit(cumsum)/reduce_window_sum | solution.py:73
  304.6 4.8 %all-to-all-start.4 = ((bf16[8,2,8192]{2,1,0:T(2,128)(2,1)}), bf16[8,2,8192]{2,1,0:T(2,128)(2,1)S(1)}, u32[]{:S(2)}, u32[]{:S(2)}) async-start(bf16[8,2,8192]{2,1,0:T(2,128)(2,1)} %reshape.140), calls=%async_computation.4 | async-start | bytes 524288 | tf_op jit(solution)/shard_map/all_to_all | solution.py:156
  310.8 5.1 %all-to-all-done.4 = bf16[8,2,8192]{2,1,0:T(2,128)(2,1)S(1)} async-done(((bf16[8,2,8192]{2,1,0:T(2,128)(2,1)}), bf16[8,2,8192]{2,1,0:T(2,128)(2,1)S(1)}, u32[]{:S(2)}, u32[]{:S(2)}) %all-to-all-start.4) | async-done | bytes 262176 | tf_op jit(solution)/shard_map/all_to_all | solution.py:156
  316.6 4.3 %all-to-all-start.2 = ((f32[8,1,128]{2,1,0:T(1,128)}), f32[8,1,128]{2,1,0:T(1,128)S(1)}, u32[]{:S(2)}, u32[]{:S(2)}) async-start(f32[8,1,128]{2,1,0:T(1,128)} %broadcast_in_dim.26), calls=%async_computation.2 | async-start | bytes 8192 | tf_op jit(solution)/shard_map/all_to_all | solution.py:51
  322.4 2.9 all-to-all-done.2
  327.2 11.2 %all-to-all-start.3 = ((f32[16,1,1]{2,1,0:T(1,128)}), f32[16,1,1]{2,1,0:T(1,128)S(1)}, u32[]{:S(2)}, u32[]{:S(2)}) async-start(f32[16,1,1]{2,1,0:T(1,128)} %broadcast_in_dim.27), calls=%async_computation.3 | async-start | bytes 16384 | tf_op jit(solution)/shard_map/all_to_all | solution.py:51
  338.4 6.4 %all-to-all-done.3 = f32[16,1,1]{2,1,0:T(1,128)S(1)} async-done(((f32[16,1,1]{2,1,0:T(1,128)}), f32[16,1,1]{2,1,0:T(1,128)S(1)}, u32[]{:S(2)}, u32[]{:S(2)}) %all-to-all-start.3) | async-done | bytes 96 | tf_op jit(solution)/shard_map/all_to_all | solution.py:51
  (89 shorter events, 29.8 us)
Async XLA Ops:
  1.4 9.0 %copy-start = (bf16[4096,16]{0,1:T(8,128)(2,1)S(1)}, bf16[4096,16]{0,1:T(8,128)(2,1)}, u32[]{:S(2)}) copy-start(bf16[4096,16]{0,1:T(8,128)(2,1)} %param.10) | copy-start | bytes 393220
  1.4 9.0 %copy-start.1 = (s32[4096,1]{0,1:T(1,128)S(1)}, s32[4096,1]{0,1:T(1,128)}, u32[]{:S(2)}) copy-start(s32[4096,1]{0,1:T(1,128)} %param.9) | copy-start | bytes 49156
  1.4 9.0 %copy-start.2 = (bf16[4096]{0:T(1024)(128)(2,1)S(1)}, bf16[4096]{0:T(1024)(128)(2,1)}, u32[]{:S(2)}) copy-start(bf16[4096]{0:T(1024)(128)(2,1)} %param.11) | copy-start | bytes 24580
  218.4 68.8 %all-to-all-start.1 = ((f32[64,128,136]{1,2,0:T(8,128)}), f32[64,128,136]{1,2,0:T(8,128)}, u32[]{:S(2)}, u32[]{:S(2)}) async-start(f32[64,128,136]{1,2,0:T(8,128)} %reduce_sum.58), calls=%async_computation.1 | async-start | bytes 8912896 | tf_op jit(solution)/shard_map/all_to_all | solution.py:36
  287.2 17.4 %all-to-all-start.5 = ((bf16[8,2,512]{2,1,0:T(2,128)(2,1)}), bf16[8,2,512]{2,1,0:T(2,128)(2,1)S(1)}, u32[]{:S(2)}, u32[]{:S(2)}) async-start(bf16[8,2,512]{2,1,0:T(2,128)(2,1)} %reshape.142), calls=%async_computation.5 | async-start | bytes 32768 | tf_op jit(solution)/shard_map/all_to_all | solution.py:157
  304.6 11.3 %all-to-all-start.4 = ((bf16[8,2,8192]{2,1,0:T(2,128)(2,1)}), bf16[8,2,8192]{2,1,0:T(2,128)(2,1)S(1)}, u32[]{:S(2)}, u32[]{:S(2)}) async-start(bf16[8,2,8192]{2,1,0:T(2,128)(2,1)} %reshape.140), calls=%async_computation.4 | async-start | bytes 524288 | tf_op jit(solution)/shard_map/all_to_all | solution.py:156
  316.6 8.8 %all-to-all-start.2 = ((f32[8,1,128]{2,1,0:T(1,128)}), f32[8,1,128]{2,1,0:T(1,128)S(1)}, u32[]{:S(2)}, u32[]{:S(2)}) async-start(f32[8,1,128]{2,1,0:T(1,128)} %broadcast_in_dim.26), calls=%async_computation.2 | async-start | bytes 8192 | tf_op jit(solution)/shard_map/all_to_all | solution.py:51
  327.2 17.6 %all-to-all-start.3 = ((f32[16,1,1]{2,1,0:T(1,128)}), f32[16,1,1]{2,1,0:T(1,128)S(1)}, u32[]{:S(2)}, u32[]{:S(2)}) async-start(f32[16,1,1]{2,1,0:T(1,128)} %broadcast_in_dim.27), calls=%async_computation.3 | async-start | bytes 16384 | tf_op jit(solution)/shard_map/all_to_all | solution.py:51
where the time goes:
time: 348 us; the launch traced here: 346 us
  local copies, waits for them, and re-layouts  95.3 us (27%)
  matrix products  85.5 us (25%)
  other arithmetic  85.2 us (24%)
  starting transfers between devices  37.6 us (11%)
  blocking collectives  20.3 us (6%)
  waiting for transfers between devices  14.5 us (4%)
  loops' own time  5.49 us (2%)
    dot_general x8, matrix products, add_rows(): lax.dot_general(bin_hot, grad_cols, dims, preferred_element_type=jnp.floa...  45 us
    eq x8, other arithmetic, add_rows(): codes_block[:, :, None] == bin_ids[None, None, :]  42.4 us
    dot_general x8, matrix products, add_rows(): lax.dot_general(bin_hot, weight_cols, dims, preferred_element_type=jnp.fl...  40.5 us
    scatter x1, local copies, waits for them, and re-layouts, place_rows(): buf_w = jnp.zeros((LEAVES * CAP,), weights.dtype).at[slot].set(weights)  28.6 us
    all_to_all x1, blocking collectives, summed_on_arrival(): lax.all_to_all(blocks, axis, split_axis=0, concat_axis=0, tiled=True)  20.3 us
    all_to_all x2, starting transfers between devices, from_everyone(): return lax.all_to_all(copies, axis, split_axis=0, concat_axis=0, tiled=True)  15.5 us
    unnamed x13, local copies, waits for them, and re-layouts  14 us
    transpose x1, local copies, waits for them, and re-layouts, split_up(): return jnp.moveaxis(array.reshape(*before, count, -1, *after), dim, 0)  13.9 us
  transfers between devices with their start and end apart: 5, of which 3 were waited for; matrix products, arithmetic and copies ran while one was open for 20% of the time, Pallas kernels for 0%

commit v1 on v0

v1 whole, which is shorter than its diff:
```python
import functools

import jax
import jax.numpy as jnp
from jax import lax
from jax.experimental import pallas as pl
from jax.experimental.pallas import tpu as pltpu
from jax.sharding import Mesh
from jax.sharding import PartitionSpec as P

BINS = 32
TARGETS = 16
LEAVES = 8
CAP = 1024
COLS = LEAVES * TARGETS
FEATURES = 512
HALF = FEATURES // 2
ROW_DEV = 4096
ROW_BLOCK = 512
PEERS = 64
OWNED = 4
PAIRS = BINS // 2
AUX = 32
AUX_CHUNK = HALF
AUX_ROWS = ROW_DEV // AUX_CHUNK * AUX
LANES = 2 * HALF
SENT = COLS + LEAVES
GRP = ("grp_0", "grp_1")
ROWS_GRP = ("rows_0", "rows_1", "grp_0", "grp_1")
ROWS = ("rows_0", "rows_1")
CHIPS = ("rows_0", "rows_1", "grp_0")
VMEM = 56 << 20
F32 = jnp.float32
BF16 = jnp.bfloat16
I32 = jnp.int32


def iota(shape, dim):
    return lax.broadcasted_iota(I32, shape, dim)


def params(**more):
    return pltpu.CompilerParams(vmem_limit_bytes=VMEM, **more)


def prep_kernel(core_ref, feature_ref, codes_ref, aux_ref, own_ref, send_ref, column_ref, select_ref):
    step = pl.program_id(0)
    blocks = ROW_DEV // ROW_BLOCK

    @pl.when(step == 0)
    def _():
        core = core_ref[0]
        lane = iota((FEATURES, FEATURES), 1)
        side = jnp.where(lane < HALF, core, 1 - core)
        place = lax.rem(lane, HALF)
        wanted = (place // OWNED) * (2 * OWNED) + side * OWNED + lax.rem(place, OWNED)
        select_ref[...] = jnp.where(iota((FEATURES, FEATURES), 0) == wanted, 1.0, 0.0).astype(BF16)

    @pl.when(step < blocks)
    def _():
        codes = codes_ref[...].astype(F32).astype(BF16)
        both = jnp.dot(codes, select_ref[...], preferred_element_type=F32).astype(BF16)
        own_ref[...] = both[:, :HALF]
        send_ref[...] = both[:, HALF:]
        hot = jnp.where(iota((8, FEATURES), 1) == feature_ref[0], 1.0, 0.0).astype(BF16)
        column_ref[...] = lax.dot_general(
            hot, codes, (((1,), (1,)), ((), ())), preferred_element_type=F32
        )

    @pl.when(step == blocks)
    def _():
        for i in range(ROW_DEV // AUX_CHUNK):
            part = aux_ref[:, i * AUX_CHUNK : (i + 1) * AUX_CHUNK]
            own_ref[i * AUX : (i + 1) * AUX, :] = part
            send_ref[i * AUX : (i + 1) * AUX, :] = part


def prep(core, split_feature, codes, aux):
    blocks = ROW_DEV // ROW_BLOCK
    smem = pl.BlockSpec(memory_space=pltpu.SMEM)
    buffer = jax.ShapeDtypeStruct((ROW_DEV + AUX_ROWS, HALF), BF16)
    return pl.pallas_call(
        prep_kernel,
        grid=(blocks + 1,),
        in_specs=[
            smem,
            smem,
            pl.BlockSpec((ROW_BLOCK, FEATURES), lambda i: (jnp.minimum(i, blocks - 1), 0)),
            pl.BlockSpec((AUX, ROW_DEV), lambda i: (0, 0)),
        ],
        out_specs=[
            pl.BlockSpec((ROW_BLOCK, HALF), lambda i: (i, 0)),
            pl.BlockSpec((ROW_BLOCK, HALF), lambda i: (i, 0)),
            pl.BlockSpec((8, ROW_BLOCK), lambda i: (0, jnp.minimum(i, blocks - 1))),
        ],
        out_shape=[buffer, buffer, jax.ShapeDtypeStruct((8, ROW_DEV), F32)],
        scratch_shapes=[pltpu.VMEM((FEATURES, FEATURES), BF16)],
        compiler_params=params(),
        cost_estimate=pl.CostEstimate(
            flops=2 * ROW_DEV * FEATURES * FEATURES,
            bytes_accessed=ROW_DEV * FEATURES * 6,
            transcendentals=0,
        ),
    )(core, split_feature, codes, aux)


def unpack_aux(rows_ref):
    parts = [
        rows_ref[ROW_DEV + i * AUX : ROW_DEV + (i + 1) * AUX, :]
        for i in range(ROW_DEV // AUX_CHUNK)
    ]
    return jnp.concatenate(parts, axis=1).astype(F32)


def spread(rows_ref, dup_ref, data_ref):
    lane = iota((HALF, LANES), 1)
    source = (lane // (2 * OWNED)) * OWNED + lax.rem(lane, OWNED)
    twice = jnp.where(iota((HALF, LANES), 0) == source, 1.0, 0.0).astype(BF16)
    for i in range(ROW_DEV // ROW_BLOCK):
        rows = slice(i * ROW_BLOCK, (i + 1) * ROW_BLOCK)
        dup_ref[rows, :] = jnp.dot(
            rows_ref[rows, :], twice, preferred_element_type=F32
        ).astype(BF16)
    aux = unpack_aux(rows_ref)
    grads, weights, leaf = (aux[:TARGETS], aux[TARGETS : TARGETS + 1], aux[TARGETS + 1 : TARGETS + 2])
    for l in range(LEAVES):
        data_ref[l * TARGETS : (l + 1) * TARGETS, :] = jnp.where(leaf == l, grads, 0.0).astype(BF16)
    ids = iota((TARGETS, ROW_DEV), 0).astype(F32)
    data_ref[COLS : COLS + TARGETS, :] = jnp.where(leaf == ids, weights, 0.0).astype(BF16)


def pair_sums(pair, dup_ref, data_ref):
    lane = iota((1, LANES), 1)
    wanted = (2 * pair + lax.rem(lane // OWNED, 2)).astype(F32).astype(BF16)
    hot = jnp.where(dup_ref[...] == wanted, jnp.ones((), BF16), jnp.zeros((), BF16))
    return jnp.dot(data_ref[...], hot, preferred_element_type=F32)[:SENT]


UNROLL = 2


def own_kernel(rows_ref, sums_ref, dup_ref, data_ref):
    step = pl.program_id(0)

    @pl.when(step == 0)
    def _():
        spread(rows_ref, dup_ref, data_ref)

    for i in range(UNROLL):
        sums_ref[i] = pair_sums(step * UNROLL + i, dup_ref, data_ref)


def both_kernel(rows_ref, sums_ref, out_ref, dup_ref, data_ref, weights_ref):
    step = pl.program_id(0)

    @pl.when(step == 0)
    def _():
        spread(rows_ref, dup_ref, data_ref)

    for i in range(UNROLL):
        pair = step * UNROLL + i
        sums = pair_sums(pair, dup_ref, data_ref) + sums_ref[i]
        at = pl.multiple_of(pair * 8, 8)
        out_ref[:, pl.ds(at, 8), :] = sums[:COLS].T.reshape(PEERS, 8, COLS)
        weights_ref[pl.ds(at, 8), :] = sums[COLS:]

    @pl.when(step == PAIRS // UNROLL - 1)
    def _():
        out_ref[:, COLS:, :] = weights_ref[...].T.reshape(PEERS, 8, COLS)


HIST_COST = pl.CostEstimate(
    flops=2 * ROW_DEV * HALF * BINS * 256, bytes_accessed=8 << 20, transcendentals=0
)


def own_sums(rows):
    return pl.pallas_call(
        own_kernel,
        grid=(PAIRS // UNROLL,),
        in_specs=[pl.BlockSpec(rows.shape, lambda i: (0, 0))],
        out_specs=pl.BlockSpec((UNROLL, SENT, LANES), lambda i: (i, 0, 0)),
        out_shape=jax.ShapeDtypeStruct((PAIRS, SENT, LANES), F32),
        scratch_shapes=[
            pltpu.VMEM((ROW_DEV, LANES), BF16),
            pltpu.VMEM((COLS + TARGETS, ROW_DEV), BF16),
        ],
        compiler_params=params(),
        cost_estimate=HIST_COST,
    )(rows)


def both_sums(rows, sums):
    return pl.pallas_call(
        both_kernel,
        grid=(PAIRS // UNROLL,),
        in_specs=[
            pl.BlockSpec(rows.shape, lambda i: (0, 0)),
            pl.BlockSpec((UNROLL, SENT, LANES), lambda i: (i, 0, 0)),
        ],
        out_specs=pl.BlockSpec((PEERS, SENT, COLS), lambda i: (0, 0, 0)),
        out_shape=jax.ShapeDtypeStruct((PEERS, SENT, COLS), F32),
        scratch_shapes=[
            pltpu.VMEM((ROW_DEV, LANES), BF16),
            pltpu.VMEM((COLS + TARGETS, ROW_DEV), BF16),
            pltpu.VMEM((COLS, LANES), F32),
        ],
        compiler_params=params(),
        cost_estimate=HIST_COST,
    )(rows, sums)


def place_kernel(bin_ref, aux_ref, column_ref, out_ref):
    aux = aux_ref[...].astype(F32)
    grads, weights, leaf = (aux[:TARGETS], aux[TARGETS : TARGETS + 1], aux[TARGETS + 1 : TARGETS + 2])
    child = jnp.where(column_ref[0:1, :] > bin_ref[0].astype(F32), 1.0, 0.0)
    key = leaf * 2 + child
    keys = 2 * LEAVES
    hot = jnp.where(iota((keys, ROW_DEV), 0).astype(F32) == key, 1.0, 0.0)
    width = 256
    earlier = jnp.where(iota((width, width), 0) < iota((width, width), 1), 1.0, 0.0).astype(BF16)
    counts = jnp.zeros((keys, 1), F32)
    ranks = []
    for i in range(ROW_DEV // width):
        part = hot[:, i * width : (i + 1) * width]
        before = jnp.dot(part.astype(BF16), earlier, preferred_element_type=F32) + counts
        ranks.append(jnp.sum(part * before, axis=0, keepdims=True))
        counts = counts + jnp.sum(part, axis=1, keepdims=True)
    rank = jnp.concatenate(ranks, axis=1)
    sibling = iota((keys, ROW_DEV), 0).astype(F32) == leaf * 2
    first = jnp.sum(jnp.where(sibling, counts, 0.0), axis=0, keepdims=True)
    slot = (leaf * CAP + rank + child * first).astype(I32)
    dims = (((1,), (1,)), ((), ()))
    group = 128 // TARGETS
    tiled = jnp.concatenate([grads] * group, axis=0)
    own = iota((128, ROW_DEV), 0) // TARGETS == slot % group
    values = jnp.where(own, tiled, 0.0).astype(BF16)
    line = iota((CAP // group, ROW_DEV), 0)
    for l in range(LEAVES):
        pick = jnp.where(line + l * (CAP // group) == slot // group, 1.0, 0.0).astype(BF16)
        moved = lax.dot_general(pick, values, dims, preferred_element_type=F32)
        out_ref[l, :COLS, :] = moved.astype(BF16)
    lane_values = jnp.where(iota((128, ROW_DEV), 0) == slot % 128, weights, 0.0).astype(BF16)
    pick = jnp.where(iota((LEAVES * CAP // 128, ROW_DEV), 0) == slot // 128, 1.0, 0.0).astype(BF16)
    moved = lax.dot_general(pick, lane_values, dims, preferred_element_type=F32)
    for l in range(LEAVES):
        part = jnp.concatenate([moved[l * 8 : (l + 1) * 8], jnp.zeros((8, 128), F32)], axis=0)
        out_ref[l, COLS:, :] = part.astype(BF16)


def place_rows(split_bin, aux, column):
    return pl.pallas_call(
        place_kernel,
        in_specs=[
            pl.BlockSpec(memory_space=pltpu.SMEM),
            pl.BlockSpec(aux.shape, lambda: (0, 0)),
            pl.BlockSpec(column.shape, lambda: (0, 0)),
        ],
        out_specs=pl.BlockSpec((LEAVES, COLS + 16, 128), lambda: (0, 0, 0)),
        out_shape=jax.ShapeDtypeStruct((LEAVES, COLS + 16, 128), BF16),
        compiler_params=params(),
        cost_estimate=pl.CostEstimate(
            flops=2 * LEAVES * CAP * ROW_DEV * 32, bytes_accessed=1 << 20, transcendentals=0
        ),
    )(split_bin, aux, column)


def gain_kernel(parts_ref, out_ref):
    total = lax.fori_loop(
        1, PEERS, lambda i, so_far: so_far + parts_ref[i], parts_ref[0], unroll=4
    )
    expand = jnp.where(
        iota((COLS, PAIRS * COLS), 0) == iota((COLS, PAIRS * COLS), 1) // TARGETS, 1.0, 0.0
    )
    spread_w = jnp.dot(
        total[COLS:], expand, preferred_element_type=F32, precision=lax.Precision.HIGHEST
    )
    grads = [total[i * 8 : (i + 1) * 8] for i in range(PAIRS)]
    weights = [spread_w[:, i * COLS : (i + 1) * COLS] for i in range(PAIRS)]
    row = iota((8, COLS), 0)
    even = row < OWNED

    def sides(values):
        swapped = [pltpu.roll(v, OWNED, 0) for v in values]
        both = [v + s for v, s in zip(values, swapped)]
        left, right = ([], [])
        below = jnp.zeros((8, COLS), F32)
        for v, b in zip(values, both):
            left.append(below + jnp.where(even, v, b))
            below = below + b
        above = jnp.zeros((8, COLS), F32)
        for s, b in zip(reversed(swapped), reversed(both)):
            right.append(above + jnp.where(even, s, 0.0))
            above = above + b
        return (left, right[::-1])

    left_g, right_g = sides(grads)
    left_w, right_w = sides(weights)
    place = lax.rem(row, OWNED) * BINS + row // OWNED
    gains = jnp.zeros((8, COLS), F32)
    for i in range(PAIRS):
        x, y = (left_w[i] + 1.0, right_w[i] + 1.0)
        diff = left_g[i] * y - right_g[i] * x
        terms = diff * diff / (x * y * (x + y))
        sums = jnp.sum(terms, axis=1, keepdims=True)
        gains = gains + jnp.where(iota((8, COLS), 1) == place + 2 * i, sums, 0.0)
    out_ref[...] = jnp.sum(gains, axis=0, keepdims=True) / (LEAVES * TARGETS)


def owned_gains(parts):
    return pl.pallas_call(
        gain_kernel,
        out_shape=jax.ShapeDtypeStruct((1, OWNED * BINS), F32),
        in_specs=[pl.BlockSpec(parts.shape, lambda: (0, 0, 0))],
        out_specs=pl.BlockSpec((1, OWNED * BINS), lambda: (0, 0)),
        compiler_params=params(),
    )(parts)


def exchange(blocks, axis):
    return lax.all_to_all(blocks, axis, split_axis=0, concat_axis=0, tiled=True)


def shards(bin_codes, leaf_index, gradients, row_weights, split_feature, split_bin):
    core = lax.axis_index("grp_1").astype(I32).reshape(1)
    aux = jnp.concatenate(
        [
            gradients.T,
            row_weights[None, :],
            leaf_index.reshape(1, ROW_DEV).astype(BF16),
            jnp.zeros((AUX - TARGETS - 2, ROW_DEV), BF16),
        ],
        axis=0,
    )
    own, send, column = prep(core, split_feature, bin_codes, aux)
    other = lax.ppermute(send, "grp_1", [(0, 1), (1, 0)])
    sums = both_sums(other, own_sums(own))
    arrived = exchange(sums, CHIPS)
    moved = exchange(place_rows(split_bin, aux, column), GRP)
    gains = owned_gains(arrived)
    everyone = exchange(jnp.broadcast_to(gains[None], (128, 1, OWNED * BINS)), ROWS_GRP)
    group = lax.axis_index(ROWS)
    table = lax.dynamic_slice_in_dim(everyone, group * 8, 8, 0).reshape(-1)
    best = jnp.max(everyone).reshape(1)
    moved_gradients = moved[:, :COLS].reshape(1, -1)
    moved_weights = moved[:, COLS : COLS + 8].reshape(1, -1)
    return (table, best, moved_gradients, moved_weights)


def solution(mesh):
    torus = Mesh(mesh.devices.reshape(4, 4, 4, 2), ("rows_0", "rows_1", "grp_0", "grp_1"))
    in_specs = (P(ROWS_GRP, None), P(ROWS_GRP, None), P(ROWS_GRP, None), P(ROWS_GRP), P(), P())
    out_specs = (P(ROWS), P(), P(ROWS_GRP, None), P(ROWS_GRP, None))
    return jax.shard_map(
        shards, mesh=torus, in_specs=in_specs, out_specs=out_specs, check_vma=False
    )
```

time: 348 us -> 154 us (0.44)
  local copies, waits for them, and re-layouts: 95.3 us -> 5.71 us
  matrix products: 85.5 us -> 0 us
  other arithmetic: 85.2 us -> 3.06 us
  Pallas kernels: 0 us -> 51.5 us
  waiting for transfers between devices: 14.5 us -> 64.3 us
  blocking collectives: 20.3 us -> 0 us
  starting transfers between devices: 37.6 us -> 26.3 us
  loops' own time: 5.49 us -> 0 us
    dot_general x16 -> x0, matrix products: 85.5 us -> none  [the longest x8 45 us: add_rows(): lax.dot_general(bin_hot, grad_cols, dims, preferred_element_type=jnp.floa...]
    pallas_call x0 -> x5, Pallas kernels: none -> 51.5 us  [the longest x1 17.9 us: both_sums(): pl.pallas_call(both_kernel, grid=(PAIRS // UNROLL,), in_specs=[pl.BlockSp...]
    all_to_all x5 -> x3, waiting for transfers between devices: 14.5 us -> 64.3 us  [exchange(): return lax.all_to_all(blocks, axis, split_axis=0, concat_axis=0, tiled=True)]
    eq x8 -> x0, other arithmetic: 42.4 us -> none  [add_rows(): codes_block[:, :, None] == bin_ids[None, None, :]]
    scatter x2 -> x0, local copies, waits for them, and re-layouts: 40.4 us -> none  [the longest x1 28.6 us: place_rows(): buf_w = jnp.zeros((LEAVES * CAP,), weights.dtype).at[slot].set(weights)]
    all_to_all x1 -> x0, blocking collectives: 20.3 us -> none  [summed_on_arrival(): lax.all_to_all(blocks, axis, split_axis=0, concat_axis=0, tiled=True)]
    dynamic_slice x16 -> x1, local copies, waits for them, and re-layouts: 15 us -> 0.59 us  [shards(): table = lax.dynamic_slice_in_dim(everyone, group * 8, 8, 0).reshape(-1)]
    another operation x7 -> x0, other arithmetic: 14 us -> none  [the longest x1 7.63 us: split_scores(): upper_g = jnp.flip(jnp.cumsum(jnp.flip(grad_hist, axis=1), axis=1), axis=1)]
  transfers between devices with their start and end apart: 5 -> 4, of which waited for: 3 -> 3; matrix products, arithmetic and copies ran while one was open for 20% -> 1% of each run, Pallas kernels for 0% -> 16%
where the time goes in v1:
time: 154 us; the launch traced here: 153 us
  waiting for transfers between devices  64.3 us (42%)
  Pallas kernels  51.5 us (33%)
  starting transfers between devices  26.3 us (17%)
  local copies, waits for them, and re-layouts  5.71 us (4%)
  other arithmetic  3.06 us (2%)
  between operations  1.98 us (1%)
    all_to_all x3, waiting for transfers between devices, exchange(): return lax.all_to_all(blocks, axis, split_axis=0, concat_axis=0, tiled=True)  64.3 us
    all_to_all x3, starting transfers between devices, exchange(): return lax.all_to_all(blocks, axis, split_axis=0, concat_axis=0, tiled=True)  24.8 us
    pallas_call x1, Pallas kernels, both_sums(): pl.pallas_call(both_kernel, grid=(PAIRS // UNROLL,), in_specs=[pl.BlockSp...  17.9 us
    pallas_call x1, Pallas kernels, own_sums(): pl.pallas_call(own_kernel, grid=(PAIRS // UNROLL,), in_specs=[pl.BlockSpe...  15.6 us
    pallas_call x1, Pallas kernels, prep(): pl.pallas_call(prep_kernel, grid=(blocks + 1,), in_specs=[smem, smem, pl....  9.56 us
    pallas_call x1, Pallas kernels, place_rows(): pl.pallas_call(place_kernel, in_specs=[pl.BlockSpec(memory_space=pltpu.SM...  4.85 us
    pallas_call x1, Pallas kernels, owned_gains(): pl.pallas_call(gain_kernel, out_shape=jax.ShapeDtypeStruct((1, OWNED * BI...  3.59 us
  transfers between devices with their start and end apart: 4, of which 3 were waited for; matrix products, arithmetic and copies ran while one was open for 1% of the time, Pallas kernels for 16%

profile of v1, /device:TPU:1, one launch (start us, length us, event | category | flops | bytes accessed | tf_op | source)
XLA Modules:
  0.0 152.8 jit_solution(1874036574121806518)
XLA Ops:
  0.6 0.7 broadcast_in_dim.14
  1.3 0.7 convert_bitcast_fusion
  2.7 0.1 pad.3.clone
  2.8 1.7 %maximum_maximum_fusion.aux_ref = bf16[32,4096]{1,0:T(8,128)(2,1)} fusion(bf16[1,4096]{1,0:T(2,128)(2,1)S(1)} %convert_bitcast_fusion, bf16[1,4096]{1,0:T(2,128)(2,1)S(1)} %broadcast_in_dim.14, bf16[16,4096]{1,0:T(8,128)(2,1)} %bitcast.9, bf16[32]{0:T(256)(128)(2,1)S(1)} %pad.3.clone), kind=kLoop, calls=%fused_computation | loop fusion | flops 1048576 | bytes 409664 | tf_op jit(solution)/shard_map/concatenate | solution.py:326
  4.5 9.6 %shard_map.93 = (bf16[4608,256]{1,0:T(8,128)(2,1)}, bf16[4608,256]{1,0:T(8,128)(2,1)}, f32[8,4096]{1,0:T(8,128)}) custom-call(s32[1]{0:T(128)} %bitcast.core_ref, s32[1]{0:T(128)S(6)} %copy.11.feature_ref, s32[4096,512]{1,0:T(8,128)} %codes_ref.1, bf16[32,4096]{1,0:T(8,128)(2,1)} %maximum_maximum_fusion.aux_ref), custom_call_target="tpu_custom_call" | custom-call | flops 2147483648 | bytes 12582912 | tf_op jit(solution)/shard_map/pallas_call | solution.py:82
  14.1 1.4 collective-permute-start
  15.5 15.6 %shard_map.94.sums_ref = f32[16,136,512]{2,1,0:T(8,128)} custom-call(bf16[4608,256]{1,0:T(8,128)(2,1)} %get-tuple-element.8.rows_ref), custom_call_target="tpu_custom_call" | custom-call | flops 17179869184 | bytes 8388608 | tf_op jit(solution)/shard_map/pallas_call | solution.py:178
  31.1 0.0 collective-permute-done.rows_ref
  31.1 0.0 copy-start
  31.1 1.5 copy-done
  32.5 17.9 %shard_map.95 = f32[64,136,128]{2,1,0:T(8,128)} custom-call(bf16[4608,256]{1,0:T(8,128)(2,1)} %copy-done, f32[16,136,512]{2,1,0:T(8,128)} %shard_map.94.sums_ref), custom_call_target="tpu_custom_call" | custom-call | flops 17179869184 | bytes 8388608 | tf_op jit(solution)/shard_map/pallas_call | solution.py:194
  50.5 11.4 %all-to-all-start = ((f32[64,136,128]{2,1,0:T(8,128)}), f32[64,136,128]{2,1,0:T(8,128)}, u32[]{:S(2)}, u32[]{:S(2)}) async-start(f32[64,136,128]{2,1,0:T(8,128)} %shard_map.95), calls=%async_computation | async-start | bytes 8912896 | tf_op jit(solution)/shard_map/all_to_all | solution.py:321
  62.5 4.9 %shard_map.97 = bf16[8,144,128]{2,1,0:T(8,128)(2,1)} custom-call(s32[1]{0:T(128)S(6)} %copy.12.bin_ref, bf16[32,4096]{1,0:T(8,128)(2,1)} %maximum_maximum_fusion.aux_ref, f32[8,4096]{1,0:T(8,128)} %get-tuple-element.9.column_ref), custom_call_target="tpu_custom_call" | custom-call | flops 2147483648 | bytes 1048576 | tf_op jit(solution)/shard_map/pallas_call | solution.py:252
  67.4 53.1 %all-to-all-done.parts_ref = f32[64,136,128]{2,1,0:T(8,128)} async-done(((f32[64,136,128]{2,1,0:T(8,128)}), f32[64,136,128]{2,1,0:T(8,128)}, u32[]{:S(2)}, u32[]{:S(2)}) %all-to-all-start) | async-done | bytes 4456480 | tf_op jit(solution)/shard_map/all_to_all | solution.py:321
  120.5 6.1 %all-to-all-start.2 = ((bf16[8,144,128]{2,1,0:T(8,128)(2,1)}), bf16[8,144,128]{2,1,0:T(8,128)(2,1)S(1)}, u32[]{:S(2)}, u32[]{:S(2)}) async-start(bf16[8,144,128]{2,1,0:T(8,128)(2,1)} %shard_map.97), calls=%async_computation.2 | async-start | bytes 589824 | tf_op jit(solution)/shard_map/all_to_all | solution.py:321
  126.7 3.6 %shard_map.96 = f32[1,128]{1,0:T(1,128)} custom-call(f32[64,136,128]{2,1,0:T(8,128)} %all-to-all-done.parts_ref), custom_call_target="tpu_custom_call" | custom-call | tf_op jit(solution)/shard_map/pallas_call | solution.py:311
  130.2 3.2 %all-to-all-done.2 = bf16[8,144,128]{2,1,0:T(8,128)(2,1)S(1)} async-done(((bf16[8,144,128]{2,1,0:T(8,128)(2,1)}), bf16[8,144,128]{2,1,0:T(8,128)(2,1)S(1)}, u32[]{:S(2)}, u32[]{:S(2)}) %all-to-all-start.2) | async-done | bytes 294944 | tf_op jit(solution)/shard_map/all_to_all | solution.py:321
  133.5 1.3 broadcast_in_dim.17
  134.8 7.3 %all-to-all-start.1 = ((f32[128,1,128]{2,1,0:T(1,128)}), f32[128,1,128]{2,1,0:T(1,128)S(1)}, u32[]{:S(2)}, u32[]{:S(2)}) async-start(f32[128,1,128]{2,1,0:T(1,128)} %broadcast_in_dim.17), calls=%async_computation.1 | async-start | bytes 131072 | tf_op jit(solution)/shard_map/all_to_all | solution.py:321
  142.1 0.9 reshape.43
  143.0 0.6 reshape.44
  143.6 7.9 %all-to-all-done.1 = f32[128,1,128]{2,1,0:T(1,128)S(1)} async-done(((f32[128,1,128]{2,1,0:T(1,128)}), f32[128,1,128]{2,1,0:T(1,128)S(1)}, u32[]{:S(2)}, u32[]{:S(2)}) %all-to-all-start.1) | async-done | bytes 65568 | tf_op jit(solution)/shard_map/all_to_all | solution.py:321
  151.6 0.6 reduce_max.9
  152.2 0.6 constant_dynamic-slice_fusion
  (3 shorter events, 0.0 us)
Async XLA Ops:
  14.1 17.0 %collective-permute-start = (bf16[4608,256]{1,0:T(8,128)(2,1)}, bf16[4608,256]{1,0:T(8,128)(2,1)S(1)}, u32[]{:S(2)}, u32[]{:S(2)}) collective-permute-start(bf16[4608,256]{1,0:T(8,128)(2,1)} %get-tuple-element.7), channel_id=1, source_target_pairs={{0,1},{1,0},{2,3},{3,2},{4,5},{5,4},{6,7},{7,6},{8,9},{9,8},{10,11... | collective-permute-start | bytes 7077896 | tf_op jit(solution)/shard_map/ppermute | solution.py:336
  31.1 1.5 copy-start
  50.5 70.1 %all-to-all-start = ((f32[64,136,128]{2,1,0:T(8,128)}), f32[64,136,128]{2,1,0:T(8,128)}, u32[]{:S(2)}, u32[]{:S(2)}) async-start(f32[64,136,128]{2,1,0:T(8,128)} %shard_map.95), calls=%async_computation | async-start | bytes 8912896 | tf_op jit(solution)/shard_map/all_to_all | solution.py:321
  120.5 12.9 %all-to-all-start.2 = ((bf16[8,144,128]{2,1,0:T(8,128)(2,1)}), bf16[8,144,128]{2,1,0:T(8,128)(2,1)S(1)}, u32[]{:S(2)}, u32[]{:S(2)}) async-start(bf16[8,144,128]{2,1,0:T(8,128)(2,1)} %shard_map.97), calls=%async_computation.2 | async-start | bytes 589824 | tf_op jit(solution)/shard_map/all_to_all | solution.py:321
  134.8 16.8 %all-to-all-start.1 = ((f32[128,1,128]{2,1,0:T(1,128)}), f32[128,1,128]{2,1,0:T(1,128)S(1)}, u32[]{:S(2)}, u32[]{:S(2)}) async-start(f32[128,1,128]{2,1,0:T(1,128)} %broadcast_in_dim.17), calls=%async_computation.1 | async-start | bytes 131072 | tf_op jit(solution)/shard_map/all_to_all | solution.py:321

commit v2 on v1

v2 whole, which is shorter than its diff:
```python
import jax
import jax.numpy as jnp
from jax import lax
from jax.experimental import pallas as pl
from jax.experimental.pallas import tpu as pltpu
from jax.sharding import Mesh
from jax.sharding import PartitionSpec as P

BINS = 32
TARGETS = 16
LEAVES = 8
CAP = 1024
COLS = LEAVES * TARGETS
FEATURES = 512
HALF = FEATURES // 2
ROW_DEV = 4096
ROW_BLOCK = 512
PEERS = 64
OWNED = 4
PAIRS = BINS // 2
AUX = 32
AUX_CHUNK = HALF
AUX_ROWS = ROW_DEV // AUX_CHUNK * AUX
LANES = 2 * HALF
SENT = COLS + LEAVES
GRP = ("grp_0", "grp_1")
ROWS_GRP = ("rows_0", "rows_1", "grp_0", "grp_1")
ROWS = ("rows_0", "rows_1")
CHIPS = ("rows_0", "rows_1", "grp_0")
F32 = jnp.float32
BF16 = jnp.bfloat16
I32 = jnp.int32


def iota(shape, dim):
    return lax.broadcasted_iota(I32, shape, dim)


def params(mib):
    return pltpu.CompilerParams(vmem_limit_bytes=mib << 20)


def prep_kernel(
    core_ref, feature_ref, codes_ref, grads_ref, weights_ref, leaf_ref, own_ref, send_ref, column_ref, aux_ref, select_ref
):
    step = pl.program_id(0)
    blocks = ROW_DEV // ROW_BLOCK

    @pl.when(step == 0)
    def _():
        core = core_ref[0]
        lane = iota((1, FEATURES), 1)
        side = jnp.where(lane < HALF, core, 1 - core)
        place = lane & (HALF - 1)
        wanted = ((place >> 2) << 3) + (side << 2) + (place & 3)
        select_ref[...] = jnp.where(iota((FEATURES, FEATURES), 0) == wanted, 1.0, 0.0).astype(BF16)

    @pl.when(step < blocks)
    def _():
        codes = codes_ref[...].astype(F32).astype(BF16)
        both = jnp.dot(codes, select_ref[...], preferred_element_type=F32).astype(BF16)
        own_ref[...] = both[:, :HALF]
        send_ref[...] = both[:, HALF:]
        hot = jnp.where(iota((8, FEATURES), 1) == feature_ref[0], 1.0, 0.0).astype(BF16)
        column_ref[...] = lax.dot_general(
            hot, codes, (((1,), (1,)), ((), ())), preferred_element_type=F32
        )

    @pl.when(step == blocks)
    def _():
        weights = weights_ref[...].astype(F32)
        leaf = leaf_ref[...].astype(F32)
        row = iota((TARGETS, AUX_CHUNK), 0)
        for i in range(ROW_DEV // AUX_CHUNK):
            lanes = slice(i * AUX_CHUNK, (i + 1) * AUX_CHUNK)
            weight = jnp.concatenate([weights[2 * i : 2 * i + 1], weights[2 * i + 1 : 2 * i + 2]], axis=1)
            rest = jnp.where(row == 0, weight, jnp.where(row == 1, leaf[:, lanes], 0.0)).astype(BF16)
            for ref in (own_ref, send_ref, aux_ref):
                ref[i * AUX : i * AUX + TARGETS, :] = grads_ref[:, lanes]
                ref[i * AUX + TARGETS : (i + 1) * AUX, :] = rest


def prep(core, split_feature, codes, grads, weights, leaf):
    blocks = ROW_DEV // ROW_BLOCK
    smem = pl.BlockSpec(memory_space=pltpu.SMEM)
    buffer = jax.ShapeDtypeStruct((ROW_DEV + AUX_ROWS, HALF), BF16)
    return pl.pallas_call(
        prep_kernel,
        grid=(blocks + 1,),
        in_specs=[
            smem,
            smem,
            pl.BlockSpec((ROW_BLOCK, FEATURES), lambda i: (jnp.minimum(i, blocks - 1), 0)),
            pl.BlockSpec(grads.shape, lambda i: (0, 0)),
            pl.BlockSpec(weights.shape, lambda i: (0, 0)),
            pl.BlockSpec(leaf.shape, lambda i: (0, 0)),
        ],
        out_specs=[
            pl.BlockSpec((ROW_BLOCK, HALF), lambda i: (i, 0)),
            pl.BlockSpec((ROW_BLOCK, HALF), lambda i: (i, 0)),
            pl.BlockSpec((8, ROW_BLOCK), lambda i: (0, jnp.minimum(i, blocks - 1))),
            pl.BlockSpec((AUX_ROWS, HALF), lambda i: (0, 0)),
        ],
        out_shape=[
            buffer,
            buffer,
            jax.ShapeDtypeStruct((8, ROW_DEV), F32),
            jax.ShapeDtypeStruct((AUX_ROWS, HALF), BF16),
        ],
        scratch_shapes=[pltpu.VMEM((FEATURES, FEATURES), BF16)],
        compiler_params=params(56),
        cost_estimate=pl.CostEstimate(
            flops=2 * ROW_DEV * FEATURES * FEATURES,
            bytes_accessed=ROW_DEV * FEATURES * 6,
            transcendentals=0,
        ),
    )(core, split_feature, codes, grads, weights, leaf)


def unpack_aux(rows_ref, at):
    parts = [
        rows_ref[at + i * AUX : at + (i + 1) * AUX, :]
        for i in range(ROW_DEV // AUX_CHUNK)
    ]
    return jnp.concatenate(parts, axis=1).astype(F32)


def spread(rows_ref, dup_ref, data_ref):
    lane = iota((1, LANES), 1)
    source = ((lane >> 3) << 2) + (lane & 3)
    twice = jnp.where(iota((HALF, LANES), 0) == source, 1.0, 0.0).astype(BF16)
    for i in range(ROW_DEV // ROW_BLOCK):
        rows = slice(i * ROW_BLOCK, (i + 1) * ROW_BLOCK)
        dup_ref[rows, :] = jnp.dot(
            rows_ref[rows, :], twice, preferred_element_type=F32
        ).astype(BF16)
    aux = unpack_aux(rows_ref, ROW_DEV)
    grads, weights, leaf = (aux[:TARGETS], aux[TARGETS : TARGETS + 1], aux[TARGETS + 1 : TARGETS + 2])
    for l in range(LEAVES):
        data_ref[l * TARGETS : (l + 1) * TARGETS, :] = jnp.where(leaf == l, grads, 0.0).astype(BF16)
    ids = iota((TARGETS, ROW_DEV), 0).astype(F32)
    data_ref[COLS : COLS + TARGETS, :] = jnp.where(leaf == ids, weights, 0.0).astype(BF16)


def pair_sums(pair, dup_ref, data_ref):
    lane = iota((1, LANES), 1)
    wanted = (2 * pair + ((lane >> 2) & 1)).astype(F32).astype(BF16)
    hot = jnp.where(dup_ref[...] == wanted, jnp.ones((), BF16), jnp.zeros((), BF16))
    return jnp.dot(data_ref[...], hot, preferred_element_type=F32)[:SENT]


UNROLL = 4
BITS = 15.0
MESSAGE = COLS + 16


def own_kernel(rows_ref, sums_ref, dup_ref, data_ref):
    step = pl.program_id(0)

    @pl.when(step == 0)
    def _():
        spread(rows_ref, dup_ref, data_ref)

    for i in range(UNROLL):
        sums_ref[i] = pair_sums(step * UNROLL + i, dup_ref, data_ref)


def both_kernel(rows_ref, sums_ref, out_ref, dup_ref, data_ref, total_ref, largest_ref, weights_ref):
    step = pl.program_id(0)

    @pl.when(step == 0)
    def _():
        spread(rows_ref, dup_ref, data_ref)
        largest_ref[...] = jnp.zeros(largest_ref.shape, F32)

    for i in range(UNROLL):
        pair = step * UNROLL + i
        sums = pair_sums(pair, dup_ref, data_ref) + sums_ref[i]
        at = pl.multiple_of(pair * 8, 8)
        turned = sums[:COLS].T.reshape(PEERS, 8, COLS)
        total_ref[:, pl.ds(at, 8), :] = turned
        largest_ref[...] = jnp.maximum(largest_ref[...], jnp.abs(turned))
        weights_ref[pl.ds(at, 8), :] = sums[COLS:]

    @pl.when(step == PAIRS // UNROLL - 1)
    def _():
        weights = weights_ref[...].T.reshape(PEERS, 8, COLS)
        most = jnp.abs(weights)
        for lanes in (8, 16, 32, 64):
            most = jnp.maximum(most, pltpu.roll(most, lanes, 2))
        exp_g, exp_w = (exponents(largest_ref[...]), exponents(most))
        scale_g, scale_w = (jnp.exp2(BITS - exp_g), jnp.exp2(BITS - exp_w))
        for i in range(COLS // 16):
            rows = slice(i * 16, (i + 1) * 16)
            twice = jnp.concatenate([scale_g, scale_g], axis=1)
            out_ref[:, rows, :] = whole(total_ref[:, rows, :] * twice)
        even = iota((PEERS, 8, COLS), 1) < OWNED
        last = [weights * scale_w, jnp.where(even, exp_g, exp_w)]
        out_ref[:, COLS:, :] = whole(jnp.concatenate(last, axis=1))


def exponents(magnitudes):
    most = jnp.maximum(magnitudes, pltpu.roll(magnitudes, OWNED, 1))
    return jnp.ceil(jnp.log2(jnp.maximum(most, 1e-30)) + 0.001)


def whole(values):
    return jnp.round(values).astype(I32).astype(jnp.int16)


HIST_COST = pl.CostEstimate(
    flops=2 * ROW_DEV * HALF * BINS * 256, bytes_accessed=8 << 20, transcendentals=0
)


def own_sums(rows):
    return pl.pallas_call(
        own_kernel,
        grid=(PAIRS // UNROLL,),
        in_specs=[pl.BlockSpec(rows.shape, lambda i: (0, 0))],
        out_specs=pl.BlockSpec((UNROLL, SENT, LANES), lambda i: (i, 0, 0)),
        out_shape=jax.ShapeDtypeStruct((PAIRS, SENT, LANES), F32),
        scratch_shapes=[
            pltpu.VMEM((ROW_DEV, LANES), BF16),
            pltpu.VMEM((COLS + TARGETS, ROW_DEV), BF16),
        ],
        compiler_params=params(36),
        cost_estimate=HIST_COST,
    )(rows)


def both_sums(rows, sums):
    return pl.pallas_call(
        both_kernel,
        grid=(PAIRS // UNROLL,),
        in_specs=[
            pl.BlockSpec(rows.shape, lambda i: (0, 0)),
            pl.BlockSpec((UNROLL, SENT, LANES), lambda i: (i, 0, 0)),
        ],
        out_specs=pl.BlockSpec((PEERS, MESSAGE, COLS), lambda i: (0, 0, 0)),
        out_shape=pltpu.HBM((PEERS, MESSAGE, COLS), jnp.int16),
        scratch_shapes=[
            pltpu.VMEM((ROW_DEV, LANES), BF16),
            pltpu.VMEM((COLS + TARGETS, ROW_DEV), BF16),
            pltpu.VMEM((PEERS, COLS, COLS), F32),
            pltpu.VMEM((PEERS, 8, COLS), F32),
            pltpu.VMEM((COLS, LANES), F32),
        ],
        compiler_params=params(40),
        cost_estimate=HIST_COST,
    )(rows, sums)


def place_kernel(core_ref, bin_ref, aux_ref, column_ref, keep_ref, give_ref):
    core = core_ref[0]
    aux = unpack_aux(aux_ref, 0)
    grads, weights, leaf = (aux[:TARGETS], aux[TARGETS : TARGETS + 1], aux[TARGETS + 1 : TARGETS + 2])
    child = jnp.where(column_ref[0:1, :] > bin_ref[0].astype(F32), 1.0, 0.0)
    key = leaf * 2 + child
    keys = 2 * LEAVES
    hot = jnp.where(iota((keys, ROW_DEV), 0).astype(F32) == key, 1.0, 0.0)
    width = 256
    earlier = jnp.where(iota((width, width), 0) < iota((width, width), 1), 1.0, 0.0).astype(BF16)
    counts = jnp.zeros((keys, 1), F32)
    ranks = []
    for i in range(ROW_DEV // width):
        part = hot[:, i * width : (i + 1) * width]
        before = jnp.dot(part.astype(BF16), earlier, preferred_element_type=F32) + counts
        ranks.append(jnp.sum(part * before, axis=0, keepdims=True))
        counts = counts + jnp.sum(part, axis=1, keepdims=True)
    rank = jnp.concatenate(ranks, axis=1)
    sibling = iota((keys, ROW_DEV), 0).astype(F32) == leaf * 2
    first = jnp.sum(jnp.where(sibling, counts, 0.0), axis=0, keepdims=True)
    slot = (leaf * CAP + rank + child * first).astype(I32)
    dims = (((1,), (1,)), ((), ()))
    group = 128 // TARGETS
    tiled = jnp.concatenate([grads] * group, axis=0)
    values = jnp.where(iota((128, 1), 0) >> 4 == (slot & (group - 1)), tiled, 0.0).astype(BF16)
    lines = CAP // group
    line = iota((lines, 1), 0)
    for l in range(LEAVES):
        target = 2 * (l % 4) + (core if l < 4 else 1 - core)
        out_ref = keep_ref if l < 4 else give_ref
        pick = jnp.where(line == (slot >> 3) - target * lines, 1.0, 0.0).astype(BF16)
        moved = lax.dot_general(pick, values, dims, preferred_element_type=F32)
        out_ref[l % 4, :COLS, :] = moved.astype(BF16)
    lane_values = jnp.where(iota((128, 1), 0) == (slot & 127), weights, 0.0).astype(BF16)
    blocks = CAP // 128
    for l in range(LEAVES):
        target = 2 * (l % 4) + (core if l < 4 else 1 - core)
        out_ref = keep_ref if l < 4 else give_ref
        pick = jnp.where(iota((16, 1), 0) == (slot >> 7) - target * blocks, 1.0, 0.0)
        pick = jnp.where(iota((16, 1), 0) < blocks, pick, 0.0).astype(BF16)
        moved = lax.dot_general(pick, lane_values, dims, preferred_element_type=F32)
        out_ref[l % 4, COLS:, :] = moved.astype(BF16)


def place_rows(core, split_bin, aux, column):
    smem = pl.BlockSpec(memory_space=pltpu.SMEM)
    block = jax.ShapeDtypeStruct((LEAVES // 2, COLS + 16, 128), BF16)
    spec = pl.BlockSpec(block.shape, lambda i: (0, 0, 0))
    return pl.pallas_call(
        place_kernel,
        grid=(1,),
        in_specs=[
            smem,
            smem,
            pl.BlockSpec(aux.shape, lambda i: (0, 0)),
            pl.BlockSpec(column.shape, lambda i: (0, 0)),
        ],
        out_specs=[spec, spec],
        out_shape=[block, block],
        compiler_params=params(24),
        cost_estimate=pl.CostEstimate(
            flops=2 * LEAVES * CAP * ROW_DEV * 32, bytes_accessed=1 << 20, transcendentals=0
        ),
    )(core, split_bin, aux, column)


def deliver(keep, give):
    core, chip = (lax.axis_index("grp_1"), lax.axis_index("grp_0"))
    got = lax.ppermute(give, "grp_1", [(0, 1), (1, 0)])
    first = jnp.where(core == 0, keep, got)
    second = jnp.where(core == 0, got, keep)
    blocks = jnp.stack([first, second], axis=1)
    arrived = []
    for s in range(4):
        block = lax.dynamic_index_in_dim(blocks, (chip + s) % 4, 0, keepdims=False)
        if s:
            block = lax.ppermute(block, "grp_0", [(i, (i + s) % 4) for i in range(4)])
        arrived.append(block)
    turned = jnp.stack([arrived[0], arrived[3], arrived[2], arrived[1]] * 2)
    ordered = lax.dynamic_slice_in_dim(turned, (4 - chip) % 4, 4, 0)
    return ordered.reshape(8, COLS + 16, 128)


def gain_kernel(parts_ref, out_ref):
    upper = iota((8, COLS), 0) < OWNED

    def add_part(p, so_far):
        tail = parts_ref[p, COLS:, :].astype(I32).astype(F32)
        powers = jnp.exp2(tail[8:] - BITS)
        turned = pltpu.roll(powers, OWNED, 0)
        scale_g = jnp.where(upper, powers, turned)
        scale_w = jnp.where(upper, turned, powers)
        values = parts_ref[p, :COLS, :].astype(I32).astype(F32)
        added = [so_far[i] + values[i * 8 : (i + 1) * 8] * scale_g for i in range(PAIRS)]
        return (*added, so_far[PAIRS] + tail[:8] * scale_w)

    start = tuple(jnp.zeros((8, COLS), F32) for _ in range(PAIRS + 1))
    total = lax.fori_loop(0, PEERS, add_part, start, unroll=4)
    expand = jnp.where(
        iota((COLS, 1), 0) == iota((1, PAIRS * COLS), 1) >> 4, 1.0, 0.0
    )
    spread_w = jnp.dot(
        total[PAIRS], expand, preferred_element_type=F32, precision=lax.Precision.HIGHEST
    )
    grads = total[:PAIRS]
    weights = [spread_w[:, i * COLS : (i + 1) * COLS] for i in range(PAIRS)]
    row = iota((8, COLS), 0)
    even = row < OWNED

    def sides(values):
        swapped = [pltpu.roll(v, OWNED, 0) for v in values]
        both = [v + s for v, s in zip(values, swapped)]
        left, right = ([], [])
        below = jnp.zeros((8, COLS), F32)
        for v, b in zip(values, both):
            left.append(below + jnp.where(even, v, b))
            below = below + b
        above = jnp.zeros((8, COLS), F32)
        for s, b in zip(reversed(swapped), reversed(both)):
            right.append(above + jnp.where(even, s, 0.0))
            above = above + b
        return (left, right[::-1])

    left_g, right_g = sides(grads)
    left_w, right_w = sides(weights)
    place = (row & (OWNED - 1)) * BINS + (row >> 2)
    gains = jnp.zeros((8, COLS), F32)
    for i in range(PAIRS):
        x, y = (left_w[i] + 1.0, right_w[i] + 1.0)
        diff = left_g[i] * y - right_g[i] * x
        terms = diff * diff / (x * y * (x + y))
        sums = jnp.sum(terms, axis=1, keepdims=True)
        gains = gains + jnp.where(iota((8, COLS), 1) == place + 2 * i, sums, 0.0)
    gains = jnp.sum(gains, axis=0, keepdims=True) / (LEAVES * TARGETS)
    out_ref[...] = jnp.broadcast_to(gains[None], out_ref.shape)


def owned_gains(parts):
    shape = (2 * PEERS, 1, OWNED * BINS)
    return pl.pallas_call(
        gain_kernel,
        out_shape=jax.ShapeDtypeStruct(shape, F32),
        in_specs=[pl.BlockSpec(parts.shape, lambda: (0, 0, 0))],
        out_specs=pl.BlockSpec(shape, lambda: (0, 0, 0)),
        compiler_params=params(16),
    )(parts)


def close_kernel(group_ref, gains_ref, table_ref, best_ref):
    table_ref[...] = gains_ref[pl.ds(group_ref[0] * 8, 8)]
    highest = jnp.max(gains_ref[...], axis=0)
    best_ref[...] = jnp.max(highest, axis=1, keepdims=True)


def close(group, gains):
    return pl.pallas_call(
        close_kernel,
        out_shape=[
            jax.ShapeDtypeStruct((8, 1, OWNED * BINS), F32),
            jax.ShapeDtypeStruct((1, 1), F32),
        ],
        in_specs=[
            pl.BlockSpec(memory_space=pltpu.SMEM),
            pl.BlockSpec(gains.shape, lambda: (0, 0, 0)),
        ],
        out_specs=[
            pl.BlockSpec((8, 1, OWNED * BINS), lambda: (0, 0, 0)),
            pl.BlockSpec((1, 1), lambda: (0, 0)),
        ],
        compiler_params=params(4),
    )(group, gains)


def exchange(blocks, axis):
    return lax.all_to_all(blocks, axis, split_axis=0, concat_axis=0, tiled=True)


def shards(bin_codes, leaf_index, gradients, row_weights, split_feature, split_bin):
    core = lax.axis_index("grp_1").astype(I32).reshape(1)
    own, send, column, aux = prep(
        core,
        split_feature,
        bin_codes,
        gradients.T,
        row_weights.reshape(ROW_DEV // 128, 128),
        leaf_index.reshape(1, ROW_DEV),
    )
    other = lax.ppermute(send, "grp_1", [(0, 1), (1, 0)])
    sums = both_sums(other, own_sums(own))
    arrived = exchange(sums, CHIPS)
    aux, column, unused = lax.optimization_barrier((aux, column, sums))
    moved = deliver(*place_rows(core, split_bin, aux, column))
    everyone = exchange(owned_gains(arrived), ROWS_GRP)
    table, best = close(lax.axis_index(ROWS).astype(I32).reshape(1), everyone)
    table, best = (table.reshape(-1), best.reshape(1))
    moved_gradients = moved[:, :COLS].reshape(1, -1)
    moved_weights = moved[:, COLS : COLS + 8].reshape(1, -1)
    return (table, best, moved_gradients, moved_weights)


def solution(mesh):
    torus = Mesh(mesh.devices.reshape(4, 4, 4, 2), ("rows_0", "rows_1", "grp_0", "grp_1"))
    in_specs = (P(ROWS_GRP, None), P(ROWS_GRP, None), P(ROWS_GRP, None), P(ROWS_GRP), P(), P())
    out_specs = (P(ROWS), P(), P(ROWS_GRP, None), P(ROWS_GRP, None))
    return jax.shard_map(
        shards, mesh=torus, in_specs=in_specs, out_specs=out_specs, check_vma=False
    )
```

time: 154 us -> 108 us (0.70)
  waiting for transfers between devices: 64.3 us -> 30.9 us
  Pallas kernels: 51.5 us -> 44.6 us
  local copies, waits for them, and re-layouts: 5.71 us -> 3.35 us
  other arithmetic: 3.06 us -> 0.71 us
    all_to_all x3 -> x2, waiting for transfers between devices: 64.3 us -> 7.83 us  [exchange(): return lax.all_to_all(blocks, axis, split_axis=0, concat_axis=0, tiled=True)]
    ppermute x0 -> x4, waiting for transfers between devices: none -> 23 us  [the longest x3 21.9 us: deliver(): block = lax.ppermute(block, 'grp_0', [(i, (i + s) % 4) for i in range(4)])]
    ppermute x0 -> x4, starting transfers between devices: none -> 3.72 us  [the longest x3 3.41 us: deliver(): block = lax.ppermute(block, 'grp_0', [(i, (i + s) % 4) for i in range(4)])]
    all_to_all x3 -> x2, starting transfers between devices: 24.8 us -> 21.1 us  [exchange(): return lax.all_to_all(blocks, axis, split_axis=0, concat_axis=0, tiled=True)]
    pallas_call x1, Pallas kernels: 15.6 us -> 12.2 us  [own_sums(): pl.pallas_call(own_kernel, grid=(PAIRS // UNROLL,), in_specs=[pl.BlockSpe...]
    pallas_call x1, Pallas kernels: 17.9 us -> 15.2 us  [both_sums(): pl.pallas_call(both_kernel, grid=(PAIRS // UNROLL,), in_specs=[pl.BlockSp...]
    broadcast_in_dim x3 -> x0, local copies, waits for them, and re-layouts: 2.03 us -> none  [the longest x1 1.32 us: shards(): jnp.broadcast_to(gains[None], (128, 1, OWNED * BINS))]
    concatenate x1 -> x0, other arithmetic: 1.71 us -> none  [shards(): jnp.concatenate([gradients.T, row_weights[None, :], leaf_index.reshape(1,...]
  transfers between devices with their start and end apart: 4 -> 7, of which waited for: 3 -> 5; matrix products, arithmetic and copies ran while one was open for 1% -> 2% of each run, Pallas kernels for 16% -> 16%
where the time goes in v2:
time: 108 us
  Pallas kernels  44.6 us (41%)
  waiting for transfers between devices  30.9 us (29%)
  starting transfers between devices  26.4 us (24%)
  local copies, waits for them, and re-layouts  3.35 us (3%)
  between operations  2.06 us (2%)
    ppermute x3, waiting for transfers between devices, deliver(): block = lax.ppermute(block, 'grp_0', [(i, (i + s) % 4) for i in range(4)])  21.9 us
    all_to_all x2, starting transfers between devices, exchange(): return lax.all_to_all(blocks, axis, split_axis=0, concat_axis=0, tiled=True)  21.1 us
    pallas_call x1, Pallas kernels, both_sums(): pl.pallas_call(both_kernel, grid=(PAIRS // UNROLL,), in_specs=[pl.BlockSp...  15.2 us
    pallas_call x1, Pallas kernels, own_sums(): pl.pallas_call(own_kernel, grid=(PAIRS // UNROLL,), in_specs=[pl.BlockSpe...  12.2 us
    pallas_call x1, Pallas kernels, prep(): pl.pallas_call(prep_kernel, grid=(blocks + 1,), in_specs=[smem, smem, pl....  9.58 us
    all_to_all x2, waiting for transfers between devices, exchange(): return lax.all_to_all(blocks, axis, split_axis=0, concat_axis=0, tiled=True)  7.83 us
    pallas_call x1, Pallas kernels, place_rows(): pl.pallas_call(place_kernel, grid=(1,), in_specs=[smem, smem, pl.BlockSpe...  4.8 us
    ppermute x3, starting transfers between devices, deliver(): block = lax.ppermute(block, 'grp_0', [(i, (i + s) % 4) for i in range(4)])  3.41 us
  transfers between devices with their start and end apart: 7, of which 5 were waited for; matrix products, arithmetic and copies ran while one was open for 2% of the time, Pallas kernels for 16%

profile of v2, /device:TPU:1, one launch (start us, length us, event | category | flops | bytes accessed | tf_op | source)
XLA Modules:
  0.0 108.0 jit_solution(866895631996800506)
XLA Ops:
  1.3 9.6 %shard_map.93 = (bf16[4608,256]{1,0:T(8,128)(2,1)}, bf16[4608,256]{1,0:T(8,128)(2,1)}, f32[8,4096]{1,0:T(8,128)}, bf16[512,256]{1,0:T(8,128)(2,1)}) custom-call(s32[1]{0:T(128)} %bitcast.1.core_ref, s32[1]{0:T(128)S(6)} %copy.18.feature_ref, s32[4096,512]{1,0:T(8,128)} %codes_ref.1, bf16[16,4096]{1,0:T(8,128)(2,1)} %bitcast.29, bf16[32,128]{1,0:T(8,128)(2,1)} %bitcast.31, ...), custom_call_target="tpu_custom_call" | custom-call | flops 2147483648 | bytes 12582912 | tf_op jit(solution)/shard_map/pallas_call | solution.py:87
  10.9 1.5 %collective-permute-start = (bf16[4608,256]{1,0:T(8,128)(2,1)}, bf16[4608,256]{1,0:T(8,128)(2,1)S(1)}, u32[]{:S(2)}, u32[]{:S(2)}) collective-permute-start(bf16[4608,256]{1,0:T(8,128)(2,1)} %get-tuple-element.14), channel_id=1, source_target_pairs={{0,1},{1,0},{2,3},{3,2},{4,5},{5,4},{6,7},{7,6},{8,9},{9,8},{10,11... | collective-permute-start | bytes 7077896 | tf_op jit(solution)/shard_map/ppermute | solution.py:441
  12.4 0.0 copy-start
  12.4 1.7 %copy-done = bf16[4608,256]{1,0:T(8,128)(2,1)S(1)} copy-done((bf16[4608,256]{1,0:T(8,128)(2,1)S(1)}, bf16[4608,256]{1,0:T(8,128)(2,1)}, u32[]{:S(2)}) %copy-start) | copy-done | bytes 2359320
  14.0 12.2 %shard_map.94.sums_ref = f32[16,136,512]{2,1,0:T(8,128)S(1)} custom-call(bf16[4608,256]{1,0:T(8,128)(2,1)S(1)} %copy-done), custom_call_target="tpu_custom_call" | custom-call | flops 17179869184 | bytes 8388608 | tf_op jit(solution)/shard_map/pallas_call | solution.py:217
  26.3 0.0 collective-permute-done.rows_ref
  26.3 15.2 %shard_map.95 = s16[64,144,128]{2,1,0:T(8,128)(2,1)} custom-call(bf16[4608,256]{1,0:T(8,128)(2,1)S(1)} %collective-permute-done.rows_ref, f32[16,136,512]{2,1,0:T(8,128)S(1)} %shard_map.94.sums_ref), custom_call_target="tpu_custom_call" | custom-call | flops 17179869184 | bytes 8388608 | tf_op jit(solution)/shard_map/pallas_call | solution.py:233
  41.4 0.0 copy-start.1
  41.4 0.0 copy-start.2
  41.4 11.5 %all-to-all-start = ((s16[64,144,128]{2,1,0:T(8,128)(2,1)}), s16[64,144,128]{2,1,0:T(8,128)(2,1)S(1)}, u32[]{:S(2)}, u32[]{:S(2)}) async-start(s16[64,144,128]{2,1,0:T(8,128)(2,1)} %shard_map.95), calls=%async_computation | async-start | bytes 4718592 | tf_op jit(solution)/shard_map/all_to_all | solution.py:428
  53.6 0.0 copy-done.1
  53.6 0.0 copy-done.2
  53.6 4.8 %shard_map.98 = (bf16[4,144,128]{2,1,0:T(8,128)(2,1)S(1)}, bf16[4,144,128]{2,1,0:T(8,128)(2,1)S(1)}) custom-call(s32[1]{0:T(128)} %bitcast.1.core_ref, s32[1]{0:T(128)S(6)} %copy.19.bin_ref, bf16[512,256]{1,0:T(8,128)(2,1)S(1)} %copy-done.1, f32[8,4096]{1,0:T(8,128)S(1)} %copy-done.2), custom_call_target="tpu_custom_call" | custom-call | flops 2147483648 | bytes 1048576 | tf_op jit(solution)/shard_map/pallas_call | solution.py:302
  58.4 0.3 collective-permute-start.1
  58.8 1.1 %collective-permute-done.1 = bf16[4,144,128]{2,1,0:T(8,128)(2,1)S(1)} collective-permute-done((bf16[4,144,128]{2,1,0:T(8,128)(2,1)S(1)}, bf16[4,144,128]{2,1,0:T(8,128)(2,1)S(1)}, u32[]{:S(2)}, u32[]{:S(2)}) %collective-permute-start.1) | collective-permute-done | bytes 147488 | tf_op jit(solution)/shard_map/ppermute | solution.py:322
  59.9 0.7 fusion.1
  60.5 2.3 %collective-permute-start.2 = (bf16[2,144,128]{2,1,0:T(8,128)(2,1)}, bf16[2,144,128]{2,1,0:T(8,128)(2,1)S(1)}, u32[]{:S(2)}, u32[]{:S(2)}) collective-permute-start(bf16[2,144,128]{2,1,0:T(8,128)(2,1)} %get-tuple-element.26), channel_id=1, source_target_pairs={{0,6},{2,0},{4,2},{6,4},{1,7},{3,1},{5,3},{7,5},{8,14},{10,8},{12,... | collective-permute-start | bytes 221192 | tf_op jit(solution)/shard_map/ppermute | solution.py:330
  62.8 0.6 collective-permute-start.3
  63.4 0.6 collective-permute-start.4
  63.9 16.2 %collective-permute-done.2 = bf16[2,144,128]{2,1,0:T(8,128)(2,1)S(1)} collective-permute-done((bf16[2,144,128]{2,1,0:T(8,128)(2,1)}, bf16[2,144,128]{2,1,0:T(8,128)(2,1)S(1)}, u32[]{:S(2)}, u32[]{:S(2)}) %collective-permute-start.2) | collective-permute-done | bytes 73760 | tf_op jit(solution)/shard_map/ppermute | solution.py:330
  80.2 3.7 %collective-permute-done.3 = bf16[2,144,128]{2,1,0:T(8,128)(2,1)S(1)} collective-permute-done((bf16[2,144,128]{2,1,0:T(8,128)(2,1)S(1)}, bf16[2,144,128]{2,1,0:T(8,128)(2,1)S(1)}, u32[]{:S(2)}, u32[]{:S(2)}) %collective-permute-start.3) | collective-permute-done | bytes 73760 | tf_op jit(solution)/shard_map/ppermute | solution.py:330
  83.8 2.1 %collective-permute-done.4 = bf16[2,144,128]{2,1,0:T(8,128)(2,1)S(1)} collective-permute-done((bf16[2,144,128]{2,1,0:T(8,128)(2,1)S(1)}, bf16[2,144,128]{2,1,0:T(8,128)(2,1)S(1)}, u32[]{:S(2)}, u32[]{:S(2)}) %collective-permute-start.4) | collective-permute-done | bytes 73760 | tf_op jit(solution)/shard_map/ppermute | solution.py:330
  86.0 0.0 all-to-all-done.parts_ref
  86.0 2.2 %shard_map.96 = f32[128,1,128]{2,1,0:T(1,128)} custom-call(s16[64,144,128]{2,1,0:T(8,128)(2,1)S(1)} %all-to-all-done.parts_ref), custom_call_target="tpu_custom_call" | custom-call | tf_op jit(solution)/shard_map/pallas_call | solution.py:393
  88.3 9.6 %all-to-all-start.1 = ((f32[128,1,128]{2,1,0:T(1,128)}), f32[128,1,128]{2,1,0:T(1,128)S(1)}, u32[]{:S(2)}, u32[]{:S(2)}) async-start(f32[128,1,128]{2,1,0:T(1,128)} %shard_map.96), calls=%async_computation.1 | async-start | bytes 131072 | tf_op jit(solution)/shard_map/all_to_all | solution.py:428
  98.0 0.9 reshape.42
  98.9 0.6 reshape.43
  99.5 7.8 %all-to-all-done.1.gains_ref = f32[128,1,128]{2,1,0:T(1,128)S(1)} async-done(((f32[128,1,128]{2,1,0:T(1,128)}), f32[128,1,128]{2,1,0:T(1,128)S(1)}, u32[]{:S(2)}, u32[]{:S(2)}) %all-to-all-start.1) | async-done | bytes 65568 | tf_op jit(solution)/shard_map/all_to_all | solution.py:428
  107.3 0.6 shard_map.97
  (12 shorter events, 0.2 us)
Async XLA Ops:
  10.9 15.4 %collective-permute-start = (bf16[4608,256]{1,0:T(8,128)(2,1)}, bf16[4608,256]{1,0:T(8,128)(2,1)S(1)}, u32[]{:S(2)}, u32[]{:S(2)}) collective-permute-start(bf16[4608,256]{1,0:T(8,128)(2,1)} %get-tuple-element.14), channel_id=1, source_target_pairs={{0,1},{1,0},{2,3},{3,2},{4,5},{5,4},{6,7},{7,6},{8,9},{9,8},{10,11... | collective-permute-start | bytes 7077896 | tf_op jit(solution)/shard_map/ppermute | solution.py:441
  12.4 1.7 %copy-start = (bf16[4608,256]{1,0:T(8,128)(2,1)S(1)}, bf16[4608,256]{1,0:T(8,128)(2,1)}, u32[]{:S(2)}) copy-start(bf16[4608,256]{1,0:T(8,128)(2,1)} %get-tuple-element.15.rows_ref) | copy-start | bytes 7077892
  41.4 12.2 %copy-start.1 = (bf16[512,256]{1,0:T(8,128)(2,1)S(1)}, bf16[512,256]{1,0:T(8,128)(2,1)}, u32[]{:S(2)}) copy-start(bf16[512,256]{1,0:T(8,128)(2,1)} %get-tuple-element.20.aux_ref) | copy-start | bytes 786436
  41.4 12.2 %copy-start.2 = (f32[8,4096]{1,0:T(8,128)S(1)}, f32[8,4096]{1,0:T(8,128)}, u32[]{:S(2)}) copy-start(f32[8,4096]{1,0:T(8,128)} %get-tuple-element.21.column_ref) | copy-start | bytes 393220
  41.4 44.6 %all-to-all-start = ((s16[64,144,128]{2,1,0:T(8,128)(2,1)}), s16[64,144,128]{2,1,0:T(8,128)(2,1)S(1)}, u32[]{:S(2)}, u32[]{:S(2)}) async-start(s16[64,144,128]{2,1,0:T(8,128)(2,1)} %shard_map.95), calls=%async_computation | async-start | bytes 4718592 | tf_op jit(solution)/shard_map/all_to_all | solution.py:428
  58.4 1.4 %collective-permute-start.1 = (bf16[4,144,128]{2,1,0:T(8,128)(2,1)S(1)}, bf16[4,144,128]{2,1,0:T(8,128)(2,1)S(1)}, u32[]{:S(2)}, u32[]{:S(2)}) collective-permute-start(bf16[4,144,128]{2,1,0:T(8,128)(2,1)S(1)} %get-tuple-element.23), channel_id=1, source_target_pairs={{0,1},{1,0},{2,3},{3,2},{4,5},{5,4},{6,7},{7,6},{8,9},{9,8},{10,11... | collective-permute-start | bytes 442376 | tf_op jit(solution)/shard_map/ppermute | solution.py:322
  60.5 19.6 %collective-permute-start.2 = (bf16[2,144,128]{2,1,0:T(8,128)(2,1)}, bf16[2,144,128]{2,1,0:T(8,128)(2,1)S(1)}, u32[]{:S(2)}, u32[]{:S(2)}) collective-permute-start(bf16[2,144,128]{2,1,0:T(8,128)(2,1)} %get-tuple-element.26), channel_id=1, source_target_pairs={{0,6},{2,0},{4,2},{6,4},{1,7},{3,1},{5,3},{7,5},{8,14},{10,8},{12,... | collective-permute-start | bytes 221192 | tf_op jit(solution)/shard_map/ppermute | solution.py:330
  62.8 21.0 %collective-permute-start.3 = (bf16[2,144,128]{2,1,0:T(8,128)(2,1)S(1)}, bf16[2,144,128]{2,1,0:T(8,128)(2,1)S(1)}, u32[]{:S(2)}, u32[]{:S(2)}) collective-permute-start(bf16[2,144,128]{2,1,0:T(8,128)(2,1)S(1)} %get-tuple-element.27), channel_id=1, source_target_pairs={{0,4},{2,6},{4,0},{6,2},{1,5},{3,7},{5,1},{7,3},{8,12},{10,14},{12... | collective-permute-start | bytes 221192 | tf_op jit(solution)/shard_map/ppermute | solution.py:330
  63.4 22.6 %collective-permute-start.4 = (bf16[2,144,128]{2,1,0:T(8,128)(2,1)S(1)}, bf16[2,144,128]{2,1,0:T(8,128)(2,1)S(1)}, u32[]{:S(2)}, u32[]{:S(2)}) collective-permute-start(bf16[2,144,128]{2,1,0:T(8,128)(2,1)S(1)} %get-tuple-element.24), channel_id=1, source_target_pairs={{0,2},{2,4},{4,6},{6,0},{1,3},{3,5},{5,7},{7,1},{8,10},{10,12},{12... | collective-permute-start | bytes 221192 | tf_op jit(solution)/shard_map/ppermute | solution.py:330
  88.3 19.1 %all-to-all-start.1 = ((f32[128,1,128]{2,1,0:T(1,128)}), f32[128,1,128]{2,1,0:T(1,128)S(1)}, u32[]{:S(2)}, u32[]{:S(2)}) async-start(f32[128,1,128]{2,1,0:T(1,128)} %shard_map.96), calls=%async_computation.1 | async-start | bytes 131072 | tf_op jit(solution)/shard_map/all_to_all | solution.py:428

commit v3 on v2

--- a/solution.py
+++ b/solution.py
@@ -36,93 +36,107 @@
     return lax.broadcasted_iota(I32, shape, dim)
 
 
+def in_hbm(array):
+    return pltpu.with_memory_space_constraint(array, pltpu.HBM)
+
+
 def params(mib):
     return pltpu.CompilerParams(vmem_limit_bytes=mib << 20)
 
 
 def prep_kernel(
-    core_ref, feature_ref, codes_ref, grads_ref, weights_ref, leaf_ref, own_ref, send_ref, column_ref, aux_ref, select_ref
+    core_ref, codes_hbm, grads_hbm, weights_hbm, leaf_hbm, dup_hbm, send_hbm, data_hbm, aux_hbm,
+    codes_ref, grads_ref, weights_ref, leaf_ref, dup_ref, send_ref, data_ref, aux_ref, in_sems, out_sems,
 ):
-    step = pl.program_id(0)
     blocks = ROW_DEV // ROW_BLOCK
-
-    @pl.when(step == 0)
-    def _():
-        core = core_ref[0]
-        lane = iota((1, FEATURES), 1)
-        side = jnp.where(lane < HALF, core, 1 - core)
-        place = lane & (HALF - 1)
-        wanted = ((place >> 2) << 3) + (side << 2) + (place & 3)
-        select_ref[...] = jnp.where(iota((FEATURES, FEATURES), 0) == wanted, 1.0, 0.0).astype(BF16)
-
-    @pl.when(step < blocks)
-    def _():
-        codes = codes_ref[...].astype(F32).astype(BF16)
-        both = jnp.dot(codes, select_ref[...], preferred_element_type=F32).astype(BF16)
-        own_ref[...] = both[:, :HALF]
-        send_ref[...] = both[:, HALF:]
-        hot = jnp.where(iota((8, FEATURES), 1) == feature_ref[0], 1.0, 0.0).astype(BF16)
-        column_ref[...] = lax.dot_general(
-            hot, codes, (((1,), (1,)), ((), ())), preferred_element_type=F32
-        )
-
-    @pl.when(step == blocks)
-    def _():
-        weights = weights_ref[...].astype(F32)
-        leaf = leaf_ref[...].astype(F32)
-        row = iota((TARGETS, AUX_CHUNK), 0)
-        for i in range(ROW_DEV // AUX_CHUNK):
-            lanes = slice(i * AUX_CHUNK, (i + 1) * AUX_CHUNK)
-            weight = jnp.concatenate([weights[2 * i : 2 * i + 1], weights[2 * i + 1 : 2 * i + 2]], axis=1)
-            rest = jnp.where(row == 0, weight, jnp.where(row == 1, leaf[:, lanes], 0.0)).astype(BF16)
-            for ref in (own_ref, send_ref, aux_ref):
-                ref[i * AUX : i * AUX + TARGETS, :] = grads_ref[:, lanes]
-                ref[i * AUX + TARGETS : (i + 1) * AUX, :] = rest
-
-
-def prep(core, split_feature, codes, grads, weights, leaf):
+    cuts = [slice(i * ROW_BLOCK, (i + 1) * ROW_BLOCK) for i in range(blocks)]
+    pairs = [(grads_hbm, grads_ref), (weights_hbm, weights_ref), (leaf_hbm, leaf_ref)]
+    pairs += [(codes_hbm.at[rows, :], codes_ref.at[rows, :]) for rows in cuts]
+    arriving = [pltpu.make_async_copy(a, b, in_sems.at[i]) for i, (a, b) in enumerate(pairs)]
+    for copy in arriving:
+        copy.start()
+    leaving = []
+
+    def leave(source, target):
+        copy = pltpu.make_async_copy(source, target, out_sems.at[len(leaving)])
+        copy.start()
+        leaving.append(copy)
+
+    core = core_ref[0]
+    lane = iota((1, LANES + HALF), 1)
+    twice = ((lane >> 3) << 3) + (core << 2) + (lane & 3)
+    place = lane - LANES
+    once = ((place >> 2) << 3) + ((1 - core) << 2) + (place & 3)
+    wanted = jnp.where(lane < LANES, twice, once)
+    select = jnp.where(iota((FEATURES, LANES + HALF), 0) == wanted, 1.0, 0.0).astype(BF16)
+
+    for copy in arriving[:3]:
+        copy.wait()
+    weights = weights_ref[...].astype(F32)
+    row = iota((TARGETS, ROW_DEV), 0)
+    weight = jnp.concatenate([weights[i : i + 1] for i in range(weights.shape[0])], axis=1)
+    leaf = leaf_ref[...].astype(F32)
+    rest = jnp.where(row == 0, weight, jnp.where(row == 1, leaf, 0.0)).astype(BF16)
+    aux_ref[:TARGETS, :] = grads_ref[...]
+    aux_ref[TARGETS:, :] = rest
+    leave(aux_ref, aux_hbm)
+    for i in range(ROW_DEV // AUX_CHUNK):
+        lanes = slice(i * AUX_CHUNK, (i + 1) * AUX_CHUNK)
+        at = ROW_DEV + i * AUX
+        send_ref[at : at + TARGETS, :] = grads_ref[:, lanes]
+        send_ref[at + TARGETS : at + AUX, :] = rest[:, lanes]
+    leave(send_ref.at[ROW_DEV:, :], send_hbm.at[ROW_DEV:, :])
+    spread_values(grads_ref[...].astype(F32), weight, leaf, data_ref)
+    leave(data_ref, data_hbm)
+
+    for rows, copy in zip(cuts, arriving[3:]):
+        copy.wait()
+        codes = codes_ref[rows, :].astype(F32).astype(BF16)
+        both = jnp.dot(codes, select, preferred_element_type=F32).astype(BF16)
+        dup_ref[rows, :] = both[:, :LANES]
+        send_ref[rows, :] = both[:, LANES:]
+        leave(dup_ref.at[rows, :], dup_hbm.at[rows, :])
+        leave(send_ref.at[rows, :], send_hbm.at[rows, :])
+    for copy in leaving:
+        copy.wait()
+
+
+def spread_values(grads, weights, leaf, data_ref):
+    for l in range(LEAVES):
+        data_ref[l * TARGETS : (l + 1) * TARGETS, :] = jnp.where(leaf == l, grads, 0.0).astype(BF16)
+    ids = iota((TARGETS, ROW_DEV), 0).astype(F32)
+    data_ref[COLS : COLS + TARGETS, :] = jnp.where(leaf == ids, weights, 0.0).astype(BF16)
+
+
+def prep(core, codes, grads, weights, leaf):
     blocks = ROW_DEV // ROW_BLOCK
-    smem = pl.BlockSpec(memory_space=pltpu.SMEM)
-    buffer = jax.ShapeDtypeStruct((ROW_DEV + AUX_ROWS, HALF), BF16)
+    there = pl.BlockSpec(memory_space=pl.ANY)
+    outs = [
+        (ROW_DEV, LANES),
+        (ROW_DEV + AUX_ROWS, HALF),
+        (COLS + TARGETS, ROW_DEV),
+        (AUX, ROW_DEV),
+    ]
+    ins = [codes, grads, weights, leaf]
     return pl.pallas_call(
         prep_kernel,
-        grid=(blocks + 1,),
-        in_specs=[
-            smem,
-            smem,
-            pl.BlockSpec((ROW_BLOCK, FEATURES), lambda i: (jnp.minimum(i, blocks - 1), 0)),
-            pl.BlockSpec(grads.shape, lambda i: (0, 0)),
-            pl.BlockSpec(weights.shape, lambda i: (0, 0)),
-            pl.BlockSpec(leaf.shape, lambda i: (0, 0)),
-        ],
-        out_specs=[
-            pl.BlockSpec((ROW_BLOCK, HALF), lambda i: (i, 0)),
-            pl.BlockSpec((ROW_BLOCK, HALF), lambda i: (i, 0)),
-            pl.BlockSpec((8, ROW_BLOCK), lambda i: (0, jnp.minimum(i, blocks - 1))),
-            pl.BlockSpec((AUX_ROWS, HALF), lambda i: (0, 0)),
-        ],
-        out_shape=[
-            buffer,
-            buffer,
-            jax.ShapeDtypeStruct((8, ROW_DEV), F32),
-            jax.ShapeDtypeStruct((AUX_ROWS, HALF), BF16),
-        ],
-        scratch_shapes=[pltpu.VMEM((FEATURES, FEATURES), BF16)],
-        compiler_params=params(56),
+        in_specs=[pl.BlockSpec(memory_space=pltpu.SMEM)] + [there] * len(ins),
+        out_specs=[there] * len(outs),
+        out_shape=[pltpu.HBM(shape, BF16) for shape in outs],
+        scratch_shapes=[pltpu.VMEM(a.shape, a.dtype) for a in ins]
+        + [pltpu.VMEM(shape, BF16) for shape in outs]
+        + [pltpu.SemaphoreType.DMA((blocks + 3,)), pltpu.SemaphoreType.DMA((2 * blocks + 3,))],
+        compiler_params=params(48),
         cost_estimate=pl.CostEstimate(
             flops=2 * ROW_DEV * FEATURES * FEATURES,
-            bytes_accessed=ROW_DEV * FEATURES * 6,
+            bytes_accessed=ROW_DEV * FEATURES * 8,
             transcendentals=0,
         ),
-    )(core, split_feature, codes, grads, weights, leaf)
-
-
-def unpack_aux(rows_ref, at):
-    parts = [
-        rows_ref[at + i * AUX : at + (i + 1) * AUX, :]
-        for i in range(ROW_DEV // AUX_CHUNK)
-    ]
-    return jnp.concatenate(parts, axis=1).astype(F32)
+    )(core, *[in_hbm(a) for a in ins])
+
+
+def split_aux(aux):
+    return (aux[:TARGETS], aux[TARGETS : TARGETS + 1], aux[TARGETS + 1 : TARGETS + 2])
 
 
 def spread(rows_ref, dup_ref, data_ref):
@@ -134,12 +148,12 @@
         dup_ref[rows, :] = jnp.dot(
             rows_ref[rows, :], twice, preferred_element_type=F32
         ).astype(BF16)
-    aux = unpack_aux(rows_ref, ROW_DEV)
-    grads, weights, leaf = (aux[:TARGETS], aux[TARGETS : TARGETS + 1], aux[TARGETS + 1 : TARGETS + 2])
-    for l in range(LEAVES):
-        data_ref[l * TARGETS : (l + 1) * TARGETS, :] = jnp.where(leaf == l, grads, 0.0).astype(BF16)
-    ids = iota((TARGETS, ROW_DEV), 0).astype(F32)
-    data_ref[COLS : COLS + TARGETS, :] = jnp.where(leaf == ids, weights, 0.0).astype(BF16)
+    parts = [
+        rows_ref[ROW_DEV + i * AUX : ROW_DEV + (i + 1) * AUX, :]
+        for i in range(ROW_DEV // AUX_CHUNK)
+    ]
+    aux = jnp.concatenate(parts, axis=1).astype(F32)
+    spread_values(*split_aux(aux), data_ref)
 
 
 def pair_sums(pair, dup_ref, data_ref):
@@ -154,13 +168,8 @@
 MESSAGE = COLS + 16
 
 
-def own_kernel(rows_ref, sums_ref, dup_ref, data_ref):
+def own_kernel(dup_ref, data_ref, sums_ref):
     step = pl.program_id(0)
-
-    @pl.when(step == 0)
-    def _():
-        spread(rows_ref, dup_ref, data_ref)
-
     for i in range(UNROLL):
         sums_ref[i] = pair_sums(step * UNROLL + i, dup_ref, data_ref)
 
@@ -213,20 +222,20 @@
 )
 
 
-def own_sums(rows):
+def own_sums(dup, data):
+    still = pl.Buffered(1)
     return pl.pallas_call(
         own_kernel,
         grid=(PAIRS // UNROLL,),
-        in_specs=[pl.BlockSpec(rows.shape, lambda i: (0, 0))],
+        in_specs=[
+            pl.BlockSpec(dup.shape, lambda i: (0, 0), pipeline_mode=still),
+            pl.BlockSpec(data.shape, lambda i: (0, 0), pipeline_mode=still),
+        ],
         out_specs=pl.BlockSpec((UNROLL, SENT, LANES), lambda i: (i, 0, 0)),
         out_shape=jax.ShapeDtypeStruct((PAIRS, SENT, LANES), F32),
-        scratch_shapes=[
-            pltpu.VMEM((ROW_DEV, LANES), BF16),
-            pltpu.VMEM((COLS + TARGETS, ROW_DEV), BF16),
-        ],
         compiler_params=params(36),
         cost_estimate=HIST_COST,
-    )(rows)
+    )(in_hbm(dup), in_hbm(data))
 
 
 def both_sums(rows, sums):
@@ -251,11 +260,17 @@
     )(rows, sums)
 
 
-def place_kernel(core_ref, bin_ref, aux_ref, column_ref, keep_ref, give_ref):
+def place_kernel(feature_ref, core_ref, bin_ref, aux_ref, codes_ref, keep_ref, give_ref):
     core = core_ref[0]
-    aux = unpack_aux(aux_ref, 0)
-    grads, weights, leaf = (aux[:TARGETS], aux[TARGETS : TARGETS + 1], aux[TARGETS + 1 : TARGETS + 2])
-    child = jnp.where(column_ref[0:1, :] > bin_ref[0].astype(F32), 1.0, 0.0)
+    grads, weights, leaf = split_aux(aux_ref[...].astype(F32))
+    chosen = jnp.where(iota((8, 128), 1) == (feature_ref[0] & 127), 1.0, 0.0).astype(BF16)
+    column = lax.dot_general(
+        chosen,
+        codes_ref[...].astype(F32).astype(BF16),
+        (((1,), (1,)), ((), ())),
+        preferred_element_type=F32,
+    )[0:1]
+    child = jnp.where(column > bin_ref[0].astype(F32), 1.0, 0.0)
     key = leaf * 2 + child
     keys = 2 * LEAVES
     hot = jnp.where(iota((keys, ROW_DEV), 0).astype(F32) == key, 1.0, 0.0)
@@ -295,26 +310,29 @@
         out_ref[l % 4, COLS:, :] = moved.astype(BF16)
 
 
-def place_rows(core, split_bin, aux, column):
+def place_rows(split_feature, core, split_bin, aux, codes):
     smem = pl.BlockSpec(memory_space=pltpu.SMEM)
     block = jax.ShapeDtypeStruct((LEAVES // 2, COLS + 16, 128), BF16)
-    spec = pl.BlockSpec(block.shape, lambda i: (0, 0, 0))
+    spec = pl.BlockSpec(block.shape, lambda i, feature: (0, 0, 0))
     return pl.pallas_call(
         place_kernel,
-        grid=(1,),
-        in_specs=[
-            smem,
-            smem,
-            pl.BlockSpec(aux.shape, lambda i: (0, 0)),
-            pl.BlockSpec(column.shape, lambda i: (0, 0)),
-        ],
-        out_specs=[spec, spec],
+        grid_spec=pltpu.PrefetchScalarGridSpec(
+            num_scalar_prefetch=1,
+            grid=(1,),
+            in_specs=[
+                smem,
+                smem,
+                pl.BlockSpec(aux.shape, lambda i, feature: (0, 0)),
+                pl.BlockSpec((ROW_DEV, 128), lambda i, feature: (0, feature[0] >> 7)),
+            ],
+            out_specs=[spec, spec],
+        ),
         out_shape=[block, block],
-        compiler_params=params(24),
+        compiler_params=params(56),
         cost_estimate=pl.CostEstimate(
             flops=2 * LEAVES * CAP * ROW_DEV * 32, bytes_accessed=1 << 20, transcendentals=0
         ),
-    )(core, split_bin, aux, column)
+    )(split_feature, core, split_bin, aux, codes)
 
 
 def deliver(keep, give):
@@ -430,19 +448,18 @@
 
 def shards(bin_codes, leaf_index, gradients, row_weights, split_feature, split_bin):
     core = lax.axis_index("grp_1").astype(I32).reshape(1)
-    own, send, column, aux = prep(
+    dup, send, data, aux = prep(
         core,
-        split_feature,
         bin_codes,
         gradients.T,
         row_weights.reshape(ROW_DEV // 128, 128),
         leaf_index.reshape(1, ROW_DEV),
     )
     other = lax.ppermute(send, "grp_1", [(0, 1), (1, 0)])
-    sums = both_sums(other, own_sums(own))
+    sums = both_sums(other, own_sums(dup, data))
     arrived = exchange(sums, CHIPS)
-    aux, column, unused = lax.optimization_barrier((aux, column, sums))
-    moved = deliver(*place_rows(core, split_bin, aux, column))
+    aux, unused = lax.optimization_barrier((aux, sums))
+    moved = deliver(*place_rows(split_feature, core, split_bin, aux, bin_codes))
     everyone = exchange(owned_gains(arrived), ROWS_GRP)
     table, best = close(lax.axis_index(ROWS).astype(I32).reshape(1), everyone)
     table, best = (table.reshape(-1), best.reshape(1))

time: 108 us -> 105 us (0.972)
  waiting for transfers between devices: 30.9 us -> 27.2 us
  Pallas kernels: 44.6 us -> 46.5 us
  local copies, waits for them, and re-layouts: 3.35 us -> 1.68 us
    ppermute x3, waiting for transfers between devices: 21.9 us -> 18.1 us  [deliver(): block = lax.ppermute(block, 'grp_0', [(i, (i + s) % 4) for i in range(4)])]
    unnamed x11 -> x5, local copies, waits for them, and re-layouts: 1.74 us -> 0.07 us
    pallas_call x2, Pallas kernels: 14.4 us -> 15.5 us  [the longest x1 8.02 us: prep(): pl.pallas_call(prep_kernel, in_specs=[pl.BlockSpec(memory_space=pltpu.SME...]
  transfers between devices with their start and end apart: 7 -> 7, of which waited for: 5 -> 5; matrix products, arithmetic and copies ran while one was open for 2% -> 3% of each run, Pallas kernels for 16% -> 20%
where the time goes in v3:
time: 105 us
  Pallas kernels  46.5 us (44%)
  waiting for transfers between devices  27.2 us (26%)
  starting transfers between devices  26.5 us (25%)
  between operations  2.05 us (2%)
  local copies, waits for them, and re-layouts  1.68 us (2%)
    all_to_all x2, starting transfers between devices, exchange(): return lax.all_to_all(blocks, axis, split_axis=0, concat_axis=0, tiled=True)  21 us
    ppermute x3, waiting for transfers between devices, deliver(): block = lax.ppermute(block, 'grp_0', [(i, (i + s) % 4) for i in range(4)])  18.1 us
    pallas_call x1, Pallas kernels, both_sums(): pl.pallas_call(both_kernel, grid=(PAIRS // UNROLL,), in_specs=[pl.BlockSp...  15.1 us
    pallas_call x1, Pallas kernels, own_sums(): pl.pallas_call(own_kernel, grid=(PAIRS // UNROLL,), in_specs=[pl.BlockSpe...  13 us
    pallas_call x1, Pallas kernels, prep(): pl.pallas_call(prep_kernel, in_specs=[pl.BlockSpec(memory_space=pltpu.SME...  8.02 us
    all_to_all x2, waiting for transfers between devices, exchange(): return lax.all_to_all(blocks, axis, split_axis=0, concat_axis=0, tiled=True)  7.86 us
    pallas_call x1, Pallas kernels, place_rows(): pl.pallas_call(place_kernel, grid_spec=pltpu.PrefetchScalarGridSpec(num_s...  7.44 us
    ppermute x3, starting transfers between devices, deliver(): block = lax.ppermute(block, 'grp_0', [(i, (i + s) % 4) for i in range(4)])  3.46 us
  transfers between devices with their start and end apart: 7, of which 5 were waited for; matrix products, arithmetic and copies ran while one was open for 3% of the time, Pallas kernels for 20%

profile of v3, /device:TPU:1, one launch (start us, length us, event | category | flops | bytes accessed | tf_op | source)
XLA Modules:
  0.0 104.9 jit_solution(1097086688161547301)
XLA Ops:
  0.6 8.0 %shard_map.93 = (bf16[4096,512]{1,0:T(8,128)(2,1)}, bf16[4608,256]{1,0:T(8,128)(2,1)}, bf16[144,4096]{1,0:T(8,128)(2,1)}, bf16[32,4096]{1,0:T(8,128)(2,1)}) custom-call(s32[1]{0:T(128)} %bitcast.1.core_ref, s32[4096,512]{1,0:T(8,128)} %codes_ref.1, bf16[16,4096]{1,0:T(8,128)(2,1)} %bitcast.29, bf16[32,128]{1,0:T(8,128)(2,1)} %bitcast.31, s32[1,4096]{1,0:T(1,128)} %bitcast.30), custom_call_target="tpu_custom_call" | custom-call | flops 2147483648 | bytes 16777216 | tf_op jit(solution)/shard_map/pallas_call | solution.py:121
  8.7 1.7 %collective-permute-start = (bf16[4608,256]{1,0:T(8,128)(2,1)}, bf16[4608,256]{1,0:T(8,128)(2,1)S(1)}, u32[]{:S(2)}, u32[]{:S(2)}) collective-permute-start(bf16[4608,256]{1,0:T(8,128)(2,1)} %get-tuple-element.13), channel_id=1, source_target_pairs={{0,1},{1,0},{2,3},{3,2},{4,5},{5,4},{6,7},{7,6},{8,9},{9,8},{10,11... | collective-permute-start | bytes 7077896 | tf_op jit(solution)/shard_map/ppermute | solution.py:458
  10.3 13.0 %shard_map.94.sums_ref = f32[16,136,512]{2,1,0:T(8,128)S(1)} custom-call(bf16[4096,512]{1,0:T(8,128)(2,1)} %get-tuple-element.14.dup_ref, bf16[144,4096]{1,0:T(8,128)(2,1)} %get-tuple-element.15.data_ref), custom_call_target="tpu_custom_call" | custom-call | flops 17179869184 | bytes 8388608 | tf_op jit(solution)/shard_map/pallas_call | solution.py:227
  23.4 0.0 collective-permute-done.rows_ref
  23.4 15.1 %shard_map.95 = s16[64,144,128]{2,1,0:T(8,128)(2,1)} custom-call(bf16[4608,256]{1,0:T(8,128)(2,1)S(1)} %collective-permute-done.rows_ref, f32[16,136,512]{2,1,0:T(8,128)S(1)} %shard_map.94.sums_ref), custom_call_target="tpu_custom_call" | custom-call | flops 17179869184 | bytes 8388608 | tf_op jit(solution)/shard_map/pallas_call | solution.py:242
  38.5 11.4 %all-to-all-start = ((s16[64,144,128]{2,1,0:T(8,128)(2,1)}), s16[64,144,128]{2,1,0:T(8,128)(2,1)S(1)}, u32[]{:S(2)}, u32[]{:S(2)}) async-start(s16[64,144,128]{2,1,0:T(8,128)(2,1)} %shard_map.95), calls=%async_computation | async-start | bytes 4718592 | tf_op jit(solution)/shard_map/all_to_all | solution.py:446
  51.3 7.4 %shard_map.98 = (bf16[4,144,128]{2,1,0:T(8,128)(2,1)}, bf16[4,144,128]{2,1,0:T(8,128)(2,1)}) custom-call(s32[1]{0:T(128)S(6)} %copy.18.feature_ref, s32[1]{0:T(128)} %bitcast.1.core_ref, s32[1]{0:T(128)S(6)} %copy.19.bin_ref, bf16[32,4096]{1,0:T(8,128)(2,1)} %get-tuple-element.19.aux_ref, s32[4096,512]{1,0:T(8,128)} %codes_ref.1), custom_call_target="tpu_custom_call" | custom-call | flops 2147483648 | bytes 1048576 | tf_op jit(solution)/shard_map/pallas_call | solution.py:317
  58.7 0.3 collective-permute-start.1
  59.0 1.3 %collective-permute-done.1 = bf16[4,144,128]{2,1,0:T(8,128)(2,1)S(1)} collective-permute-done((bf16[4,144,128]{2,1,0:T(8,128)(2,1)}, bf16[4,144,128]{2,1,0:T(8,128)(2,1)S(1)}, u32[]{:S(2)}, u32[]{:S(2)}) %collective-permute-start.1) | collective-permute-done | bytes 147488 | tf_op jit(solution)/shard_map/ppermute | solution.py:340
  60.3 0.9 select_bitcast_fusion.1
  61.3 2.3 %collective-permute-start.2 = (bf16[2,144,128]{2,1,0:T(8,128)(2,1)S(1)}, bf16[2,144,128]{2,1,0:T(8,128)(2,1)S(1)}, u32[]{:S(2)}, u32[]{:S(2)}) collective-permute-start(bf16[2,144,128]{2,1,0:T(8,128)(2,1)S(1)} %get-tuple-element.24), channel_id=1, source_target_pairs={{0,6},{2,0},{4,2},{6,4},{1,7},{3,1},{5,3},{7,5},{8,14},{10,8},{12,... | collective-permute-start | bytes 221192 | tf_op jit(solution)/shard_map/ppermute | solution.py:348
  63.6 0.6 collective-permute-start.3
  64.1 0.6 collective-permute-start.4
  64.7 12.2 %collective-permute-done.2 = bf16[2,144,128]{2,1,0:T(8,128)(2,1)S(1)} collective-permute-done((bf16[2,144,128]{2,1,0:T(8,128)(2,1)S(1)}, bf16[2,144,128]{2,1,0:T(8,128)(2,1)S(1)}, u32[]{:S(2)}, u32[]{:S(2)}) %collective-permute-start.2) | collective-permute-done | bytes 73760 | tf_op jit(solution)/shard_map/ppermute | solution.py:348
  77.0 3.7 %collective-permute-done.3 = bf16[2,144,128]{2,1,0:T(8,128)(2,1)S(1)} collective-permute-done((bf16[2,144,128]{2,1,0:T(8,128)(2,1)S(1)}, bf16[2,144,128]{2,1,0:T(8,128)(2,1)S(1)}, u32[]{:S(2)}, u32[]{:S(2)}) %collective-permute-start.3) | collective-permute-done | bytes 73760 | tf_op jit(solution)/shard_map/ppermute | solution.py:348
  80.7 2.1 %collective-permute-done.4 = bf16[2,144,128]{2,1,0:T(8,128)(2,1)S(1)} collective-permute-done((bf16[2,144,128]{2,1,0:T(8,128)(2,1)S(1)}, bf16[2,144,128]{2,1,0:T(8,128)(2,1)S(1)}, u32[]{:S(2)}, u32[]{:S(2)}) %collective-permute-start.4) | collective-permute-done | bytes 73760 | tf_op jit(solution)/shard_map/ppermute | solution.py:348
  83.0 0.0 all-to-all-done.parts_ref
  83.0 2.2 %shard_map.96 = f32[128,1,128]{2,1,0:T(1,128)} custom-call(s16[64,144,128]{2,1,0:T(8,128)(2,1)S(1)} %all-to-all-done.parts_ref), custom_call_target="tpu_custom_call" | custom-call | tf_op jit(solution)/shard_map/pallas_call | solution.py:411
  85.2 9.6 %all-to-all-start.1 = ((f32[128,1,128]{2,1,0:T(1,128)}), f32[128,1,128]{2,1,0:T(1,128)S(1)}, u32[]{:S(2)}, u32[]{:S(2)}) async-start(f32[128,1,128]{2,1,0:T(1,128)} %shard_map.96), calls=%async_computation.1 | async-start | bytes 131072 | tf_op jit(solution)/shard_map/all_to_all | solution.py:446
  94.9 0.9 reshape.42
  95.8 0.6 reshape.43
  96.4 7.9 %all-to-all-done.1.gains_ref = f32[128,1,128]{2,1,0:T(1,128)S(1)} async-done(((f32[128,1,128]{2,1,0:T(1,128)}), f32[128,1,128]{2,1,0:T(1,128)S(1)}, u32[]{:S(2)}, u32[]{:S(2)}) %all-to-all-start.1) | async-done | bytes 65568 | tf_op jit(solution)/shard_map/all_to_all | solution.py:446
  104.2 0.6 shard_map.97
  (12 shorter events, 0.2 us)
Async XLA Ops:
  8.7 14.7 %collective-permute-start = (bf16[4608,256]{1,0:T(8,128)(2,1)}, bf16[4608,256]{1,0:T(8,128)(2,1)S(1)}, u32[]{:S(2)}, u32[]{:S(2)}) collective-permute-start(bf16[4608,256]{1,0:T(8,128)(2,1)} %get-tuple-element.13), channel_id=1, source_target_pairs={{0,1},{1,0},{2,3},{3,2},{4,5},{5,4},{6,7},{7,6},{8,9},{9,8},{10,11... | collective-permute-start | bytes 7077896 | tf_op jit(solution)/shard_map/ppermute | solution.py:458
  38.5 44.4 %all-to-all-start = ((s16[64,144,128]{2,1,0:T(8,128)(2,1)}), s16[64,144,128]{2,1,0:T(8,128)(2,1)S(1)}, u32[]{:S(2)}, u32[]{:S(2)}) async-start(s16[64,144,128]{2,1,0:T(8,128)(2,1)} %shard_map.95), calls=%async_computation | async-start | bytes 4718592 | tf_op jit(solution)/shard_map/all_to_all | solution.py:446
  58.7 1.6 %collective-permute-start.1 = (bf16[4,144,128]{2,1,0:T(8,128)(2,1)}, bf16[4,144,128]{2,1,0:T(8,128)(2,1)S(1)}, u32[]{:S(2)}, u32[]{:S(2)}) collective-permute-start(bf16[4,144,128]{2,1,0:T(8,128)(2,1)} %get-tuple-element.21), channel_id=1, source_target_pairs={{0,1},{1,0},{2,3},{3,2},{4,5},{5,4},{6,7},{7,6},{8,9},{9,8},{10,11... | collective-permute-start | bytes 442376 | tf_op jit(solution)/shard_map/ppermute | solution.py:340
  61.3 15.7 %collective-permute-start.2 = (bf16[2,144,128]{2,1,0:T(8,128)(2,1)S(1)}, bf16[2,144,128]{2,1,0:T(8,128)(2,1)S(1)}, u32[]{:S(2)}, u32[]{:S(2)}) collective-permute-start(bf16[2,144,128]{2,1,0:T(8,128)(2,1)S(1)} %get-tuple-element.24), channel_id=1, source_target_pairs={{0,6},{2,0},{4,2},{6,4},{1,7},{3,1},{5,3},{7,5},{8,14},{10,8},{12,... | collective-permute-start | bytes 221192 | tf_op jit(solution)/shard_map/ppermute | solution.py:348
  63.6 17.1 %collective-permute-start.3 = (bf16[2,144,128]{2,1,0:T(8,128)(2,1)S(1)}, bf16[2,144,128]{2,1,0:T(8,128)(2,1)S(1)}, u32[]{:S(2)}, u32[]{:S(2)}) collective-permute-start(bf16[2,144,128]{2,1,0:T(8,128)(2,1)S(1)} %get-tuple-element.25), channel_id=1, source_target_pairs={{0,4},{2,6},{4,0},{6,2},{1,5},{3,7},{5,1},{7,3},{8,12},{10,14},{12... | collective-permute-start | bytes 221192 | tf_op jit(solution)/shard_map/ppermute | solution.py:348
  64.1 18.7 %collective-permute-start.4 = (bf16[2,144,128]{2,1,0:T(8,128)(2,1)S(1)}, bf16[2,144,128]{2,1,0:T(8,128)(2,1)S(1)}, u32[]{:S(2)}, u32[]{:S(2)}) collective-permute-start(bf16[2,144,128]{2,1,0:T(8,128)(2,1)S(1)} %get-tuple-element.22), channel_id=1, source_target_pairs={{0,2},{2,4},{4,6},{6,0},{1,3},{3,5},{5,7},{7,1},{8,10},{10,12},{12... | collective-permute-start | bytes 221192 | tf_op jit(solution)/shard_map/ppermute | solution.py:348
  85.2 19.1 %all-to-all-start.1 = ((f32[128,1,128]{2,1,0:T(1,128)}), f32[128,1,128]{2,1,0:T(1,128)S(1)}, u32[]{:S(2)}, u32[]{:S(2)}) async-start(f32[128,1,128]{2,1,0:T(1,128)} %shard_map.96), calls=%async_computation.1 | async-start | bytes 131072 | tf_op jit(solution)/shard_map/all_to_all | solution.py:446

commit v4 on v3

--- a/solution.py
+++ b/solution.py
@@ -21,7 +21,6 @@
 AUX = 32
 AUX_CHUNK = HALF
 AUX_ROWS = ROW_DEV // AUX_CHUNK * AUX
-LANES = 2 * HALF
 SENT = COLS + LEAVES
 GRP = ("grp_0", "grp_1")
 ROWS_GRP = ("rows_0", "rows_1", "grp_0", "grp_1")
@@ -44,14 +43,20 @@
     return pltpu.CompilerParams(vmem_limit_bytes=mib << 20)
 
 
+def value_rows(weights, leaf):
+    lines = weights.astype(F32)
+    weight = jnp.concatenate([lines[i : i + 1] for i in range(lines.shape[0])], axis=1)
+    return (weight, leaf.astype(F32))
+
+
 def prep_kernel(
-    core_ref, codes_hbm, grads_hbm, weights_hbm, leaf_hbm, dup_hbm, send_hbm, data_hbm, aux_hbm,
-    codes_ref, grads_ref, weights_ref, leaf_ref, dup_ref, send_ref, data_ref, aux_ref, in_sems, out_sems,
+    core_ref, codes_hbm, grads_hbm, weights_hbm, leaf_hbm, send_hbm, aux_hbm,
+    codes_ref, grads_ref, weights_ref, leaf_ref, send_ref, aux_ref, in_sems, out_sems,
 ):
-    blocks = ROW_DEV // ROW_BLOCK
-    cuts = [slice(i * ROW_BLOCK, (i + 1) * ROW_BLOCK) for i in range(blocks)]
+    cuts = row_cuts()
+    theirs = pl.ds(pl.multiple_of((1 - core_ref[0]) * HALF, HALF), HALF)
     pairs = [(grads_hbm, grads_ref), (weights_hbm, weights_ref), (leaf_hbm, leaf_ref)]
-    pairs += [(codes_hbm.at[rows, :], codes_ref.at[rows, :]) for rows in cuts]
+    pairs += [(codes_hbm.at[rows, theirs], codes_ref.at[rows, :]) for rows in cuts]
     arriving = [pltpu.make_async_copy(a, b, in_sems.at[i]) for i, (a, b) in enumerate(pairs)]
     for copy in arriving:
         copy.start()
@@ -62,20 +67,10 @@
         copy.start()
         leaving.append(copy)
 
-    core = core_ref[0]
-    lane = iota((1, LANES + HALF), 1)
-    twice = ((lane >> 3) << 3) + (core << 2) + (lane & 3)
-    place = lane - LANES
-    once = ((place >> 2) << 3) + ((1 - core) << 2) + (place & 3)
-    wanted = jnp.where(lane < LANES, twice, once)
-    select = jnp.where(iota((FEATURES, LANES + HALF), 0) == wanted, 1.0, 0.0).astype(BF16)
-
     for copy in arriving[:3]:
         copy.wait()
-    weights = weights_ref[...].astype(F32)
+    weight, leaf = value_rows(weights_ref[...], leaf_ref[...])
     row = iota((TARGETS, ROW_DEV), 0)
-    weight = jnp.concatenate([weights[i : i + 1] for i in range(weights.shape[0])], axis=1)
-    leaf = leaf_ref[...].astype(F32)
     rest = jnp.where(row == 0, weight, jnp.where(row == 1, leaf, 0.0)).astype(BF16)
     aux_ref[:TARGETS, :] = grads_ref[...]
     aux_ref[TARGETS:, :] = rest
@@ -86,19 +81,16 @@
         send_ref[at : at + TARGETS, :] = grads_ref[:, lanes]
         send_ref[at + TARGETS : at + AUX, :] = rest[:, lanes]
     leave(send_ref.at[ROW_DEV:, :], send_hbm.at[ROW_DEV:, :])
-    spread_values(grads_ref[...].astype(F32), weight, leaf, data_ref)
-    leave(data_ref, data_hbm)
-
     for rows, copy in zip(cuts, arriving[3:]):
         copy.wait()
-        codes = codes_ref[rows, :].astype(F32).astype(BF16)
-        both = jnp.dot(codes, select, preferred_element_type=F32).astype(BF16)
-        dup_ref[rows, :] = both[:, :LANES]
-        send_ref[rows, :] = both[:, LANES:]
-        leave(dup_ref.at[rows, :], dup_hbm.at[rows, :])
+        send_ref[rows, :] = codes_ref[rows, :].astype(F32).astype(BF16)
         leave(send_ref.at[rows, :], send_hbm.at[rows, :])
     for copy in leaving:
         copy.wait()
+
+
+def row_cuts():
+    return [slice(i * ROW_BLOCK, (i + 1) * ROW_BLOCK) for i in range(ROW_DEV // ROW_BLOCK)]
 
 
 def spread_values(grads, weights, leaf, data_ref):
@@ -111,26 +103,20 @@
 def prep(core, codes, grads, weights, leaf):
     blocks = ROW_DEV // ROW_BLOCK
     there = pl.BlockSpec(memory_space=pl.ANY)
-    outs = [
-        (ROW_DEV, LANES),
-        (ROW_DEV + AUX_ROWS, HALF),
-        (COLS + TARGETS, ROW_DEV),
-        (AUX, ROW_DEV),
-    ]
+    outs = [(ROW_DEV + AUX_ROWS, HALF), (AUX, ROW_DEV)]
     ins = [codes, grads, weights, leaf]
     return pl.pallas_call(
         prep_kernel,
         in_specs=[pl.BlockSpec(memory_space=pltpu.SMEM)] + [there] * len(ins),
         out_specs=[there] * len(outs),
         out_shape=[pltpu.HBM(shape, BF16) for shape in outs],
-        scratch_shapes=[pltpu.VMEM(a.shape, a.dtype) for a in ins]
+        scratch_shapes=[pltpu.VMEM((ROW_DEV, HALF), I32)]
+        + [pltpu.VMEM(a.shape, a.dtype) for a in ins[1:]]
         + [pltpu.VMEM(shape, BF16) for shape in outs]
-        + [pltpu.SemaphoreType.DMA((blocks + 3,)), pltpu.SemaphoreType.DMA((2 * blocks + 3,))],
-        compiler_params=params(48),
+        + [pltpu.SemaphoreType.DMA((blocks + 3,)), pltpu.SemaphoreType.DMA((blocks + 2,))],
+        compiler_params=params(32),
         cost_estimate=pl.CostEstimate(
-            flops=2 * ROW_DEV * FEATURES * FEATURES,
-            bytes_accessed=ROW_DEV * FEATURES * 8,
-            transcendentals=0,
+            flops=ROW_DEV * HALF, bytes_accessed=ROW_DEV * HALF * 6, transcendentals=0
         ),
     )(core, *[in_hbm(a) for a in ins])
 
@@ -139,27 +125,9 @@
     return (aux[:TARGETS], aux[TARGETS : TARGETS + 1], aux[TARGETS + 1 : TARGETS + 2])
 
 
-def spread(rows_ref, dup_ref, data_ref):
-    lane = iota((1, LANES), 1)
-    source = ((lane >> 3) << 2) + (lane & 3)
-    twice = jnp.where(iota((HALF, LANES), 0) == source, 1.0, 0.0).astype(BF16)
-    for i in range(ROW_DEV // ROW_BLOCK):
-        rows = slice(i * ROW_BLOCK, (i + 1) * ROW_BLOCK)
-        dup_ref[rows, :] = jnp.dot(
-            rows_ref[rows, :], twice, preferred_element_type=F32
-        ).astype(BF16)
-    parts = [
-        rows_ref[ROW_DEV + i * AUX : ROW_DEV + (i + 1) * AUX, :]
-        for i in range(ROW_DEV // AUX_CHUNK)
-    ]
-    aux = jnp.concatenate(parts, axis=1).astype(F32)
-    spread_values(*split_aux(aux), data_ref)
-
-
-def pair_sums(pair, dup_ref, data_ref):
-    lane = iota((1, LANES), 1)
-    wanted = (2 * pair + ((lane >> 2) & 1)).astype(F32).astype(BF16)
-    hot = jnp.where(dup_ref[...] == wanted, jnp.ones((), BF16), jnp.zeros((), BF16))
+def bin_sums(index, codes_ref, data_ref):
+    wanted = jnp.full((1, HALF), 0.0, F32) + index.astype(F32)
+    hot = jnp.where(codes_ref[...] == wanted.astype(BF16), jnp.ones((), BF16), jnp.zeros((), BF16))
     return jnp.dot(data_ref[...], hot, preferred_element_type=F32)[:SENT]
 
 
@@ -168,44 +136,80 @@
 MESSAGE = COLS + 16
 
 
-def own_kernel(dup_ref, data_ref, sums_ref):
-    step = pl.program_id(0)
-    for i in range(UNROLL):
-        sums_ref[i] = pair_sums(step * UNROLL + i, dup_ref, data_ref)
-
-
-def both_kernel(rows_ref, sums_ref, out_ref, dup_ref, data_ref, total_ref, largest_ref, weights_ref):
+def own_kernel(
+    core_ref, codes_hbm, grads_hbm, weights_hbm, leaf_hbm, sums_ref,
+    whole_ref, grads_ref, weights_ref, leaf_ref, codes_ref, data_ref, sems,
+):
     step = pl.program_id(0)
 
     @pl.when(step == 0)
     def _():
-        spread(rows_ref, dup_ref, data_ref)
+        ours = pl.ds(pl.multiple_of(core_ref[0] * HALF, HALF), HALF)
+        pairs = [(grads_hbm, grads_ref), (weights_hbm, weights_ref), (leaf_hbm, leaf_ref)]
+        pairs += [(codes_hbm.at[rows, ours], whole_ref.at[rows, :]) for rows in row_cuts()]
+        arriving = [pltpu.make_async_copy(a, b, sems.at[i]) for i, (a, b) in enumerate(pairs)]
+        for copy in arriving:
+            copy.start()
+        for copy in arriving[:3]:
+            copy.wait()
+        weight, leaf = value_rows(weights_ref[...], leaf_ref[...])
+        spread_values(grads_ref[...].astype(F32), weight, leaf, data_ref)
+        for rows, copy in zip(row_cuts(), arriving[3:]):
+            copy.wait()
+            codes_ref[rows, :] = whole_ref[rows, :].astype(F32).astype(BF16)
+
+    for i in range(2 * UNROLL):
+        sums_ref[i] = bin_sums(step * (2 * UNROLL) + i, codes_ref, data_ref)
+
+
+def interleave(even, odd):
+    even, odd = (v.T.reshape(PEERS // 2, 8, COLS) for v in (even, odd))
+    low = iota(even.shape, 1) < OWNED
+    first = jnp.where(low, even, pltpu.roll(odd, OWNED, 1))
+    second = jnp.where(low, pltpu.roll(even, OWNED, 1), odd)
+    return (first, second)
+
+
+def both_kernel(rows_ref, sums_ref, out_ref, data_ref, total_ref, largest_ref, even_ref, odd_ref):
+    step = pl.program_id(0)
+
+    @pl.when(step == 0)
+    def _():
+        parts = [
+            rows_ref[ROW_DEV + i * AUX : ROW_DEV + (i + 1) * AUX, :]
+            for i in range(ROW_DEV // AUX_CHUNK)
+        ]
+        aux = jnp.concatenate(parts, axis=1).astype(F32)
+        spread_values(*split_aux(aux), data_ref)
         largest_ref[...] = jnp.zeros(largest_ref.shape, F32)
 
+    codes_ref = rows_ref.at[:ROW_DEV, :]
     for i in range(UNROLL):
         pair = step * UNROLL + i
-        sums = pair_sums(pair, dup_ref, data_ref) + sums_ref[i]
+        even = bin_sums(2 * pair, codes_ref, data_ref) + sums_ref[2 * i]
+        odd = bin_sums(2 * pair + 1, codes_ref, data_ref) + sums_ref[2 * i + 1]
         at = pl.multiple_of(pair * 8, 8)
-        turned = sums[:COLS].T.reshape(PEERS, 8, COLS)
-        total_ref[:, pl.ds(at, 8), :] = turned
-        largest_ref[...] = jnp.maximum(largest_ref[...], jnp.abs(turned))
-        weights_ref[pl.ds(at, 8), :] = sums[COLS:]
+        for side, values in enumerate(interleave(even[:COLS], odd[:COLS])):
+            total_ref[:, side, pl.ds(at, 8), :] = values
+            largest_ref[:, side] = jnp.maximum(largest_ref[:, side], jnp.abs(values))
+        even_ref[pl.ds(at, 8), :] = even[COLS:]
+        odd_ref[pl.ds(at, 8), :] = odd[COLS:]
 
     @pl.when(step == PAIRS // UNROLL - 1)
     def _():
-        weights = weights_ref[...].T.reshape(PEERS, 8, COLS)
-        most = jnp.abs(weights)
-        for lanes in (8, 16, 32, 64):
-            most = jnp.maximum(most, pltpu.roll(most, lanes, 2))
-        exp_g, exp_w = (exponents(largest_ref[...]), exponents(most))
-        scale_g, scale_w = (jnp.exp2(BITS - exp_g), jnp.exp2(BITS - exp_w))
-        for i in range(COLS // 16):
-            rows = slice(i * 16, (i + 1) * 16)
+        low = iota((PEERS // 2, 8, COLS), 1) < OWNED
+        for side, weights in enumerate(interleave(even_ref[...], odd_ref[...])):
+            most = jnp.abs(weights)
+            for lanes in (8, 16, 32, 64):
+                most = jnp.maximum(most, pltpu.roll(most, lanes, 2))
+            exp_g, exp_w = (exponents(largest_ref[:, side]), exponents(most))
+            scale_g, scale_w = (jnp.exp2(BITS - exp_g), jnp.exp2(BITS - exp_w))
             twice = jnp.concatenate([scale_g, scale_g], axis=1)
-            out_ref[:, rows, :] = whole(total_ref[:, rows, :] * twice)
-        even = iota((PEERS, 8, COLS), 1) < OWNED
-        last = [weights * scale_w, jnp.where(even, exp_g, exp_w)]
-        out_ref[:, COLS:, :] = whole(jnp.concatenate(last, axis=1))
+            for i in range(COLS // 16):
+                rows = slice(i * 16, (i + 1) * 16)
+                out_ref[:, side, rows, :] = whole(total_ref[:, side, rows, :] * twice)
+            last = [weights * scale_w, jnp.where(low, exp_g, exp_w)]
+            out_ref[:, side, COLS:, :] = whole(jnp.concatenate(last, axis=1))
 
 
 def exponents(magnitudes):
@@ -222,42 +226,49 @@
 )
 
 
-def own_sums(dup, data):
-    still = pl.Buffered(1)
+def own_sums(core, codes, grads, weights, leaf):
+    ins = [codes, grads, weights, leaf]
     return pl.pallas_call(
         own_kernel,
         grid=(PAIRS // UNROLL,),
-        in_specs=[
-            pl.BlockSpec(dup.shape, lambda i: (0, 0), pipeline_mode=still),
-            pl.BlockSpec(data.shape, lambda i: (0, 0), pipeline_mode=still),
-        ],
-        out_specs=pl.BlockSpec((UNROLL, SENT, LANES), lambda i: (i, 0, 0)),
-        out_shape=jax.ShapeDtypeStruct((PAIRS, SENT, LANES), F32),
+        in_specs=[pl.BlockSpec(memory_space=pltpu.SMEM)]
+        + [pl.BlockSpec(memory_space=pl.ANY)] * len(ins),
+        out_specs=pl.BlockSpec((2 * UNROLL, SENT, HALF), lambda i: (i, 0, 0)),
+        out_shape=jax.ShapeDtypeStruct((BINS, SENT, HALF), F32),
+        scratch_shapes=[pltpu.VMEM((ROW_DEV, HALF), I32)]
+        + [pltpu.VMEM(a.shape, a.dtype) for a in ins[1:]]
+        + [
+            pltpu.VMEM((ROW_DEV, HALF), BF16),
+            pltpu.VMEM((COLS + TARGETS, ROW_DEV), BF16),
+            pltpu.SemaphoreType.DMA((ROW_DEV // ROW_BLOCK + 3,)),
+        ],
         compiler_params=params(36),
         cost_estimate=HIST_COST,
-    )(in_hbm(dup), in_hbm(data))
+    )(core, *[in_hbm(a) for a in ins])
 
 
 def both_sums(rows, sums):
-    return pl.pallas_call(
+    halved = (PEERS // 2, 2)
+    out = pl.pallas_call(
         both_kernel,
         grid=(PAIRS // UNROLL,),
         in_specs=[
-            pl.BlockSpec(rows.shape, lambda i: (0, 0)),
-            pl.BlockSpec((UNROLL, SENT, LANES), lambda i: (i, 0, 0)),
-        ],
-        out_specs=pl.BlockSpec((PEERS, MESSAGE, COLS), lambda i: (0, 0, 0)),
-        out_shape=pltpu.HBM((PEERS, MESSAGE, COLS), jnp.int16),
+            pl.BlockSpec(rows.shape, lambda i: (0, 0), pipeline_mode=pl.Buffered(1)),
+            pl.BlockSpec((2 * UNROLL, SENT, HALF), lambda i: (i, 0, 0)),
+        ],
+        out_specs=pl.BlockSpec((*halved, MESSAGE, COLS), lambda i: (0, 0, 0, 0)),
+        out_shape=pltpu.HBM((*halved, MESSAGE, COLS), jnp.int16),
         scratch_shapes=[
-            pltpu.VMEM((ROW_DEV, LANES), BF16),
             pltpu.VMEM((COLS + TARGETS, ROW_DEV), BF16),
-            pltpu.VMEM((PEERS, COLS, COLS), F32),
-            pltpu.VMEM((PEERS, 8, COLS), F32),
-            pltpu.VMEM((COLS, LANES), F32),
+            pltpu.VMEM((*halved, COLS, COLS), F32),
+            pltpu.VMEM((*halved, 8, COLS), F32),
+            pltpu.VMEM((COLS, HALF), F32),
+            pltpu.VMEM((COLS, HALF), F32),
         ],
         compiler_params=params(40),
         cost_estimate=HIST_COST,
     )(rows, sums)
+    return out.reshape(PEERS, MESSAGE, COLS)
 
 
 def place_kernel(feature_ref, core_ref, bin_ref, aux_ref, codes_ref, keep_ref, give_ref):
@@ -418,7 +429,10 @@
 
 
 def close_kernel(group_ref, gains_ref, table_ref, best_ref):
-    table_ref[...] = gains_ref[pl.ds(group_ref[0] * 8, 8)]
+    group = group_ref[0]
+    first = (group & 7) * 16 + (group >> 3)
+    for i in range(8):
+        table_ref[i] = gains_ref[first + 2 * i]
     highest = jnp.max(gains_ref[...], axis=0)
     best_ref[...] = jnp.max(highest, axis=1, keepdims=True)
 
@@ -448,15 +462,10 @@
 
 def shards(bin_codes, leaf_index, gradients, row_weights, split_feature, split_bin):
     core = lax.axis_index("grp_1").astype(I32).reshape(1)
-    dup, send, data, aux = prep(
-        core,
-        bin_codes,
-        gradients.T,
-        row_weights.reshape(ROW_DEV // 128, 128),
-        leaf_index.reshape(1, ROW_DEV),
-    )
+    values = (gradients.T, row_weights.reshape(ROW_DEV // 128, 128), leaf_index.reshape(1, ROW_DEV))
+    send, aux = prep(core, bin_codes, *values)
     other = lax.ppermute(send, "grp_1", [(0, 1), (1, 0)])
-    sums = both_sums(other, own_sums(dup, data))
+    sums = both_sums(other, own_sums(core, bin_codes, *values))
     arrived = exchange(sums, CHIPS)
     aux, unused = lax.optimization_barrier((aux, sums))
     moved = deliver(*place_rows(split_feature, core, split_bin, aux, bin_codes))

time: 105 us -> 99.7 us (0.950)
  Pallas kernels: 46.5 us -> 41.1 us
    pallas_call x1, Pallas kernels: 8.02 us -> 3.85 us  [prep(): pl.pallas_call(prep_kernel, in_specs=[pl.BlockSpec(memory_space=pltpu.SME...]
where the time goes in v4:
time: 99.7 us; the launch traced here: 99.4 us
  Pallas kernels  41.1 us (41%)
  waiting for transfers between devices  27.2 us (27%)
  starting transfers between devices  26.3 us (26%)
  between operations  2.05 us (2%)
  local copies, waits for them, and re-layouts  1.68 us (2%)
    all_to_all x2, starting transfers between devices, exchange(): return lax.all_to_all(blocks, axis, split_axis=0, concat_axis=0, tiled=True)  21 us
    ppermute x3, waiting for transfers between devices, deliver(): block = lax.ppermute(block, 'grp_0', [(i, (i + s) % 4) for i in range(4)])  18.1 us
    pallas_call x1, Pallas kernels, both_sums(): pl.pallas_call(both_kernel, grid=(PAIRS // UNROLL,), in_specs=[pl.BlockSp...  14.2 us
    pallas_call x1, Pallas kernels, own_sums(): pl.pallas_call(own_kernel, grid=(PAIRS // UNROLL,), in_specs=[pl.BlockSpe...  12.8 us
    all_to_all x2, waiting for transfers between devices, exchange(): return lax.all_to_all(blocks, axis, split_axis=0, concat_axis=0, tiled=True)  7.86 us
    pallas_call x1, Pallas kernels, place_rows(): pl.pallas_call(place_kernel, grid_spec=pltpu.PrefetchScalarGridSpec(num_s...  7.44 us
    pallas_call x1, Pallas kernels, prep(): pl.pallas_call(prep_kernel, in_specs=[pl.BlockSpec(memory_space=pltpu.SME...  3.85 us
    ppermute x3, starting transfers between devices, deliver(): block = lax.ppermute(block, 'grp_0', [(i, (i + s) % 4) for i in range(4)])  3.51 us
  transfers between devices with their start and end apart: 7, of which 5 were waited for; matrix products, arithmetic and copies ran while one was open for 3% of the time, Pallas kernels for 20%

profile of v4, /device:TPU:1, one launch (start us, length us, event | category | flops | bytes accessed | tf_op | source)
XLA Modules:
  0.0 99.4 jit_solution(2381254395722661463)
XLA Ops:
  0.6 3.9 %shard_map.93 = (bf16[4608,256]{1,0:T(8,128)(2,1)}, bf16[32,4096]{1,0:T(8,128)(2,1)}) custom-call(s32[1]{0:T(128)} %bitcast.1.core_ref, s32[4096,512]{1,0:T(8,128)} %codes_ref.1, bf16[16,4096]{1,0:T(8,128)(2,1)} %bitcast.31, bf16[32,128]{1,0:T(8,128)(2,1)} %bitcast.35, s32[1,4096]{1,0:T(1,128)} %bitcast.33), custom_call_target="tpu_custom_call" | custom-call | flops 1048576 | bytes 6291456 | tf_op jit(solution)/shard_map/pallas_call | solution.py:108
  4.5 1.5 %collective-permute-start = (bf16[4608,256]{1,0:T(8,128)(2,1)}, bf16[4608,256]{1,0:T(8,128)(2,1)S(1)}, u32[]{:S(2)}, u32[]{:S(2)}) collective-permute-start(bf16[4608,256]{1,0:T(8,128)(2,1)} %get-tuple-element.11), channel_id=1, source_target_pairs={{0,1},{1,0},{2,3},{3,2},{4,5},{5,4},{6,7},{7,6},{8,9},{9,8},{10,11... | collective-permute-start | bytes 7077896 | tf_op jit(solution)/shard_map/ppermute | solution.py:467
  6.0 12.8 %shard_map.94.sums_ref = f32[32,136,256]{2,1,0:T(8,128)S(1)} custom-call(s32[1]{0:T(128)} %bitcast.1.core_ref, s32[4096,512]{1,0:T(8,128)} %codes_ref.1, bf16[16,4096]{1,0:T(8,128)(2,1)} %bitcast.32, bf16[32,128]{1,0:T(8,128)(2,1)} %bitcast.36, s32[1,4096]{1,0:T(1,128)} %bitcast.34), custom_call_target="tpu_custom_call" | custom-call | flops 17179869184 | bytes 8388608 | tf_op jit(solution)/shard_map/pallas_call | solution.py:231
  18.8 0.0 collective-permute-done.rows_ref
  18.9 14.2 %shard_map.95 = s16[32,2,144,128]{3,2,1,0:T(8,128)(2,1)} custom-call(bf16[4608,256]{1,0:T(8,128)(2,1)S(1)} %collective-permute-done.rows_ref, f32[32,136,256]{2,1,0:T(8,128)S(1)} %shard_map.94.sums_ref), custom_call_target="tpu_custom_call" | custom-call | flops 17179869184 | bytes 8388608 | tf_op jit(solution)/shard_map/pallas_call | solution.py:252
  33.0 11.4 %all-to-all-start = ((s16[64,144,128]{2,1,0:T(8,128)(2,1)}), s16[64,144,128]{2,1,0:T(8,128)(2,1)S(1)}, u32[]{:S(2)}, u32[]{:S(2)}) async-start(s16[64,144,128]{2,1,0:T(8,128)(2,1)} %bitcast.28), calls=%async_computation | async-start | bytes 4718592 | tf_op jit(solution)/shard_map/all_to_all | solution.py:460
  45.7 7.4 %shard_map.98 = (bf16[4,144,128]{2,1,0:T(8,128)(2,1)}, bf16[4,144,128]{2,1,0:T(8,128)(2,1)}) custom-call(s32[1]{0:T(128)S(6)} %copy.18.feature_ref, s32[1]{0:T(128)} %bitcast.1.core_ref, s32[1]{0:T(128)S(6)} %copy.19.bin_ref, bf16[32,4096]{1,0:T(8,128)(2,1)} %get-tuple-element.15.aux_ref, s32[4096,512]{1,0:T(8,128)} %codes_ref.1), custom_call_target="tpu_custom_call" | custom-call | flops 2147483648 | bytes 1048576 | tf_op jit(solution)/shard_map/pallas_call | solution.py:328
  53.1 0.3 collective-permute-start.1
  53.5 1.3 %collective-permute-done.1 = bf16[4,144,128]{2,1,0:T(8,128)(2,1)S(1)} collective-permute-done((bf16[4,144,128]{2,1,0:T(8,128)(2,1)}, bf16[4,144,128]{2,1,0:T(8,128)(2,1)S(1)}, u32[]{:S(2)}, u32[]{:S(2)}) %collective-permute-start.1) | collective-permute-done | bytes 147488 | tf_op jit(solution)/shard_map/ppermute | solution.py:351
  54.7 0.9 select_bitcast_fusion.1
  55.7 2.4 %collective-permute-start.2 = (bf16[2,144,128]{2,1,0:T(8,128)(2,1)S(1)}, bf16[2,144,128]{2,1,0:T(8,128)(2,1)S(1)}, u32[]{:S(2)}, u32[]{:S(2)}) collective-permute-start(bf16[2,144,128]{2,1,0:T(8,128)(2,1)S(1)} %get-tuple-element.20), channel_id=1, source_target_pairs={{0,6},{2,0},{4,2},{6,4},{1,7},{3,1},{5,3},{7,5},{8,14},{10,8},{12,... | collective-permute-start | bytes 221192 | tf_op jit(solution)/shard_map/ppermute | solution.py:359
  58.1 0.6 collective-permute-start.3
  58.6 0.6 collective-permute-start.4
  59.2 12.2 %collective-permute-done.2 = bf16[2,144,128]{2,1,0:T(8,128)(2,1)S(1)} collective-permute-done((bf16[2,144,128]{2,1,0:T(8,128)(2,1)S(1)}, bf16[2,144,128]{2,1,0:T(8,128)(2,1)S(1)}, u32[]{:S(2)}, u32[]{:S(2)}) %collective-permute-start.2) | collective-permute-done | bytes 73760 | tf_op jit(solution)/shard_map/ppermute | solution.py:359
  71.4 3.8 %collective-permute-done.3 = bf16[2,144,128]{2,1,0:T(8,128)(2,1)S(1)} collective-permute-done((bf16[2,144,128]{2,1,0:T(8,128)(2,1)S(1)}, bf16[2,144,128]{2,1,0:T(8,128)(2,1)S(1)}, u32[]{:S(2)}, u32[]{:S(2)}) %collective-permute-start.3) | collective-permute-done | bytes 73760 | tf_op jit(solution)/shard_map/ppermute | solution.py:359
  75.2 2.1 %collective-permute-done.4 = bf16[2,144,128]{2,1,0:T(8,128)(2,1)S(1)} collective-permute-done((bf16[2,144,128]{2,1,0:T(8,128)(2,1)S(1)}, bf16[2,144,128]{2,1,0:T(8,128)(2,1)S(1)}, u32[]{:S(2)}, u32[]{:S(2)}) %collective-permute-start.4) | collective-permute-done | bytes 73760 | tf_op jit(solution)/shard_map/ppermute | solution.py:359
  77.4 0.0 all-to-all-done.parts_ref
  77.5 2.2 %shard_map.96 = f32[128,1,128]{2,1,0:T(1,128)} custom-call(s16[64,144,128]{2,1,0:T(8,128)(2,1)S(1)} %all-to-all-done.parts_ref), custom_call_target="tpu_custom_call" | custom-call | tf_op jit(solution)/shard_map/pallas_call | solution.py:422
  79.7 9.6 %all-to-all-start.1 = ((f32[128,1,128]{2,1,0:T(1,128)}), f32[128,1,128]{2,1,0:T(1,128)S(1)}, u32[]{:S(2)}, u32[]{:S(2)}) async-start(f32[128,1,128]{2,1,0:T(1,128)} %shard_map.96), calls=%async_computation.1 | async-start | bytes 131072 | tf_op jit(solution)/shard_map/all_to_all | solution.py:460
  89.3 0.9 reshape.46
  90.2 0.6 reshape.47
  90.9 7.9 %all-to-all-done.1.gains_ref = f32[128,1,128]{2,1,0:T(1,128)S(1)} async-done(((f32[128,1,128]{2,1,0:T(1,128)}), f32[128,1,128]{2,1,0:T(1,128)S(1)}, u32[]{:S(2)}, u32[]{:S(2)}) %all-to-all-start.1) | async-done | bytes 65568 | tf_op jit(solution)/shard_map/all_to_all | solution.py:460
  98.7 0.6 shard_map.97
  (12 shorter events, 0.2 us)
Async XLA Ops:
  4.5 14.3 %collective-permute-start = (bf16[4608,256]{1,0:T(8,128)(2,1)}, bf16[4608,256]{1,0:T(8,128)(2,1)S(1)}, u32[]{:S(2)}, u32[]{:S(2)}) collective-permute-start(bf16[4608,256]{1,0:T(8,128)(2,1)} %get-tuple-element.11), channel_id=1, source_target_pairs={{0,1},{1,0},{2,3},{3,2},{4,5},{5,4},{6,7},{7,6},{8,9},{9,8},{10,11... | collective-permute-start | bytes 7077896 | tf_op jit(solution)/shard_map/ppermute | solution.py:467
  33.0 44.4 %all-to-all-start = ((s16[64,144,128]{2,1,0:T(8,128)(2,1)}), s16[64,144,128]{2,1,0:T(8,128)(2,1)S(1)}, u32[]{:S(2)}, u32[]{:S(2)}) async-start(s16[64,144,128]{2,1,0:T(8,128)(2,1)} %bitcast.28), calls=%async_computation | async-start | bytes 4718592 | tf_op jit(solution)/shard_map/all_to_all | solution.py:460
  53.1 1.6 %collective-permute-start.1 = (bf16[4,144,128]{2,1,0:T(8,128)(2,1)}, bf16[4,144,128]{2,1,0:T(8,128)(2,1)S(1)}, u32[]{:S(2)}, u32[]{:S(2)}) collective-permute-start(bf16[4,144,128]{2,1,0:T(8,128)(2,1)} %get-tuple-element.17), channel_id=1, source_target_pairs={{0,1},{1,0},{2,3},{3,2},{4,5},{5,4},{6,7},{7,6},{8,9},{9,8},{10,11... | collective-permute-start | bytes 442376 | tf_op jit(solution)/shard_map/ppermute | solution.py:351
  55.7 15.7 %collective-permute-start.2 = (bf16[2,144,128]{2,1,0:T(8,128)(2,1)S(1)}, bf16[2,144,128]{2,1,0:T(8,128)(2,1)S(1)}, u32[]{:S(2)}, u32[]{:S(2)}) collective-permute-start(bf16[2,144,128]{2,1,0:T(8,128)(2,1)S(1)} %get-tuple-element.20), channel_id=1, source_target_pairs={{0,6},{2,0},{4,2},{6,4},{1,7},{3,1},{5,3},{7,5},{8,14},{10,8},{12,... | collective-permute-start | bytes 221192 | tf_op jit(solution)/shard_map/ppermute | solution.py:359
  58.1 17.1 %collective-permute-start.3 = (bf16[2,144,128]{2,1,0:T(8,128)(2,1)S(1)}, bf16[2,144,128]{2,1,0:T(8,128)(2,1)S(1)}, u32[]{:S(2)}, u32[]{:S(2)}) collective-permute-start(bf16[2,144,128]{2,1,0:T(8,128)(2,1)S(1)} %get-tuple-element.21), channel_id=1, source_target_pairs={{0,4},{2,6},{4,0},{6,2},{1,5},{3,7},{5,1},{7,3},{8,12},{10,14},{12... | collective-permute-start | bytes 221192 | tf_op jit(solution)/shard_map/ppermute | solution.py:359
  58.6 18.7 %collective-permute-start.4 = (bf16[2,144,128]{2,1,0:T(8,128)(2,1)S(1)}, bf16[2,144,128]{2,1,0:T(8,128)(2,1)S(1)}, u32[]{:S(2)}, u32[]{:S(2)}) collective-permute-start(bf16[2,144,128]{2,1,0:T(8,128)(2,1)S(1)} %get-tuple-element.18), channel_id=1, source_target_pairs={{0,2},{2,4},{4,6},{6,0},{1,3},{3,5},{5,7},{7,1},{8,10},{10,12},{12... | collective-permute-start | bytes 221192 | tf_op jit(solution)/shard_map/ppermute | solution.py:359
  79.7 19.0 %all-to-all-start.1 = ((f32[128,1,128]{2,1,0:T(1,128)}), f32[128,1,128]{2,1,0:T(1,128)S(1)}, u32[]{:S(2)}, u32[]{:S(2)}) async-start(f32[128,1,128]{2,1,0:T(1,128)} %shard_map.96), calls=%async_computation.1 | async-start | bytes 131072 | tf_op jit(solution)/shard_map/all_to_all | solution.py:460

commit v5 on v4

--- a/solution.py
+++ b/solution.py
@@ -125,13 +125,18 @@
     return (aux[:TARGETS], aux[TARGETS : TARGETS + 1], aux[TARGETS + 1 : TARGETS + 2])
 
 
-def bin_sums(index, codes_ref, data_ref):
+def bin_sums(index, codes_ref, data_ref, rows=slice(None)):
     wanted = jnp.full((1, HALF), 0.0, F32) + index.astype(F32)
-    hot = jnp.where(codes_ref[...] == wanted.astype(BF16), jnp.ones((), BF16), jnp.zeros((), BF16))
-    return jnp.dot(data_ref[...], hot, preferred_element_type=F32)[:SENT]
+    codes = codes_ref[rows, :]
+    hot = jnp.where(codes == wanted.astype(BF16), jnp.ones((), BF16), jnp.zeros((), BF16))
+    return jnp.dot(data_ref[:, rows], hot, preferred_element_type=F32)[:SENT]
+
+
+ROW_HALVES = (slice(0, ROW_DEV // 2), slice(ROW_DEV // 2, ROW_DEV))
 
 
 UNROLL = 4
+DEEPER = 8
 BITS = 15.0
 MESSAGE = COLS + 16
 
@@ -154,12 +159,20 @@
             copy.wait()
         weight, leaf = value_rows(weights_ref[...], leaf_ref[...])
         spread_values(grads_ref[...].astype(F32), weight, leaf, data_ref)
-        for rows, copy in zip(row_cuts(), arriving[3:]):
-            copy.wait()
-            codes_ref[rows, :] = whole_ref[rows, :].astype(F32).astype(BF16)
-
-    for i in range(2 * UNROLL):
-        sums_ref[i] = bin_sums(step * (2 * UNROLL) + i, codes_ref, data_ref)
+        codes_arriving = list(zip(row_cuts(), arriving[3:]))
+        count = len(codes_arriving) // 2
+        for part, half in enumerate(ROW_HALVES):
+            for rows, copy in codes_arriving[part * count : (part + 1) * count]:
+                copy.wait()
+                codes_ref[rows, :] = whole_ref[rows, :].astype(F32).astype(BF16)
+            for i in range(2 * UNROLL):
+                sums = bin_sums(step + i, codes_ref, data_ref, half)
+                sums_ref[i] = sums_ref[i] + sums if part else sums
+
+    @pl.when(step > 0)
+    def _():
+        for i in range(2 * UNROLL):
+            sums_ref[i] = bin_sums(step * (2 * UNROLL) + i, codes_ref, data_ref)
 
 
 def interleave(even, odd):
@@ -184,8 +197,8 @@
         largest_ref[...] = jnp.zeros(largest_ref.shape, F32)
 
     codes_ref = rows_ref.at[:ROW_DEV, :]
-    for i in range(UNROLL):
-        pair = step * UNROLL + i
+    for i in range(DEEPER):
+        pair = step * DEEPER + i
         even = bin_sums(2 * pair, codes_ref, data_ref) + sums_ref[2 * i]
         odd = bin_sums(2 * pair + 1, codes_ref, data_ref) + sums_ref[2 * i + 1]
         at = pl.multiple_of(pair * 8, 8)
@@ -195,7 +208,7 @@
         even_ref[pl.ds(at, 8), :] = even[COLS:]
         odd_ref[pl.ds(at, 8), :] = odd[COLS:]
 
-    @pl.when(step == PAIRS // UNROLL - 1)
+    @pl.when(step == PAIRS // DEEPER - 1)
     def _():
         low = iota((PEERS // 2, 8, COLS), 1) < OWNED
         for side, weights in enumerate(interleave(even_ref[...], odd_ref[...])):
@@ -251,10 +264,10 @@
     halved = (PEERS // 2, 2)
     out = pl.pallas_call(
         both_kernel,
-        grid=(PAIRS // UNROLL,),
+        grid=(PAIRS // DEEPER,),
         in_specs=[
             pl.BlockSpec(rows.shape, lambda i: (0, 0), pipeline_mode=pl.Buffered(1)),
-            pl.BlockSpec((2 * UNROLL, SENT, HALF), lambda i: (i, 0, 0)),
+            pl.BlockSpec((2 * DEEPER, SENT, HALF), lambda i: (i, 0, 0)),
         ],
         out_specs=pl.BlockSpec((*halved, MESSAGE, COLS), lambda i: (0, 0, 0, 0)),
         out_shape=pltpu.HBM((*halved, MESSAGE, COLS), jnp.int16),

time: 99.7 us -> 99 us (level)
  no operation moved by 1% of the time
where the time goes in v5:
time: 99 us; the launch traced here: 98.7 us
  Pallas kernels  40.2 us (41%)
  waiting for transfers between devices  27 us (27%)
  starting transfers between devices  26.8 us (27%)
  between operations  2.05 us (2%)
  local copies, waits for them, and re-layouts  1.68 us (2%)
  other arithmetic  0.99 us (1%)
    all_to_all x2, starting transfers between devices, exchange(): return lax.all_to_all(blocks, axis, split_axis=0, concat_axis=0, tiled=True)  21.1 us
    ppermute x3, waiting for transfers between devices, deliver(): block = lax.ppermute(block, 'grp_0', [(i, (i + s) % 4) for i in range(4)])  17.9 us
    pallas_call x1, Pallas kernels, both_sums(): pl.pallas_call(both_kernel, grid=(PAIRS // DEEPER,), in_specs=[pl.BlockSp...  13.7 us
    pallas_call x1, Pallas kernels, own_sums(): pl.pallas_call(own_kernel, grid=(PAIRS // UNROLL,), in_specs=[pl.BlockSpe...  12.4 us
    all_to_all x2, waiting for transfers between devices, exchange(): return lax.all_to_all(blocks, axis, split_axis=0, concat_axis=0, tiled=True)  7.86 us
    pallas_call x1, Pallas kernels, place_rows(): pl.pallas_call(place_kernel, grid_spec=pltpu.PrefetchScalarGridSpec(num_s...  7.44 us
    ppermute x3, starting transfers between devices, deliver(): block = lax.ppermute(block, 'grp_0', [(i, (i + s) % 4) for i in range(4)])  3.9 us
    pallas_call x1, Pallas kernels, prep(): pl.pallas_call(prep_kernel, in_specs=[pl.BlockSpec(memory_space=pltpu.SME...  3.85 us
  transfers between devices with their start and end apart: 7, of which 5 were waited for; matrix products, arithmetic and copies ran while one was open for 3% of the time, Pallas kernels for 20%

profile of v5, /device:TPU:1, one launch (start us, length us, event | category | flops | bytes accessed | tf_op | source)
XLA Modules:
  0.0 98.7 jit_solution(12200796378579638004)
XLA Ops:
  0.6 3.9 %shard_map.93 = (bf16[4608,256]{1,0:T(8,128)(2,1)}, bf16[32,4096]{1,0:T(8,128)(2,1)}) custom-call(s32[1]{0:T(128)} %bitcast.1.core_ref, s32[4096,512]{1,0:T(8,128)} %codes_ref.1, bf16[16,4096]{1,0:T(8,128)(2,1)} %bitcast.31, bf16[32,128]{1,0:T(8,128)(2,1)} %bitcast.35, s32[1,4096]{1,0:T(1,128)} %bitcast.33), custom_call_target="tpu_custom_call" | custom-call | flops 1048576 | bytes 6291456 | tf_op jit(solution)/shard_map/pallas_call | solution.py:108
  4.5 1.5 %collective-permute-start = (bf16[4608,256]{1,0:T(8,128)(2,1)}, bf16[4608,256]{1,0:T(8,128)(2,1)S(1)}, u32[]{:S(2)}, u32[]{:S(2)}) collective-permute-start(bf16[4608,256]{1,0:T(8,128)(2,1)} %get-tuple-element.11), channel_id=1, source_target_pairs={{0,1},{1,0},{2,3},{3,2},{4,5},{5,4},{6,7},{7,6},{8,9},{9,8},{10,11... | collective-permute-start | bytes 7077896 | tf_op jit(solution)/shard_map/ppermute | solution.py:480
  6.0 12.4 %shard_map.94.sums_ref = f32[32,136,256]{2,1,0:T(8,128)S(1)} custom-call(s32[1]{0:T(128)} %bitcast.1.core_ref, s32[4096,512]{1,0:T(8,128)} %codes_ref.1, bf16[16,4096]{1,0:T(8,128)(2,1)} %bitcast.32, bf16[32,128]{1,0:T(8,128)(2,1)} %bitcast.36, s32[1,4096]{1,0:T(1,128)} %bitcast.34), custom_call_target="tpu_custom_call" | custom-call | flops 17179869184 | bytes 8388608 | tf_op jit(solution)/shard_map/pallas_call | solution.py:244
  18.4 0.0 collective-permute-done.rows_ref
  18.4 13.7 %shard_map.95 = s16[32,2,144,128]{3,2,1,0:T(8,128)(2,1)} custom-call(bf16[4608,256]{1,0:T(8,128)(2,1)S(1)} %collective-permute-done.rows_ref, f32[32,136,256]{2,1,0:T(8,128)S(1)} %shard_map.94.sums_ref), custom_call_target="tpu_custom_call" | custom-call | flops 17179869184 | bytes 8388608 | tf_op jit(solution)/shard_map/pallas_call | solution.py:265
  32.1 11.2 %all-to-all-start = ((s16[64,144,128]{2,1,0:T(8,128)(2,1)}), s16[64,144,128]{2,1,0:T(8,128)(2,1)S(1)}, u32[]{:S(2)}, u32[]{:S(2)}) async-start(s16[64,144,128]{2,1,0:T(8,128)(2,1)} %bitcast.28), calls=%async_computation | async-start | bytes 4718592 | tf_op jit(solution)/shard_map/all_to_all | solution.py:473
  44.6 7.4 %shard_map.98 = (bf16[4,144,128]{2,1,0:T(8,128)(2,1)}, bf16[4,144,128]{2,1,0:T(8,128)(2,1)}) custom-call(s32[1]{0:T(128)S(6)} %copy.18.feature_ref, s32[1]{0:T(128)} %bitcast.1.core_ref, s32[1]{0:T(128)S(6)} %copy.19.bin_ref, bf16[32,4096]{1,0:T(8,128)(2,1)} %get-tuple-element.15.aux_ref, s32[4096,512]{1,0:T(8,128)} %codes_ref.1), custom_call_target="tpu_custom_call" | custom-call | flops 2147483648 | bytes 1048576 | tf_op jit(solution)/shard_map/pallas_call | solution.py:341
  52.0 0.3 collective-permute-start.1
  52.3 1.3 %collective-permute-done.1 = bf16[4,144,128]{2,1,0:T(8,128)(2,1)S(1)} collective-permute-done((bf16[4,144,128]{2,1,0:T(8,128)(2,1)}, bf16[4,144,128]{2,1,0:T(8,128)(2,1)S(1)}, u32[]{:S(2)}, u32[]{:S(2)}) %collective-permute-start.1) | collective-permute-done | bytes 147488 | tf_op jit(solution)/shard_map/ppermute | solution.py:364
  53.6 0.9 select_bitcast_fusion.1
  54.6 2.8 %collective-permute-start.2 = (bf16[2,144,128]{2,1,0:T(8,128)(2,1)S(1)}, bf16[2,144,128]{2,1,0:T(8,128)(2,1)S(1)}, u32[]{:S(2)}, u32[]{:S(2)}) collective-permute-start(bf16[2,144,128]{2,1,0:T(8,128)(2,1)S(1)} %get-tuple-element.20), channel_id=1, source_target_pairs={{0,6},{2,0},{4,2},{6,4},{1,7},{3,1},{5,3},{7,5},{8,14},{10,8},{12,... | collective-permute-start | bytes 221192 | tf_op jit(solution)/shard_map/ppermute | solution.py:372
  57.3 0.6 collective-permute-start.3
  57.9 0.6 collective-permute-start.4
  58.5 11.9 %collective-permute-done.2 = bf16[2,144,128]{2,1,0:T(8,128)(2,1)S(1)} collective-permute-done((bf16[2,144,128]{2,1,0:T(8,128)(2,1)S(1)}, bf16[2,144,128]{2,1,0:T(8,128)(2,1)S(1)}, u32[]{:S(2)}, u32[]{:S(2)}) %collective-permute-start.2) | collective-permute-done | bytes 73760 | tf_op jit(solution)/shard_map/ppermute | solution.py:372
  70.4 3.8 %collective-permute-done.3 = bf16[2,144,128]{2,1,0:T(8,128)(2,1)S(1)} collective-permute-done((bf16[2,144,128]{2,1,0:T(8,128)(2,1)S(1)}, bf16[2,144,128]{2,1,0:T(8,128)(2,1)S(1)}, u32[]{:S(2)}, u32[]{:S(2)}) %collective-permute-start.3) | collective-permute-done | bytes 73760 | tf_op jit(solution)/shard_map/ppermute | solution.py:372
  74.3 2.1 %collective-permute-done.4 = bf16[2,144,128]{2,1,0:T(8,128)(2,1)S(1)} collective-permute-done((bf16[2,144,128]{2,1,0:T(8,128)(2,1)S(1)}, bf16[2,144,128]{2,1,0:T(8,128)(2,1)S(1)}, u32[]{:S(2)}, u32[]{:S(2)}) %collective-permute-start.4) | collective-permute-done | bytes 73760 | tf_op jit(solution)/shard_map/ppermute | solution.py:372
  76.5 0.0 all-to-all-done.parts_ref
  76.5 2.2 %shard_map.96 = f32[128,1,128]{2,1,0:T(1,128)} custom-call(s16[64,144,128]{2,1,0:T(8,128)(2,1)S(1)} %all-to-all-done.parts_ref), custom_call_target="tpu_custom_call" | custom-call | tf_op jit(solution)/shard_map/pallas_call | solution.py:435
  78.7 9.9 %all-to-all-start.1 = ((f32[128,1,128]{2,1,0:T(1,128)}), f32[128,1,128]{2,1,0:T(1,128)S(1)}, u32[]{:S(2)}, u32[]{:S(2)}) async-start(f32[128,1,128]{2,1,0:T(1,128)} %shard_map.96), calls=%async_computation.1 | async-start | bytes 131072 | tf_op jit(solution)/shard_map/all_to_all | solution.py:473
  88.7 0.9 reshape.46
  89.6 0.6 reshape.47
  90.2 7.9 %all-to-all-done.1.gains_ref = f32[128,1,128]{2,1,0:T(1,128)S(1)} async-done(((f32[128,1,128]{2,1,0:T(1,128)}), f32[128,1,128]{2,1,0:T(1,128)S(1)}, u32[]{:S(2)}, u32[]{:S(2)}) %all-to-all-start.1) | async-done | bytes 65568 | tf_op jit(solution)/shard_map/all_to_all | solution.py:473
  98.1 0.6 shard_map.97
  (12 shorter events, 0.2 us)
Async XLA Ops:
  4.5 13.9 %collective-permute-start = (bf16[4608,256]{1,0:T(8,128)(2,1)}, bf16[4608,256]{1,0:T(8,128)(2,1)S(1)}, u32[]{:S(2)}, u32[]{:S(2)}) collective-permute-start(bf16[4608,256]{1,0:T(8,128)(2,1)} %get-tuple-element.11), channel_id=1, source_target_pairs={{0,1},{1,0},{2,3},{3,2},{4,5},{5,4},{6,7},{7,6},{8,9},{9,8},{10,11... | collective-permute-start | bytes 7077896 | tf_op jit(solution)/shard_map/ppermute | solution.py:480
  32.1 44.4 %all-to-all-start = ((s16[64,144,128]{2,1,0:T(8,128)(2,1)}), s16[64,144,128]{2,1,0:T(8,128)(2,1)S(1)}, u32[]{:S(2)}, u32[]{:S(2)}) async-start(s16[64,144,128]{2,1,0:T(8,128)(2,1)} %bitcast.28), calls=%async_computation | async-start | bytes 4718592 | tf_op jit(solution)/shard_map/all_to_all | solution.py:473
  52.0 1.6 %collective-permute-start.1 = (bf16[4,144,128]{2,1,0:T(8,128)(2,1)}, bf16[4,144,128]{2,1,0:T(8,128)(2,1)S(1)}, u32[]{:S(2)}, u32[]{:S(2)}) collective-permute-start(bf16[4,144,128]{2,1,0:T(8,128)(2,1)} %get-tuple-element.17), channel_id=1, source_target_pairs={{0,1},{1,0},{2,3},{3,2},{4,5},{5,4},{6,7},{7,6},{8,9},{9,8},{10,11... | collective-permute-start | bytes 442376 | tf_op jit(solution)/shard_map/ppermute | solution.py:364
  54.6 15.8 %collective-permute-start.2 = (bf16[2,144,128]{2,1,0:T(8,128)(2,1)S(1)}, bf16[2,144,128]{2,1,0:T(8,128)(2,1)S(1)}, u32[]{:S(2)}, u32[]{:S(2)}) collective-permute-start(bf16[2,144,128]{2,1,0:T(8,128)(2,1)S(1)} %get-tuple-element.20), channel_id=1, source_target_pairs={{0,6},{2,0},{4,2},{6,4},{1,7},{3,1},{5,3},{7,5},{8,14},{10,8},{12,... | collective-permute-start | bytes 221192 | tf_op jit(solution)/shard_map/ppermute | solution.py:372
  57.3 16.9 %collective-permute-start.3 = (bf16[2,144,128]{2,1,0:T(8,128)(2,1)S(1)}, bf16[2,144,128]{2,1,0:T(8,128)(2,1)S(1)}, u32[]{:S(2)}, u32[]{:S(2)}) collective-permute-start(bf16[2,144,128]{2,1,0:T(8,128)(2,1)S(1)} %get-tuple-element.21), channel_id=1, source_target_pairs={{0,4},{2,6},{4,0},{6,2},{1,5},{3,7},{5,1},{7,3},{8,12},{10,14},{12... | collective-permute-start | bytes 221192 | tf_op jit(solution)/shard_map/ppermute | solution.py:372
  57.9 18.5 %collective-permute-start.4 = (bf16[2,144,128]{2,1,0:T(8,128)(2,1)S(1)}, bf16[2,144,128]{2,1,0:T(8,128)(2,1)S(1)}, u32[]{:S(2)}, u32[]{:S(2)}) collective-permute-start(bf16[2,144,128]{2,1,0:T(8,128)(2,1)S(1)} %get-tuple-element.18), channel_id=1, source_target_pairs={{0,2},{2,4},{4,6},{6,0},{1,3},{3,5},{5,7},{7,1},{8,10},{10,12},{12... | collective-permute-start | bytes 221192 | tf_op jit(solution)/shard_map/ppermute | solution.py:372
  78.7 19.3 %all-to-all-start.1 = ((f32[128,1,128]{2,1,0:T(1,128)}), f32[128,1,128]{2,1,0:T(1,128)S(1)}, u32[]{:S(2)}, u32[]{:S(2)}) async-start(f32[128,1,128]{2,1,0:T(1,128)} %shard_map.96), calls=%async_computation.1 | async-start | bytes 131072 | tf_op jit(solution)/shard_map/all_to_all | solution.py:473

commit v6 on v5

--- a/solution.py
+++ b/solution.py
@@ -359,7 +359,7 @@
     )(split_feature, core, split_bin, aux, codes)
 
 
-def deliver(keep, give):
+def deliver(keep, give, gains):
     core, chip = (lax.axis_index("grp_1"), lax.axis_index("grp_0"))
     got = lax.ppermute(give, "grp_1", [(0, 1), (1, 0)])
     first = jnp.where(core == 0, keep, got)
@@ -371,6 +371,7 @@
         if s:
             block = lax.ppermute(block, "grp_0", [(i, (i + s) % 4) for i in range(4)])
         arrived.append(block)
+    *arrived, gains = lax.optimization_barrier((*arrived, gains))
     turned = jnp.stack([arrived[0], arrived[3], arrived[2], arrived[1]] * 2)
     ordered = lax.dynamic_slice_in_dim(turned, (4 - chip) % 4, 4, 0)
     return ordered.reshape(8, COLS + 16, 128)
@@ -481,8 +482,9 @@
     sums = both_sums(other, own_sums(core, bin_codes, *values))
     arrived = exchange(sums, CHIPS)
     aux, unused = lax.optimization_barrier((aux, sums))
-    moved = deliver(*place_rows(split_feature, core, split_bin, aux, bin_codes))
-    everyone = exchange(owned_gains(arrived), ROWS_GRP)
+    gains = owned_gains(arrived)
+    moved = deliver(*place_rows(split_feature, core, split_bin, aux, bin_codes), gains)
+    everyone = exchange(gains, ROWS_GRP)
     table, best = close(lax.axis_index(ROWS).astype(I32).reshape(1), everyone)
     table, best = (table.reshape(-1), best.reshape(1))
     moved_gradients = moved[:, :COLS].reshape(1, -1)

time: 99 us -> 98 us (0.990)
  waiting for transfers between devices: 27 us -> 24.5 us
  starting transfers between devices: 26.8 us -> 28.3 us
    ppermute x3, waiting for transfers between devices: 17.9 us -> 0.01 us  [deliver(): block = lax.ppermute(block, 'grp_0', [(i, (i + s) % 4) for i in range(4)])]
    all_to_all x2, waiting for transfers between devices: 7.86 us -> 23.2 us  [exchange(): return lax.all_to_all(blocks, axis, split_axis=0, concat_axis=0, tiled=True)]
    ppermute x3, starting transfers between devices: 3.9 us -> 5.11 us  [deliver(): block = lax.ppermute(block, 'grp_0', [(i, (i + s) % 4) for i in range(4)])]
  transfers between devices with their start and end apart: 7 -> 7, of which waited for: 5 -> 3; matrix products, arithmetic and copies ran while one was open for 3% -> 3% of each run, Pallas kernels for 20% -> 23%
where the time goes in v6:
time: 98 us; the launch traced here: 97.6 us
  Pallas kernels  40.2 us (41%)
  starting transfers between devices  28.3 us (29%)
  waiting for transfers between devices  24.5 us (25%)
  between operations  2.07 us (2%)
  local copies, waits for them, and re-layouts  1.68 us (2%)
  other arithmetic  0.98 us (1%)
    all_to_all x2, waiting for transfers between devices, exchange(): return lax.all_to_all(blocks, axis, split_axis=0, concat_axis=0, tiled=True)  23.2 us
    all_to_all x2, starting transfers between devices, exchange(): return lax.all_to_all(blocks, axis, split_axis=0, concat_axis=0, tiled=True)  21.3 us
    pallas_call x1, Pallas kernels, both_sums(): pl.pallas_call(both_kernel, grid=(PAIRS // DEEPER,), in_specs=[pl.BlockSp...  13.7 us
    pallas_call x1, Pallas kernels, own_sums(): pl.pallas_call(own_kernel, grid=(PAIRS // UNROLL,), in_specs=[pl.BlockSpe...  12.4 us
    pallas_call x1, Pallas kernels, place_rows(): pl.pallas_call(place_kernel, grid_spec=pltpu.PrefetchScalarGridSpec(num_s...  7.44 us
    ppermute x3, starting transfers between devices, deliver(): block = lax.ppermute(block, 'grp_0', [(i, (i + s) % 4) for i in range(4)])  5.11 us
    pallas_call x1, Pallas kernels, prep(): pl.pallas_call(prep_kernel, in_specs=[pl.BlockSpec(memory_space=pltpu.SME...  3.85 us
    pallas_call x1, Pallas kernels, owned_gains(): pl.pallas_call(gain_kernel, out_shape=jax.ShapeDtypeStruct(shape, F32), i...  2.22 us
  transfers between devices with their start and end apart: 7, of which 3 were waited for; matrix products, arithmetic and copies ran while one was open for 3% of the time, Pallas kernels for 23%

profile of v6, /device:TPU:1, one launch (start us, length us, event | category | flops | bytes accessed | tf_op | source)
XLA Modules:
  0.0 97.6 jit_solution(10031492977965103341)
XLA Ops:
  0.6 3.9 %shard_map.93 = (bf16[4608,256]{1,0:T(8,128)(2,1)}, bf16[32,4096]{1,0:T(8,128)(2,1)}) custom-call(s32[1]{0:T(128)} %bitcast.1.core_ref, s32[4096,512]{1,0:T(8,128)} %codes_ref.1, bf16[16,4096]{1,0:T(8,128)(2,1)} %bitcast.36, bf16[32,128]{1,0:T(8,128)(2,1)} %bitcast.40, s32[1,4096]{1,0:T(1,128)} %bitcast.38), custom_call_target="tpu_custom_call" | custom-call | flops 1048576 | bytes 6291456 | tf_op jit(solution)/shard_map/pallas_call | solution.py:108
  4.5 1.5 %collective-permute-start = (bf16[4608,256]{1,0:T(8,128)(2,1)}, bf16[4608,256]{1,0:T(8,128)(2,1)S(1)}, u32[]{:S(2)}, u32[]{:S(2)}) collective-permute-start(bf16[4608,256]{1,0:T(8,128)(2,1)} %get-tuple-element.15), channel_id=1, source_target_pairs={{0,1},{1,0},{2,3},{3,2},{4,5},{5,4},{6,7},{7,6},{8,9},{9,8},{10,11... | collective-permute-start | bytes 7077896 | tf_op jit(solution)/shard_map/ppermute | solution.py:481
  6.0 12.4 %shard_map.94.sums_ref = f32[32,136,256]{2,1,0:T(8,128)S(1)} custom-call(s32[1]{0:T(128)} %bitcast.1.core_ref, s32[4096,512]{1,0:T(8,128)} %codes_ref.1, bf16[16,4096]{1,0:T(8,128)(2,1)} %bitcast.37, bf16[32,128]{1,0:T(8,128)(2,1)} %bitcast.41, s32[1,4096]{1,0:T(1,128)} %bitcast.39), custom_call_target="tpu_custom_call" | custom-call | flops 17179869184 | bytes 8388608 | tf_op jit(solution)/shard_map/pallas_call | solution.py:244
  18.4 0.0 collective-permute-done.rows_ref
  18.4 13.7 %shard_map.95 = s16[32,2,144,128]{3,2,1,0:T(8,128)(2,1)} custom-call(bf16[4608,256]{1,0:T(8,128)(2,1)S(1)} %collective-permute-done.rows_ref, f32[32,136,256]{2,1,0:T(8,128)S(1)} %shard_map.94.sums_ref), custom_call_target="tpu_custom_call" | custom-call | flops 17179869184 | bytes 8388608 | tf_op jit(solution)/shard_map/pallas_call | solution.py:265
  32.1 11.2 %all-to-all-start = ((s16[64,144,128]{2,1,0:T(8,128)(2,1)}), s16[64,144,128]{2,1,0:T(8,128)(2,1)S(1)}, u32[]{:S(2)}, u32[]{:S(2)}) async-start(s16[64,144,128]{2,1,0:T(8,128)(2,1)} %bitcast.33), calls=%async_computation | async-start | bytes 4718592 | tf_op jit(solution)/shard_map/all_to_all | solution.py:474
  44.6 7.4 %shard_map.98 = (bf16[4,144,128]{2,1,0:T(8,128)(2,1)}, bf16[4,144,128]{2,1,0:T(8,128)(2,1)}) custom-call(s32[1]{0:T(128)S(6)} %copy.17.feature_ref, s32[1]{0:T(128)} %bitcast.1.core_ref, s32[1]{0:T(128)S(6)} %copy.18.bin_ref, bf16[32,4096]{1,0:T(8,128)(2,1)} %get-tuple-element.19.aux_ref, s32[4096,512]{1,0:T(8,128)} %codes_ref.1), custom_call_target="tpu_custom_call" | custom-call | flops 2147483648 | bytes 1048576 | tf_op jit(solution)/shard_map/pallas_call | solution.py:341
  52.0 0.3 collective-permute-start.1
  52.3 1.3 %collective-permute-done.1 = bf16[4,144,128]{2,1,0:T(8,128)(2,1)S(1)} collective-permute-done((bf16[4,144,128]{2,1,0:T(8,128)(2,1)}, bf16[4,144,128]{2,1,0:T(8,128)(2,1)S(1)}, u32[]{:S(2)}, u32[]{:S(2)}) %collective-permute-start.1) | collective-permute-done | bytes 147488 | tf_op jit(solution)/shard_map/ppermute | solution.py:364
  53.6 0.9 select_bitcast_fusion
  54.6 1.5 %collective-permute-start.2 = (bf16[2,144,128]{2,1,0:T(8,128)(2,1)S(1)}, bf16[2,144,128]{2,1,0:T(8,128)(2,1)S(1)}, u32[]{:S(2)}, u32[]{:S(2)}) collective-permute-start(bf16[2,144,128]{2,1,0:T(8,128)(2,1)S(1)} %get-tuple-element.28), channel_id=1, source_target_pairs={{0,2},{2,4},{4,6},{6,0},{1,3},{3,5},{5,7},{7,1},{8,10},{10,12},{12... | collective-permute-start | bytes 221192 | tf_op jit(solution)/shard_map/ppermute | solution.py:372
  56.1 2.4 %collective-permute-start.3 = (bf16[2,144,128]{2,1,0:T(8,128)(2,1)S(1)}, bf16[2,144,128]{2,1,0:T(8,128)(2,1)S(1)}, u32[]{:S(2)}, u32[]{:S(2)}) collective-permute-start(bf16[2,144,128]{2,1,0:T(8,128)(2,1)S(1)} %get-tuple-element.29), channel_id=1, source_target_pairs={{0,4},{2,6},{4,0},{6,2},{1,5},{3,7},{5,1},{7,3},{8,12},{10,14},{12... | collective-permute-start | bytes 221192 | tf_op jit(solution)/shard_map/ppermute | solution.py:372
  58.5 1.2 %collective-permute-start.4 = (bf16[2,144,128]{2,1,0:T(8,128)(2,1)S(1)}, bf16[2,144,128]{2,1,0:T(8,128)(2,1)S(1)}, u32[]{:S(2)}, u32[]{:S(2)}) collective-permute-start(bf16[2,144,128]{2,1,0:T(8,128)(2,1)S(1)} %get-tuple-element.26), channel_id=1, source_target_pairs={{0,6},{2,0},{4,2},{6,4},{1,7},{3,1},{5,3},{7,5},{8,14},{10,8},{12,... | collective-permute-start | bytes 221192 | tf_op jit(solution)/shard_map/ppermute | solution.py:372
  59.7 15.5 %all-to-all-done.parts_ref = s16[64,144,128]{2,1,0:T(8,128)(2,1)S(1)} async-done(((s16[64,144,128]{2,1,0:T(8,128)(2,1)}), s16[64,144,128]{2,1,0:T(8,128)(2,1)S(1)}, u32[]{:S(2)}, u32[]{:S(2)}) %all-to-all-start) | async-done | bytes 2359328 | tf_op jit(solution)/shard_map/all_to_all | solution.py:474
  75.2 2.2 %shard_map.96 = f32[128,1,128]{2,1,0:T(1,128)} custom-call(s16[64,144,128]{2,1,0:T(8,128)(2,1)S(1)} %all-to-all-done.parts_ref), custom_call_target="tpu_custom_call" | custom-call | tf_op jit(solution)/shard_map/pallas_call | solution.py:436
  77.4 10.1 %all-to-all-start.1 = ((f32[128,1,128]{2,1,0:T(1,128)}), f32[128,1,128]{2,1,0:T(1,128)S(1)}, u32[]{:S(2)}, u32[]{:S(2)}) async-start(f32[128,1,128]{2,1,0:T(1,128)} %shard_map.96), calls=%async_computation.1 | async-start | bytes 131072 | tf_op jit(solution)/shard_map/all_to_all | solution.py:474
  87.5 0.0 collective-permute-done.2
  87.5 0.0 collective-permute-done.3
  87.6 0.0 collective-permute-done.4
  87.8 0.9 reshape.46
  88.7 0.6 reshape.47
  89.3 7.7 %all-to-all-done.1.gains_ref = f32[128,1,128]{2,1,0:T(1,128)S(1)} async-done(((f32[128,1,128]{2,1,0:T(1,128)}), f32[128,1,128]{2,1,0:T(1,128)S(1)}, u32[]{:S(2)}, u32[]{:S(2)}) %all-to-all-start.1) | async-done | bytes 65568 | tf_op jit(solution)/shard_map/all_to_all | solution.py:474
  97.0 0.6 shard_map.97
  (12 shorter events, 0.2 us)
Async XLA Ops:
  4.5 13.9 %collective-permute-start = (bf16[4608,256]{1,0:T(8,128)(2,1)}, bf16[4608,256]{1,0:T(8,128)(2,1)S(1)}, u32[]{:S(2)}, u32[]{:S(2)}) collective-permute-start(bf16[4608,256]{1,0:T(8,128)(2,1)} %get-tuple-element.15), channel_id=1, source_target_pairs={{0,1},{1,0},{2,3},{3,2},{4,5},{5,4},{6,7},{7,6},{8,9},{9,8},{10,11... | collective-permute-start | bytes 7077896 | tf_op jit(solution)/shard_map/ppermute | solution.py:481
  32.1 43.1 %all-to-all-start = ((s16[64,144,128]{2,1,0:T(8,128)(2,1)}), s16[64,144,128]{2,1,0:T(8,128)(2,1)S(1)}, u32[]{:S(2)}, u32[]{:S(2)}) async-start(s16[64,144,128]{2,1,0:T(8,128)(2,1)} %bitcast.33), calls=%async_computation | async-start | bytes 4718592 | tf_op jit(solution)/shard_map/all_to_all | solution.py:474
  52.0 1.6 %collective-permute-start.1 = (bf16[4,144,128]{2,1,0:T(8,128)(2,1)}, bf16[4,144,128]{2,1,0:T(8,128)(2,1)S(1)}, u32[]{:S(2)}, u32[]{:S(2)}) collective-permute-start(bf16[4,144,128]{2,1,0:T(8,128)(2,1)} %get-tuple-element.21), channel_id=1, source_target_pairs={{0,1},{1,0},{2,3},{3,2},{4,5},{5,4},{6,7},{7,6},{8,9},{9,8},{10,11... | collective-permute-start | bytes 442376 | tf_op jit(solution)/shard_map/ppermute | solution.py:364
  54.6 33.0 %collective-permute-start.2 = (bf16[2,144,128]{2,1,0:T(8,128)(2,1)S(1)}, bf16[2,144,128]{2,1,0:T(8,128)(2,1)S(1)}, u32[]{:S(2)}, u32[]{:S(2)}) collective-permute-start(bf16[2,144,128]{2,1,0:T(8,128)(2,1)S(1)} %get-tuple-element.28), channel_id=1, source_target_pairs={{0,2},{2,4},{4,6},{6,0},{1,3},{3,5},{5,7},{7,1},{8,10},{10,12},{12... | collective-permute-start | bytes 221192 | tf_op jit(solution)/shard_map/ppermute | solution.py:372
  56.1 31.4 %collective-permute-start.3 = (bf16[2,144,128]{2,1,0:T(8,128)(2,1)S(1)}, bf16[2,144,128]{2,1,0:T(8,128)(2,1)S(1)}, u32[]{:S(2)}, u32[]{:S(2)}) collective-permute-start(bf16[2,144,128]{2,1,0:T(8,128)(2,1)S(1)} %get-tuple-element.29), channel_id=1, source_target_pairs={{0,4},{2,6},{4,0},{6,2},{1,5},{3,7},{5,1},{7,3},{8,12},{10,14},{12... | collective-permute-start | bytes 221192 | tf_op jit(solution)/shard_map/ppermute | solution.py:372
  58.5 29.0 %collective-permute-start.4 = (bf16[2,144,128]{2,1,0:T(8,128)(2,1)S(1)}, bf16[2,144,128]{2,1,0:T(8,128)(2,1)S(1)}, u32[]{:S(2)}, u32[]{:S(2)}) collective-permute-start(bf16[2,144,128]{2,1,0:T(8,128)(2,1)S(1)} %get-tuple-element.26), channel_id=1, source_target_pairs={{0,6},{2,0},{4,2},{6,4},{1,7},{3,1},{5,3},{7,5},{8,14},{10,8},{12,... | collective-permute-start | bytes 221192 | tf_op jit(solution)/shard_map/ppermute | solution.py:372
  77.4 19.6 %all-to-all-start.1 = ((f32[128,1,128]{2,1,0:T(1,128)}), f32[128,1,128]{2,1,0:T(1,128)S(1)}, u32[]{:S(2)}, u32[]{:S(2)}) async-start(f32[128,1,128]{2,1,0:T(1,128)} %shard_map.96), calls=%async_computation.1 | async-start | bytes 131072 | tf_op jit(solution)/shard_map/all_to_all | solution.py:474

commit v7 on v6

--- a/solution.py
+++ b/solution.py
@@ -25,7 +25,7 @@
 GRP = ("grp_0", "grp_1")
 ROWS_GRP = ("rows_0", "rows_1", "grp_0", "grp_1")
 ROWS = ("rows_0", "rows_1")
-CHIPS = ("rows_0", "rows_1", "grp_0")
+CHIPS = ("grp_0", "rows_0", "rows_1")
 F32 = jnp.float32
 BF16 = jnp.bfloat16
 I32 = jnp.int32
@@ -444,9 +444,9 @@
 
 def close_kernel(group_ref, gains_ref, table_ref, best_ref):
     group = group_ref[0]
-    first = (group & 7) * 16 + (group >> 3)
+    first = (group & 1) * 64 + ((group & 7) >> 1) * 2 + (group >> 3)
     for i in range(8):
-        table_ref[i] = gains_ref[first + 2 * i]
+        table_ref[i] = gains_ref[first + 8 * i]
     highest = jnp.max(gains_ref[...], axis=0)
     best_ref[...] = jnp.max(highest, axis=1, keepdims=True)
 

time: 98 us -> 94.2 us (0.961)
  starting transfers between devices: 28.3 us -> 25.2 us
    all_to_all x2, starting transfers between devices: 21.3 us -> 18.1 us  [exchange(): return lax.all_to_all(blocks, axis, split_axis=0, concat_axis=0, tiled=True)]
where the time goes in v7:
time: 94.2 us; the launch traced here: 93.9 us
  Pallas kernels  40.2 us (43%)
  starting transfers between devices  25.2 us (27%)
  waiting for transfers between devices  23.8 us (25%)
  between operations  2.07 us (2%)
  local copies, waits for them, and re-layouts  1.68 us (2%)
  other arithmetic  0.98 us (1%)
    all_to_all x2, waiting for transfers between devices, exchange(): return lax.all_to_all(blocks, axis, split_axis=0, concat_axis=0, tiled=True)  22.6 us
    all_to_all x2, starting transfers between devices, exchange(): return lax.all_to_all(blocks, axis, split_axis=0, concat_axis=0, tiled=True)  18.1 us
    pallas_call x1, Pallas kernels, both_sums(): pl.pallas_call(both_kernel, grid=(PAIRS // DEEPER,), in_specs=[pl.BlockSp...  13.7 us
    pallas_call x1, Pallas kernels, own_sums(): pl.pallas_call(own_kernel, grid=(PAIRS // UNROLL,), in_specs=[pl.BlockSpe...  12.4 us
    pallas_call x1, Pallas kernels, place_rows(): pl.pallas_call(place_kernel, grid_spec=pltpu.PrefetchScalarGridSpec(num_s...  7.44 us
    ppermute x3, starting transfers between devices, deliver(): block = lax.ppermute(block, 'grp_0', [(i, (i + s) % 4) for i in range(4)])  5.21 us
    pallas_call x1, Pallas kernels, prep(): pl.pallas_call(prep_kernel, in_specs=[pl.BlockSpec(memory_space=pltpu.SME...  3.85 us
    pallas_call x1, Pallas kernels, owned_gains(): pl.pallas_call(gain_kernel, out_shape=jax.ShapeDtypeStruct(shape, F32), i...  2.22 us
  transfers between devices with their start and end apart: 7, of which 3 were waited for; matrix products, arithmetic and copies ran while one was open for 3% of the time, Pallas kernels for 23%

profile of v7, /device:TPU:1, one launch (start us, length us, event | category | flops | bytes accessed | tf_op | source)
XLA Modules:
  0.0 93.9 jit_solution(11985463015318180311)
XLA Ops:
  0.6 3.9 %shard_map.93 = (bf16[4608,256]{1,0:T(8,128)(2,1)}, bf16[32,4096]{1,0:T(8,128)(2,1)}) custom-call(s32[1]{0:T(128)} %bitcast.1.core_ref, s32[4096,512]{1,0:T(8,128)} %codes_ref.1, bf16[16,4096]{1,0:T(8,128)(2,1)} %bitcast.36, bf16[32,128]{1,0:T(8,128)(2,1)} %bitcast.40, s32[1,4096]{1,0:T(1,128)} %bitcast.38), custom_call_target="tpu_custom_call" | custom-call | flops 1048576 | bytes 6291456 | tf_op jit(solution)/shard_map/pallas_call | solution.py:108
  4.5 1.5 %collective-permute-start = (bf16[4608,256]{1,0:T(8,128)(2,1)}, bf16[4608,256]{1,0:T(8,128)(2,1)S(1)}, u32[]{:S(2)}, u32[]{:S(2)}) collective-permute-start(bf16[4608,256]{1,0:T(8,128)(2,1)} %get-tuple-element.15), channel_id=1, source_target_pairs={{0,1},{1,0},{2,3},{3,2},{4,5},{5,4},{6,7},{7,6},{8,9},{9,8},{10,11... | collective-permute-start | bytes 7077896 | tf_op jit(solution)/shard_map/ppermute | solution.py:481
  6.0 12.4 %shard_map.94.sums_ref = f32[32,136,256]{2,1,0:T(8,128)S(1)} custom-call(s32[1]{0:T(128)} %bitcast.1.core_ref, s32[4096,512]{1,0:T(8,128)} %codes_ref.1, bf16[16,4096]{1,0:T(8,128)(2,1)} %bitcast.37, bf16[32,128]{1,0:T(8,128)(2,1)} %bitcast.41, s32[1,4096]{1,0:T(1,128)} %bitcast.39), custom_call_target="tpu_custom_call" | custom-call | flops 17179869184 | bytes 8388608 | tf_op jit(solution)/shard_map/pallas_call | solution.py:244
  18.4 0.0 collective-permute-done.rows_ref
  18.4 13.7 %shard_map.95 = s16[32,2,144,128]{3,2,1,0:T(8,128)(2,1)} custom-call(bf16[4608,256]{1,0:T(8,128)(2,1)S(1)} %collective-permute-done.rows_ref, f32[32,136,256]{2,1,0:T(8,128)S(1)} %shard_map.94.sums_ref), custom_call_target="tpu_custom_call" | custom-call | flops 17179869184 | bytes 8388608 | tf_op jit(solution)/shard_map/pallas_call | solution.py:265
  32.1 11.2 %all-to-all-start = ((s16[64,144,128]{2,1,0:T(8,128)(2,1)}), s16[64,144,128]{2,1,0:T(8,128)(2,1)S(1)}, u32[]{:S(2)}, u32[]{:S(2)}) async-start(s16[64,144,128]{2,1,0:T(8,128)(2,1)} %bitcast.33), calls=%async_computation | async-start | bytes 4718592 | tf_op jit(solution)/shard_map/all_to_all | solution.py:474
  44.6 7.4 %shard_map.98 = (bf16[4,144,128]{2,1,0:T(8,128)(2,1)}, bf16[4,144,128]{2,1,0:T(8,128)(2,1)}) custom-call(s32[1]{0:T(128)S(6)} %copy.17.feature_ref, s32[1]{0:T(128)} %bitcast.1.core_ref, s32[1]{0:T(128)S(6)} %copy.18.bin_ref, bf16[32,4096]{1,0:T(8,128)(2,1)} %get-tuple-element.19.aux_ref, s32[4096,512]{1,0:T(8,128)} %codes_ref.1), custom_call_target="tpu_custom_call" | custom-call | flops 2147483648 | bytes 1048576 | tf_op jit(solution)/shard_map/pallas_call | solution.py:341
  52.0 0.3 collective-permute-start.1
  52.3 1.3 %collective-permute-done.1 = bf16[4,144,128]{2,1,0:T(8,128)(2,1)S(1)} collective-permute-done((bf16[4,144,128]{2,1,0:T(8,128)(2,1)}, bf16[4,144,128]{2,1,0:T(8,128)(2,1)S(1)}, u32[]{:S(2)}, u32[]{:S(2)}) %collective-permute-start.1) | collective-permute-done | bytes 147488 | tf_op jit(solution)/shard_map/ppermute | solution.py:364
  53.6 0.9 select_bitcast_fusion
  54.6 1.5 %collective-permute-start.2 = (bf16[2,144,128]{2,1,0:T(8,128)(2,1)S(1)}, bf16[2,144,128]{2,1,0:T(8,128)(2,1)S(1)}, u32[]{:S(2)}, u32[]{:S(2)}) collective-permute-start(bf16[2,144,128]{2,1,0:T(8,128)(2,1)S(1)} %get-tuple-element.28), channel_id=1, source_target_pairs={{0,2},{2,4},{4,6},{6,0},{1,3},{3,5},{5,7},{7,1},{8,10},{10,12},{12... | collective-permute-start | bytes 221192 | tf_op jit(solution)/shard_map/ppermute | solution.py:372
  56.1 2.6 %collective-permute-start.3 = (bf16[2,144,128]{2,1,0:T(8,128)(2,1)S(1)}, bf16[2,144,128]{2,1,0:T(8,128)(2,1)S(1)}, u32[]{:S(2)}, u32[]{:S(2)}) collective-permute-start(bf16[2,144,128]{2,1,0:T(8,128)(2,1)S(1)} %get-tuple-element.29), channel_id=1, source_target_pairs={{0,4},{2,6},{4,0},{6,2},{1,5},{3,7},{5,1},{7,3},{8,12},{10,14},{12... | collective-permute-start | bytes 221192 | tf_op jit(solution)/shard_map/ppermute | solution.py:372
  58.7 1.1 %collective-permute-start.4 = (bf16[2,144,128]{2,1,0:T(8,128)(2,1)S(1)}, bf16[2,144,128]{2,1,0:T(8,128)(2,1)S(1)}, u32[]{:S(2)}, u32[]{:S(2)}) collective-permute-start(bf16[2,144,128]{2,1,0:T(8,128)(2,1)S(1)} %get-tuple-element.26), channel_id=1, source_target_pairs={{0,6},{2,0},{4,2},{6,4},{1,7},{3,1},{5,3},{7,5},{8,14},{10,8},{12,... | collective-permute-start | bytes 221192 | tf_op jit(solution)/shard_map/ppermute | solution.py:372
  59.8 14.9 %all-to-all-done.parts_ref = s16[64,144,128]{2,1,0:T(8,128)(2,1)S(1)} async-done(((s16[64,144,128]{2,1,0:T(8,128)(2,1)}), s16[64,144,128]{2,1,0:T(8,128)(2,1)S(1)}, u32[]{:S(2)}, u32[]{:S(2)}) %all-to-all-start) | async-done | bytes 2359328 | tf_op jit(solution)/shard_map/all_to_all | solution.py:474
  74.7 2.2 %shard_map.96 = f32[128,1,128]{2,1,0:T(1,128)} custom-call(s16[64,144,128]{2,1,0:T(8,128)(2,1)S(1)} %all-to-all-done.parts_ref), custom_call_target="tpu_custom_call" | custom-call | tf_op jit(solution)/shard_map/pallas_call | solution.py:436
  76.9 6.9 %all-to-all-start.1 = ((f32[128,1,128]{2,1,0:T(1,128)}), f32[128,1,128]{2,1,0:T(1,128)S(1)}, u32[]{:S(2)}, u32[]{:S(2)}) async-start(f32[128,1,128]{2,1,0:T(1,128)} %shard_map.96), calls=%async_computation.1 | async-start | bytes 131072 | tf_op jit(solution)/shard_map/all_to_all | solution.py:474
  83.8 0.0 collective-permute-done.2
  83.8 0.0 collective-permute-done.3
  83.8 0.0 collective-permute-done.4
  84.1 0.9 reshape.46
  84.9 0.6 reshape.47
  85.6 7.7 %all-to-all-done.1.gains_ref = f32[128,1,128]{2,1,0:T(1,128)S(1)} async-done(((f32[128,1,128]{2,1,0:T(1,128)}), f32[128,1,128]{2,1,0:T(1,128)S(1)}, u32[]{:S(2)}, u32[]{:S(2)}) %all-to-all-start.1) | async-done | bytes 65568 | tf_op jit(solution)/shard_map/all_to_all | solution.py:474
  93.3 0.6 shard_map.97
  (12 shorter events, 0.2 us)
Async XLA Ops:
  4.5 13.9 %collective-permute-start = (bf16[4608,256]{1,0:T(8,128)(2,1)}, bf16[4608,256]{1,0:T(8,128)(2,1)S(1)}, u32[]{:S(2)}, u32[]{:S(2)}) collective-permute-start(bf16[4608,256]{1,0:T(8,128)(2,1)} %get-tuple-element.15), channel_id=1, source_target_pairs={{0,1},{1,0},{2,3},{3,2},{4,5},{5,4},{6,7},{7,6},{8,9},{9,8},{10,11... | collective-permute-start | bytes 7077896 | tf_op jit(solution)/shard_map/ppermute | solution.py:481
  32.1 42.6 %all-to-all-start = ((s16[64,144,128]{2,1,0:T(8,128)(2,1)}), s16[64,144,128]{2,1,0:T(8,128)(2,1)S(1)}, u32[]{:S(2)}, u32[]{:S(2)}) async-start(s16[64,144,128]{2,1,0:T(8,128)(2,1)} %bitcast.33), calls=%async_computation | async-start | bytes 4718592 | tf_op jit(solution)/shard_map/all_to_all | solution.py:474
  52.0 1.6 %collective-permute-start.1 = (bf16[4,144,128]{2,1,0:T(8,128)(2,1)}, bf16[4,144,128]{2,1,0:T(8,128)(2,1)S(1)}, u32[]{:S(2)}, u32[]{:S(2)}) collective-permute-start(bf16[4,144,128]{2,1,0:T(8,128)(2,1)} %get-tuple-element.21), channel_id=1, source_target_pairs={{0,1},{1,0},{2,3},{3,2},{4,5},{5,4},{6,7},{7,6},{8,9},{9,8},{10,11... | collective-permute-start | bytes 442376 | tf_op jit(solution)/shard_map/ppermute | solution.py:364
  54.6 29.2 %collective-permute-start.2 = (bf16[2,144,128]{2,1,0:T(8,128)(2,1)S(1)}, bf16[2,144,128]{2,1,0:T(8,128)(2,1)S(1)}, u32[]{:S(2)}, u32[]{:S(2)}) collective-permute-start(bf16[2,144,128]{2,1,0:T(8,128)(2,1)S(1)} %get-tuple-element.28), channel_id=1, source_target_pairs={{0,2},{2,4},{4,6},{6,0},{1,3},{3,5},{5,7},{7,1},{8,10},{10,12},{12... | collective-permute-start | bytes 221192 | tf_op jit(solution)/shard_map/ppermute | solution.py:372
  56.1 27.7 %collective-permute-start.3 = (bf16[2,144,128]{2,1,0:T(8,128)(2,1)S(1)}, bf16[2,144,128]{2,1,0:T(8,128)(2,1)S(1)}, u32[]{:S(2)}, u32[]{:S(2)}) collective-permute-start(bf16[2,144,128]{2,1,0:T(8,128)(2,1)S(1)} %get-tuple-element.29), channel_id=1, source_target_pairs={{0,4},{2,6},{4,0},{6,2},{1,5},{3,7},{5,1},{7,3},{8,12},{10,14},{12... | collective-permute-start | bytes 221192 | tf_op jit(solution)/shard_map/ppermute | solution.py:372
  58.7 25.1 %collective-permute-start.4 = (bf16[2,144,128]{2,1,0:T(8,128)(2,1)S(1)}, bf16[2,144,128]{2,1,0:T(8,128)(2,1)S(1)}, u32[]{:S(2)}, u32[]{:S(2)}) collective-permute-start(bf16[2,144,128]{2,1,0:T(8,128)(2,1)S(1)} %get-tuple-element.26), channel_id=1, source_target_pairs={{0,6},{2,0},{4,2},{6,4},{1,7},{3,1},{5,3},{7,5},{8,14},{10,8},{12,... | collective-permute-start | bytes 221192 | tf_op jit(solution)/shard_map/ppermute | solution.py:372
  76.9 16.4 %all-to-all-start.1 = ((f32[128,1,128]{2,1,0:T(1,128)}), f32[128,1,128]{2,1,0:T(1,128)S(1)}, u32[]{:S(2)}, u32[]{:S(2)}) async-start(f32[128,1,128]{2,1,0:T(1,128)} %shard_map.96), calls=%async_computation.1 | async-start | bytes 131072 | tf_op jit(solution)/shard_map/all_to_all | solution.py:474
